TPU v7x, 32 devices: a whole 2x2x4 slice. The times are simulated.
32 devices in a mesh: dp: 4 (over x, core), expert: 8 (over z, y).
Axes of the slice: x: 2, y: 2, z: 4, core: 2. Of those that a mesh axis runs over, the one named last changes fastest.
Arguments:
- tokens: bfloat16 [4096, 2048], P(('dp', 'expert')), may hold values from -6 to 6
- cotangent: bfloat16 [4096, 2048], P(('dp', 'expert')), may hold values from -1.5 to 1.5
- routes: int32 [4096, 8], P(('dp', 'expert')), may hold values from 0 to 31, all different within a row; in each aligned block of 128 rows (0 to 127, 128 to 255, ...) at most 56 rows name the same one
- gates: bfloat16 [4096, 8], P(('dp', 'expert')), may hold values from 0.049804688 to 0.44921875
- w_gate: bfloat16 [32, 2048, 768], P(('dp', 'expert')), may hold values from -0.125 to 0.125
- w_up: bfloat16 [32, 2048, 768], P(('dp', 'expert')), may hold values from -0.125 to 0.125
- w_down: bfloat16 [32, 768, 2048], P(('dp', 'expert')), may hold values from -0.21875 to 0.21875
Outputs:
- input_grad: bfloat16 [4096, 2048], P(('dp', 'expert'))
- gate_grad: bfloat16 [4096, 8], P(('dp', 'expert'))
- w_gate_grad: bfloat16 [32, 2048, 768], P(('dp', 'expert'))
- w_up_grad: bfloat16 [32, 2048, 768], P(('dp', 'expert'))
- w_down_grad: bfloat16 [32, 768, 2048], P(('dp', 'expert'))
Inputs may be any that keep to these rules, and one draw needn't show every extreme that they name: `routes`: each row names 8 different experts. The tokens of one device name one expert at most 56 times, and in every draw some expert is named exactly 56 times by the tokens of some device.
All inputs are finite; a program needn't handle non-finite values.
Results may differ from a plain program's by a relative error of at most 0.0064.
Values may be sent and summed in bfloat16 or wider, within the bound.
No kernel may reach another device: no remote copies, remote signals or barrier semaphores. Data moves between devices by JAX's collectives and lax.ppermute only.
A program may use at most 192 MiB of HBM per device.

v0:
```python
import jax
import jax.numpy as jnp
from jax import lax
from jax.sharding import PartitionSpec as P

block_rows = 256


def expert_parts(inputs, cotangent_rows, router_weight, gate_matrix, up_matrix, down_matrix):
    pre_gate = jnp.dot(inputs, gate_matrix, preferred_element_type=jnp.float32)
    pre_up = jnp.dot(inputs, up_matrix, preferred_element_type=jnp.float32)
    sigmoid_gate = jax.nn.sigmoid(pre_gate)
    silu_gate = pre_gate * sigmoid_gate
    hidden = (silu_gate * pre_up).astype(jnp.bfloat16)
    expert_out = jnp.dot(hidden, down_matrix, preferred_element_type=jnp.float32)
    gate_grad = jnp.sum(cotangent_rows.astype(jnp.float32) * expert_out, axis=1).astype(
        jnp.bfloat16
    )
    out_grad = (
        router_weight.astype(jnp.float32)[:, None] * cotangent_rows.astype(jnp.float32)
    ).astype(jnp.bfloat16)
    hidden_grad = lax.dot_general(
        out_grad, down_matrix, (((1,), (1,)), ((), ())), preferred_element_type=jnp.float32
    )
    pre_gate_grad = (
        hidden_grad * pre_up * sigmoid_gate * (1.0 + pre_gate * (1.0 - sigmoid_gate))
    ).astype(jnp.bfloat16)
    pre_up_grad = (hidden_grad * silu_gate).astype(jnp.bfloat16)
    row_grad = lax.dot_general(
        pre_gate_grad, gate_matrix, (((1,), (1,)), ((), ())), preferred_element_type=jnp.float32
    )
    row_grad = row_grad + lax.dot_general(
        pre_up_grad, up_matrix, (((1,), (1,)), ((), ())), preferred_element_type=jnp.float32
    )
    return (row_grad.astype(jnp.bfloat16), gate_grad, pre_gate_grad, pre_up_grad, hidden, out_grad)


def outer_terms(inputs, pre_gate_grad, pre_up_grad, hidden, out_grad):
    gate_term = lax.dot_general(
        inputs, pre_gate_grad, (((0,), (0,)), ((), ())), preferred_element_type=jnp.float32
    )
    up_term = lax.dot_general(
        inputs, pre_up_grad, (((0,), (0,)), ((), ())), preferred_element_type=jnp.float32
    )
    down_term = lax.dot_general(
        hidden, out_grad, (((0,), (0,)), ((), ())), preferred_element_type=jnp.float32
    )
    return (gate_term, up_term, down_term)


def on_device(tokens, cotangent, routes, gates, w_gate, w_up, w_down):
    dp_count = lax.axis_size("dp")
    expert_count = lax.axis_size("expert")
    device_count = dp_count * expert_count
    tok_local, model_width = tokens.shape
    top_count = routes.shape[1]
    row_count = tok_local * top_count
    most_rows = 7 * row_count // (4 * device_count)
    slot_total = device_count * most_rows
    zero_value = jnp.zeros((), jnp.bfloat16)
    flat_expert = routes.reshape(row_count)
    onehot = (flat_expert[:, None] == jnp.arange(device_count, dtype=jnp.int32)[None, :]).astype(
        jnp.int32
    )
    rank_in_expert = jnp.sum(jnp.cumsum(onehot, axis=0) * onehot, axis=1) - 1
    slot_index = flat_expert * most_rows + rank_in_expert
    row_of_slot = (
        jnp.full((slot_total,), row_count, jnp.int32)
        .at[slot_index]
        .set(jnp.arange(row_count, dtype=jnp.int32))
    )
    slot_live = row_of_slot < row_count
    safe_row = jnp.minimum(row_of_slot, row_count - 1)
    token_of_slot = safe_row // top_count
    send_tokens = jnp.where(slot_live[:, None], tokens[token_of_slot], zero_value).reshape(
        device_count, most_rows, model_width
    )
    send_cotangent = jnp.where(slot_live[:, None], cotangent[token_of_slot], zero_value).reshape(
        device_count, most_rows, model_width
    )
    send_weight = jnp.where(slot_live, gates.reshape(row_count)[safe_row], zero_value).reshape(
        device_count, most_rows
    )
    arrived = (
        lax.all_to_all(send_tokens, ("dp", "expert"), split_axis=0, concat_axis=0, tiled=True),
        lax.all_to_all(send_cotangent, ("dp", "expert"), split_axis=0, concat_axis=0, tiled=True),
        lax.all_to_all(send_weight, ("dp", "expert"), split_axis=0, concat_axis=0, tiled=True),
    )
    got_tokens = arrived[0].reshape(slot_total, model_width)
    got_cotangent = arrived[1].reshape(slot_total, model_width)
    got_weight = arrived[2].reshape(slot_total)
    gate_matrix = w_gate[0]
    up_matrix = w_up[0]
    down_matrix = w_down[0]
    hidden_width = gate_matrix.shape[1]
    is_used = got_weight != zero_value
    used_count = jnp.sum(is_used.astype(jnp.int32))
    padded_total = -(-slot_total // block_rows) * block_rows
    compact_pos = jnp.cumsum(is_used.astype(jnp.int32)) - 1
    slot_of_compact = (
        jnp.full((padded_total,), slot_total, jnp.int32)
        .at[jnp.where(is_used, compact_pos, padded_total)]
        .set(jnp.arange(slot_total, dtype=jnp.int32), mode="drop")
    )
    block_count = (used_count + block_rows - 1) // block_rows

    def block_step(block_index, carried):
        gate_acc, up_acc, down_acc, grad_slots, gate_slots = carried
        picked = lax.dynamic_slice_in_dim(slot_of_compact, block_index * block_rows, block_rows)
        is_live = picked < slot_total
        safe_pick = jnp.minimum(picked, slot_total - 1)
        block_tokens = jnp.where(is_live[:, None], got_tokens[safe_pick], zero_value)
        block_cotangent = jnp.where(is_live[:, None], got_cotangent[safe_pick], zero_value)
        block_weight = jnp.where(is_live, got_weight[safe_pick], zero_value)
        row_grad, gate_grad, pre_gate_grad, pre_up_grad, hidden, out_grad = expert_parts(
            block_tokens, block_cotangent, block_weight, gate_matrix, up_matrix, down_matrix
        )
        gate_term, up_term, down_term = outer_terms(
            block_tokens, pre_gate_grad, pre_up_grad, hidden, out_grad
        )
        target = jnp.where(is_live, picked, slot_total)
        grad_slots = grad_slots.at[target].set(row_grad, mode="drop")
        gate_slots = gate_slots.at[target].set(gate_grad, mode="drop")
        return (
            gate_acc + gate_term,
            up_acc + up_term,
            down_acc + down_term,
            grad_slots,
            gate_slots,
        )

    initial = (
        jnp.zeros((model_width, hidden_width), jnp.float32),
        jnp.zeros((model_width, hidden_width), jnp.float32),
        jnp.zeros((hidden_width, model_width), jnp.float32),
        jnp.zeros((slot_total, model_width), jnp.bfloat16),
        jnp.zeros((slot_total,), jnp.bfloat16),
    )
    finished = lax.fori_loop(0, block_count, block_step, initial)
    gate_acc, up_acc, down_acc, grad_slots, gate_slots = finished
    grad_out = grad_slots.reshape(device_count, most_rows, model_width)
    gate_out = gate_slots.reshape(device_count, most_rows)
    returned = (
        lax.all_to_all(grad_out, ("dp", "expert"), split_axis=0, concat_axis=0, tiled=True),
        lax.all_to_all(gate_out, ("dp", "expert"), split_axis=0, concat_axis=0, tiled=True),
    )
    back_grad = returned[0].reshape(slot_total, model_width)
    back_gate = returned[1].reshape(slot_total)
    row_grads = back_grad[slot_index].reshape(tok_local, top_count, model_width)
    input_grad = jnp.sum(row_grads, axis=1, dtype=jnp.float32).astype(jnp.bfloat16)
    gate_grad = back_gate[slot_index].reshape(tok_local, top_count)
    return (
        input_grad,
        gate_grad,
        gate_acc.astype(jnp.bfloat16)[None],
        up_acc.astype(jnp.bfloat16)[None],
        down_acc.astype(jnp.bfloat16)[None],
    )


def solution(mesh):
    in_specs = (
        P(("dp", "expert"), None),
        P(("dp", "expert"), None),
        P(("dp", "expert"), None),
        P(("dp", "expert"), None),
        P(("dp", "expert"), None, None),
        P(("dp", "expert"), None, None),
        P(("dp", "expert"), None, None),
    )
    out_specs = (
        P(("dp", "expert"), None),
        P(("dp", "expert"), None),
        P(("dp", "expert"), None, None),
        P(("dp", "expert"), None, None),
        P(("dp", "expert"), None, None),
    )
    return jax.shard_map(
        on_device, mesh=mesh, in_specs=in_specs, out_specs=out_specs, check_vma=False
    )
```

profile of v0, /device:TPU:0, one launch (start us, length us, event | category | flops | bytes accessed | tf_op | source)
XLA Modules:
  0.0 1046.0 jit_solution(4860548228168078904)
XLA Ops:
  3.5 9.0 reduce-window.15
  13.1 4.3 scatter_custom_fusion.2
  17.4 10.9 %gather_fusion.3 = bf16[1792]{0:T(1024)(128)(2,1)S(1)} fusion(bf16[1024]{0:T(1024)(128)(2,1)S(1)} %reshape.184, s32[2048]{0:T(1024)S(1)} %get-tuple-element.145), kind=kCustom, calls=%fused_computation.3 | custom fusion | bytes 14336 | tf_op jit(solution)/shard_map/gather | solution.py:81
  29.1 7.3 all-to-all-start
  36.5 8.0 gather_fusion.5
  44.5 8.0 gather_fusion.4
  52.5 10.5 broadcast_select_fusion.6
  63.0 168.4 %all_to_all.35 = bf16[32,56,2048]{2,1,0:T(8,128)(2,1)} all-to-all(bf16[32,56,2048]{2,1,0:T(8,128)(2,1)} %get-tuple-element.142), channel_id=1, replica_groups=mesh['dp'=4,'expert'=8] {'dp','expert'}, dimensions={0} | all-to-all | bytes 14680064 | tf_op jit(solution)/shard_map/all_to_all | solution.py:86
  231.3 3.6 all-to-all-start.1
  237.4 7.1 scatter_custom_fusion.3
  244.5 157.2 %all-to-all-done.1 = bf16[32,56,2048]{2,1,0:T(8,128)(2,1)} async-done(((bf16[32,56,2048]{2,1,0:T(8,128)(2,1)}), bf16[32,56,2048]{2,1,0:T(8,128)(2,1)}, u32[]{:S(2)}, u32[]{:S(2)}) %all-to-all-start.1) | async-done | bytes 7340064 | tf_op jit(solution)/shard_map/all_to_all | solution.py:85
  401.7 3.0 broadcast.159.clone
  404.8 3.4 broadcast_in_dim.85
  408.2 3.1 broadcast.159
  411.3 3.9 broadcast_in_dim.86
  415.1 247.9 %while.18 = (s32[]{:T(128)}, f32[2048,768]{1,0:T(8,128)}, f32[2048,768]{1,0:T(8,128)}, f32[768,2048]{1,0:T(8,128)}, bf16[1792,2048]{1,0:T(8,128)(2,1)}, /*index=...) while((s32[]{:T(128)}, f32[2048,768]{1,0:T(8,128)}, ...), condition=%wide.region_12.13_spmd, body=%wide.region_8.12_spmd.sunk | while | flops 7264866304 | bytes 172382464 | solution.py:139
  417.5 6.4 gather_fusion
  423.9 4.2 fusion.67
  428.1 6.4 gather_fusion.2
  434.6 3.3 fusion.68
  441.0 2.2 scatter_fusion.1
  443.2 3.0 fusion.69
  446.3 3.9 fusion.70
  451.5 8.9 convolution_add_fusion.8
  460.4 6.7 convolution_add_fusion.7
  467.1 10.3 scatter_fusion
  479.4 6.4 gather_fusion
  485.8 4.2 fusion.67
  490.0 6.4 gather_fusion.2
  496.4 3.3 fusion.68
  502.9 2.2 scatter_fusion.1
  505.1 3.0 fusion.69
  508.1 3.9 fusion.70
  513.4 8.9 convolution_add_fusion.8
  522.3 6.7 convolution_add_fusion.7
  528.9 10.3 scatter_fusion
  541.2 6.4 gather_fusion
  547.7 4.2 fusion.67
  551.8 6.4 gather_fusion.2
  558.3 3.3 fusion.68
  564.7 2.2 scatter_fusion.1
  566.9 3.0 fusion.69
  570.0 3.9 fusion.70
  575.2 8.9 convolution_add_fusion.8
  584.1 6.7 convolution_add_fusion.7
  590.8 10.3 scatter_fusion
  603.1 6.4 gather_fusion
  609.5 4.2 fusion.67
  613.7 6.4 gather_fusion.2
  620.1 3.3 fusion.68
  626.6 2.2 scatter_fusion.1
  628.8 3.0 fusion.69
  631.8 3.9 fusion.70
  637.1 8.9 convolution_add_fusion.8
  646.0 6.7 convolution_add_fusion.7
  652.6 10.3 scatter_fusion
  663.2 193.3 %all_to_all.36 = bf16[32,1,56]{2,1,0:T(2,128)(2,1)S(1)} all-to-all(bf16[32,1,56]{2,1,0:T(2,128)(2,1)S(1)} %all_to_all.29), channel_id=1, replica_groups=mesh['dp'=4,'expert'=8] {'dp','expert'}, dimensions={0} | all-to-all | bytes 7168 | tf_op jit(solution)/shard_map/all_to_all | solution.py:145
  856.5 3.8 all-to-all-start.3
  860.3 4.9 convert_bitcast_fusion.2
  865.2 4.9 convert_bitcast_fusion.1
  872.4 6.8 gather_fusion.7
  879.9 147.0 %all-to-all-done.3 = bf16[32,56,2048]{2,1,0:T(8,128)(2,1)} async-done(((bf16[32,56,2048]{2,1,0:T(8,128)(2,1)}), bf16[32,56,2048]{2,1,0:T(8,128)(2,1)}, u32[]{:S(2)}, u32[]{:S(2)}) %all-to-all-start.3) | async-done | bytes 7340064 | tf_op jit(solution)/shard_map/all_to_all | solution.py:144
  1027.0 12.9 %gather_fusion.6 = bf16[1024,2048]{1,0:T(8,128)(2,1)} fusion(bf16[1792,2048]{1,0:T(8,128)(2,1)} %bitcast.12, s32[1024]{0:T(1024)S(1)} %broadcast_clamp_fusion), kind=kCustom, calls=%fused_computation.6 | custom fusion | bytes 8392704 | tf_op jit(solution)/shard_map/gather | solution.py:149
  1039.9 5.9 bitcast_reduce_fusion
  (173 shorter events, 34.7 us)
Async XLA Ops:
  0.6 35.9 %copy-start = (bf16[128,2048]{1,0:T(8,128)(2,1)S(1)}, bf16[128,2048]{1,0:T(8,128)(2,1)}, u32[]{:S(2)}) copy-start(bf16[128,2048]{1,0:T(8,128)(2,1)} %param.10) | copy-start | bytes 1572868
  13.0 4.4 copy-start.9
  29.1 33.9 %all-to-all-start = ((bf16[32,1,56]{2,1,0:T(2,128)(2,1)}), bf16[32,1,56]{2,1,0:T(2,128)(2,1)S(1)}, u32[]{:S(2)}, u32[]{:S(2)}) async-start(bf16[32,1,56]{2,1,0:T(2,128)(2,1)} %all_to_all.28), calls=%async_computation | async-start | bytes 32768 | tf_op jit(solution)/shard_map/all_to_all | solution.py:87
  36.5 8.0 copy-start.2
  231.3 170.4 %all-to-all-start.1 = ((bf16[32,56,2048]{2,1,0:T(8,128)(2,1)}), bf16[32,56,2048]{2,1,0:T(8,128)(2,1)}, u32[]{:S(2)}, u32[]{:S(2)}) async-start(bf16[32,56,2048]{2,1,0:T(8,128)(2,1)} %get-tuple-element.143), calls=%async_computation.1 | async-start | bytes 14680064 | tf_op jit(solution)/shard_map/all_to_all | solution.py:85
  423.9 14.0 %copy-start.4 = (bf16[256,2048]{1,0:T(8,128)(2,1)}, bf16[256,2048]{1,0:T(8,128)(2,1)S(1)}, u32[]{:S(2)}) copy-start(bf16[256,2048]{1,0:T(8,128)(2,1)S(1)} %gather_fusion) | copy-start | bytes 3145732 | tf_op jit(solution)/shard_map/while
  434.5 4.8 copy-start.6
  434.5 3.4 copy-start.8
  434.5 3.4 copy-start.12
  437.9 1.9 copy-start.11
  441.0 9.2 slice-start
  443.2 7.0 slice-start.1
  443.2 7.0 copy-start.7
  450.2 1.3 copy-start.5
  451.5 8.9 copy-start.3
  485.8 14.0 %copy-start.4 = (bf16[256,2048]{1,0:T(8,128)(2,1)}, bf16[256,2048]{1,0:T(8,128)(2,1)S(1)}, u32[]{:S(2)}) copy-start(bf16[256,2048]{1,0:T(8,128)(2,1)S(1)} %gather_fusion) | copy-start | bytes 3145732 | tf_op jit(solution)/shard_map/while
  496.4 4.7 copy-start.6
  496.4 3.4 copy-start.8
  496.4 3.4 copy-start.12
  499.8 1.9 copy-start.11
  502.9 9.2 slice-start
  505.0 7.0 slice-start.1
  505.1 7.0 copy-start.7
  512.1 1.3 copy-start.5
  513.4 8.9 copy-start.3
  547.6 14.0 %copy-start.4 = (bf16[256,2048]{1,0:T(8,128)(2,1)}, bf16[256,2048]{1,0:T(8,128)(2,1)S(1)}, u32[]{:S(2)}) copy-start(bf16[256,2048]{1,0:T(8,128)(2,1)S(1)} %gather_fusion) | copy-start | bytes 3145732 | tf_op jit(solution)/shard_map/while
  558.2 4.7 copy-start.6
  558.2 3.4 copy-start.8
  558.2 3.4 copy-start.12
  561.6 1.9 copy-start.11
  564.7 9.2 slice-start
  566.9 7.0 slice-start.1
  566.9 7.0 copy-start.7
  573.9 1.3 copy-start.5
  575.2 8.9 copy-start.3
  609.5 14.0 %copy-start.4 = (bf16[256,2048]{1,0:T(8,128)(2,1)}, bf16[256,2048]{1,0:T(8,128)(2,1)S(1)}, u32[]{:S(2)}) copy-start(bf16[256,2048]{1,0:T(8,128)(2,1)S(1)} %gather_fusion) | copy-start | bytes 3145732 | tf_op jit(solution)/shard_map/while
  620.1 4.7 copy-start.6
  620.1 3.4 copy-start.8
  620.1 3.4 copy-start.12
  623.5 1.9 copy-start.11
  626.6 9.2 slice-start
  628.8 7.0 slice-start.1
  628.8 7.0 copy-start.7
  635.8 1.3 copy-start.5
  637.1 8.9 copy-start.3
  856.5 3.8 copy-start.10
  856.5 170.5 %all-to-all-start.3 = ((bf16[32,56,2048]{2,1,0:T(8,128)(2,1)}), bf16[32,56,2048]{2,1,0:T(8,128)(2,1)}, u32[]{:S(2)}, u32[]{:S(2)}) async-start(bf16[32,56,2048]{2,1,0:T(8,128)(2,1)} %bitcast.81), calls=%async_computation.3 | async-start | bytes 14680064 | tf_op jit(solution)/shard_map/all_to_all | solution.py:144
  860.3 9.8 slice-start.2
  865.2 4.9 slice-start.3
  1027.0 18.8 %copy-start.1 = (bf16[128,2048]{1,0:T(8,128)(2,1)S(1)}, bf16[128,2048]{1,0:T(8,128)(2,1)}, u32[]{:S(2)}) copy-start(bf16[128,2048]{1,0:T(8,128)(2,1)} %param.10) | copy-start | bytes 1572868
where the time goes:
time: 1060 us; the launch traced here: 1050 us
  blocking collectives  362 us (34%)
  waiting for transfers between devices  304 us (29%)
  local copies, waits for them, and re-layouts  187 us (18%)
  matrix products  135 us (13%)
  other arithmetic  39.9 us (4%)
  starting transfers between devices  14.7 us (1%)
    all_to_all x1, blocking collectives, on_device(): lax.all_to_all(gate_out, ('dp', 'expert'), split_axis=0, concat_axis=0, t...  193 us
    all_to_all x1, blocking collectives, on_device(): lax.all_to_all(send_cotangent, ('dp', 'expert'), split_axis=0, concat_axi...  168 us
    all_to_all x1, waiting for transfers between devices, on_device(): lax.all_to_all(send_tokens, ('dp', 'expert'), split_axis=0, concat_axis=0...  157 us
    all_to_all x1, waiting for transfers between devices, on_device(): lax.all_to_all(grad_out, ('dp', 'expert'), split_axis=0, concat_axis=0, t...  147 us
    scatter x4, local copies, waits for them, and re-layouts, block_step(): grad_slots = grad_slots.at[target].set(row_grad, mode='drop')  41.1 us
    dot_general x4, matrix products, outer_terms(): lax.dot_general(inputs, pre_up_grad, (((0,), (0,)), ((), ())), preferred_...  35.5 us
    dot_general x4, matrix products, outer_terms(): lax.dot_general(inputs, pre_gate_grad, (((0,), (0,)), ((), ())), preferre...  26.7 us
    gather x4, local copies, waits for them, and re-layouts, block_step(): got_tokens[safe_pick]  25.6 us
  transfers between devices with their start and end apart: 3, of which 2 were waited for; matrix products, arithmetic and copies ran while one was open for 5% of the time, Pallas kernels for 0%

commit v1 on v0

--- a/solution.py
+++ b/solution.py
@@ -4,6 +4,7 @@
 from jax.sharding import PartitionSpec as P
 
 block_rows = 256
+gather_limit = 32 * 2**20
 
 
 def expert_parts(inputs, cotangent_rows, router_weight, gate_matrix, up_matrix, down_matrix):
@@ -48,7 +49,7 @@
     return (gate_term, up_term, down_term)
 
 
-def on_device(tokens, cotangent, routes, gates, w_gate, w_up, w_down):
+def exchange_path(tokens, cotangent, routes, gates, w_gate, w_up, w_down):
     dp_count = lax.axis_size("dp")
     expert_count = lax.axis_size("expert")
     device_count = dp_count * expert_count
@@ -158,6 +159,220 @@
     )
 
 
+def select_lane(info, index):
+    lanes = lax.broadcasted_iota(jnp.int32, info.shape, info.ndim - 1)
+    return jnp.sum(jnp.where(lanes == index, info, jnp.zeros((), info.dtype)), axis=-1)
+
+
+def gather_path(tokens, cotangent, routes, gates, w_gate, w_up, w_down):
+    dp_count = lax.axis_size("dp")
+    expert_count = lax.axis_size("expert")
+    device_count = dp_count * expert_count
+    tok_local, model_width = tokens.shape
+    top_count = routes.shape[1]
+    most_rows = 7 * tok_local * top_count // (4 * device_count)
+    ring = expert_count // 2
+    bf16, f32 = jnp.bfloat16, jnp.float32
+
+    def swap_core(v):
+        return lax.ppermute(v, "dp", [(p, p ^ 1) for p in range(dp_count)])
+
+    def swap_x(v):
+        return lax.ppermute(v, "dp", [(p, p ^ 2) for p in range(dp_count)])
+
+    def swap_y(v):
+        return lax.ppermute(v, "expert", [(q, q ^ 1) for q in range(expert_count)])
+
+    def ring_up(v):
+        return lax.ppermute(
+            v, "expert", [(q, (q + 2) % expert_count) for q in range(expert_count)]
+        )
+
+    def ring_down(v):
+        return lax.ppermute(
+            v, "expert", [(q, (q - 2) % expert_count) for q in range(expert_count)]
+        )
+
+    dp_index = lax.axis_index("dp")
+    expert_index = lax.axis_index("expert")
+    mine = dp_index * expert_count + expert_index
+    other = (dp_index ^ 1) * expert_count + expert_index
+
+    hit = routes[:, :, None] == jnp.arange(device_count, dtype=jnp.int32)[None, None, :]
+    gate_dense = jnp.sum(jnp.where(hit, gates[:, :, None].astype(f32), 0.0), axis=1)
+    named = jnp.sum(hit.astype(f32), axis=1)
+    token_iota = jnp.arange(tok_local)
+    before = (token_iota[None, :] < token_iota[:, None]).astype(bf16)
+    rank = jnp.dot(before, named.astype(bf16), preferred_element_type=f32)
+    rank = jnp.where(named > 0.0, rank, -1.0)
+    info_width = -(-2 * device_count // 128) * 128
+    info = jnp.concatenate(
+        [
+            gate_dense.astype(bf16),
+            rank.astype(bf16),
+            jnp.zeros((tok_local, info_width - 2 * device_count), bf16),
+        ],
+        axis=1,
+    )
+
+    cuts = (0, 3 * model_width // 8, 3 * model_width // 4, model_width)
+
+    def part_of(v, n):
+        return v[:, cuts[n] : cuts[n + 1]]
+
+    def gather_zyx(v):
+        hops = [v]
+        for _ in range(ring - 1):
+            hops.append(ring_up(hops[-1]))
+        near = jnp.stack(hops)
+        far = swap_y(near)
+        both = jnp.stack([near, far])
+        return jnp.stack([both, swap_x(both)])
+
+    def gather_zxy(v):
+        hops = [v]
+        for _ in range(ring - 1):
+            hops.append(ring_up(hops[-1]))
+        near = jnp.stack(hops)
+        far = swap_x(near)
+        both = jnp.stack([near, far])
+        return jnp.stack([both, swap_y(both)], axis=1)
+
+    def gather_xyz(v):
+        pair = jnp.stack([v, swap_x(v)])
+        quad = jnp.stack([pair, swap_y(pair)], axis=1)
+        hops = [quad]
+        for _ in range(ring - 1):
+            hops.append(ring_up(hops[-1]))
+        return jnp.stack(hops, axis=2)
+
+    gathers = (gather_zyx, gather_zxy, gather_xyz)
+
+    def pick(places, v):
+        return jnp.einsum("ijrct,ijrtd->ijrcd", places, v, preferred_element_type=f32).astype(bf16)
+
+    def compact(v):
+        keep = pick(place_mine, v)
+        give = swap_core(pick(place_other, v))
+        return jnp.stack([keep, give]).reshape(2 * 4 * ring * most_rows, v.shape[-1])
+
+    token_parts = [part_of(tokens, n) for n in range(3)]
+    token_parts[0] = jnp.concatenate([info, token_parts[0]], axis=1)
+    got = [gathers[n](token_parts[n]) for n in range(3)]
+    got_info = got[0][..., :info_width]
+    slots = jnp.arange(most_rows, dtype=f32)
+
+    def places_of(index):
+        ranks = select_lane(got_info, device_count + index).astype(f32)
+        return (ranks[..., None, :] == slots[:, None]).astype(bf16)
+
+    place_mine = places_of(mine)
+    place_other = places_of(other)
+    rows = [compact(v) for v in got]
+    row_gate = select_lane(rows[0][:, :info_width], mine).astype(f32)[:, None]
+    rows[0] = rows[0][:, info_width:]
+    got_cot = [gathers[n](part_of(cotangent, n)) for n in range(3)]
+    cot_rows = [compact(v) for v in got_cot]
+
+    gate_matrix, up_matrix, down_matrix = w_gate[0], w_up[0], w_down[0]
+    x_rows = jnp.concatenate(rows, axis=1)
+    c_rows = jnp.concatenate(cot_rows, axis=1)
+    pre_gate = jnp.dot(x_rows, gate_matrix, preferred_element_type=f32)
+    pre_up = jnp.dot(x_rows, up_matrix, preferred_element_type=f32)
+    back = lax.dot_general(
+        c_rows, down_matrix, (((1,), (1,)), ((), ())), preferred_element_type=f32
+    )
+    sigmoid_gate = jax.nn.sigmoid(pre_gate)
+    silu_gate = pre_gate * sigmoid_gate
+    hidden = silu_gate * pre_up
+    gate_grad = jnp.sum(hidden * back, axis=1, keepdims=True)
+    weighted = (hidden * row_gate).astype(bf16)
+    hidden_grad = back * row_gate
+    pre_gate_grad = (
+        hidden_grad * pre_up * sigmoid_gate * (1.0 + pre_gate * (1.0 - sigmoid_gate))
+    ).astype(bf16)
+    pre_up_grad = (hidden_grad * silu_gate).astype(bf16)
+    lanes = lax.broadcasted_iota(jnp.int32, (1, info_width), 1)
+    gate_lanes = jnp.where(lanes == mine, gate_grad, 0.0).astype(bf16)
+
+    def row_grad_of(n):
+        matrix = slice(cuts[n], cuts[n + 1])
+        nt = (((1,), (1,)), ((), ()))
+        total = lax.dot_general(
+            pre_gate_grad, gate_matrix[matrix], nt, preferred_element_type=f32
+        ) + lax.dot_general(pre_up_grad, up_matrix[matrix], nt, preferred_element_type=f32)
+        return total.astype(bf16)
+
+    place_both = jnp.concatenate([place_mine, place_other], axis=-2)
+
+    def pair_rows(v):
+        halves = v.reshape(2, 2, 2, ring, most_rows, v.shape[-1])
+        return jnp.concatenate([halves[0], swap_core(halves[1])], axis=-2)
+
+    def spread(places, v):
+        return jnp.einsum("...ct,...cd->...td", places, v, preferred_element_type=f32)
+
+    def add(own, arrived):
+        return (own.astype(f32) + arrived.astype(f32)).astype(bf16)
+
+    def ring_sum(blocks):
+        moving = blocks[ring - 1]
+        for r in range(ring - 2, -1, -1):
+            moving = add(blocks[r], ring_down(moving))
+        return moving
+
+    def sum_xyz(v):
+        first = swap_x(spread(place_both[1], v[1]).astype(bf16))
+        both = (spread(place_both[0], v[0]) + first.astype(f32)).astype(bf16)
+        return ring_sum(add(both[0], swap_y(both[1])))
+
+    def sum_yxz(v):
+        first = swap_y(spread(place_both[:, 1], v[:, 1]).astype(bf16))
+        both = (spread(place_both[:, 0], v[:, 0]) + first.astype(f32)).astype(bf16)
+        return ring_sum(add(both[0], swap_x(both[1])))
+
+    def sum_zyx(v):
+        moving = spread(place_both[:, :, ring - 1], v[:, :, ring - 1]).astype(bf16)
+        for r in range(ring - 2, -1, -1):
+            here = spread(place_both[:, :, r], v[:, :, r])
+            moving = (here + ring_down(moving).astype(f32)).astype(bf16)
+        pair = add(moving[:, 0], swap_y(moving[:, 1]))
+        return add(pair[0], swap_x(pair[1]))
+
+    sums = (sum_xyz, sum_yxz, sum_zyx)
+    grads = []
+    for n in (2, 0, 1):
+        part = row_grad_of(n)
+        if n == 0:
+            part = jnp.concatenate([gate_lanes, part], axis=1)
+        grads.append(sums[n](pair_rows(part)))
+    grads = [grads[1], grads[2], grads[0]]
+    gate_back = grads[0][:, :device_count].astype(f32)
+    input_grad = jnp.concatenate([grads[0][:, info_width:], grads[1], grads[2]], axis=1)
+    gate_grad_out = jnp.sum(jnp.where(hit, gate_back[:, None, :], 0.0), axis=2).astype(bf16)
+
+    tn = (((0,), (0,)), ((), ()))
+    w_gate_grad = lax.dot_general(x_rows, pre_gate_grad, tn, preferred_element_type=f32)
+    w_up_grad = lax.dot_general(x_rows, pre_up_grad, tn, preferred_element_type=f32)
+    w_down_grad = lax.dot_general(weighted, c_rows, tn, preferred_element_type=f32)
+    return (
+        input_grad,
+        gate_grad_out,
+        w_gate_grad.astype(bf16)[None],
+        w_up_grad.astype(bf16)[None],
+        w_down_grad.astype(bf16)[None],
+    )
+
+
+def on_device(tokens, cotangent, routes, gates, w_gate, w_up, w_down):
+    dp_count = lax.axis_size("dp")
+    expert_count = lax.axis_size("expert")
+    gathered_bytes = dp_count * expert_count * tokens.size * 2
+    if dp_count == 4 and expert_count % 2 == 0 and gathered_bytes <= gather_limit:
+        return gather_path(tokens, cotangent, routes, gates, w_gate, w_up, w_down)
+    return exchange_path(tokens, cotangent, routes, gates, w_gate, w_up, w_down)
+
+
 def solution(mesh):
     in_specs = (
         P(("dp", "expert"), None),

time: 1060 us -> 424 us (0.40)
  blocking collectives: 362 us -> 0 us
  local copies, waits for them, and re-layouts: 187 us -> 33.6 us
  waiting for transfers between devices: 304 us -> 192 us
  starting transfers between devices: 14.7 us -> 46.9 us
  matrix products: 135 us -> 116 us
  other arithmetic: 39.9 us -> 29.1 us
    all_to_all x2 -> x0, blocking collectives: 362 us -> none  [the longest x1 193 us: on_device(): lax.all_to_all(gate_out, ('dp', 'expert'), split_axis=0, concat_axis=0, t...]
    all_to_all x3 -> x0, waiting for transfers between devices: 304 us -> none  [the longest x1 157 us: on_device(): lax.all_to_all(send_tokens, ('dp', 'expert'), split_axis=0, concat_axis=0...]
    ppermute x0 -> x54, waiting for transfers between devices: none -> 192 us  [the longest x18 75.5 us: ring_up(): lax.ppermute(v, 'expert', [(q, (q + 2) % expert_count) for q in range(exp...]
    gather x17 -> x0, local copies, waits for them, and re-layouts: 106 us -> none  [the longest x4 25.6 us: block_step(): got_tokens[safe_pick]]
    scatter x10 -> x0, local copies, waits for them, and re-layouts: 61.3 us -> none  [the longest x4 41.1 us: block_step(): grad_slots = grad_slots.at[target].set(row_grad, mode='drop')]
    ppermute x0 -> x54, starting transfers between devices: none -> 46.9 us  [the longest x9 13.9 us: ring_down(): lax.ppermute(v, 'expert', [(q, (q - 2) % expert_count) for q in range(exp...]
    dot_general x36 -> x33, matrix products: 135 us -> 116 us  [the longest x12 20.4 us: pick(): jnp.einsum('ijrct,ijrtd->ijrcd', places, v, preferred_element_type=f32)]
    all_to_all x3 -> x0, starting transfers between devices: 14.7 us -> none  [the longest x1 7.3 us: on_device(): lax.all_to_all(send_weight, ('dp', 'expert'), split_axis=0, concat_axis=0...]
  transfers between devices with their start and end apart: 3 -> 54, of which waited for: 2 -> 28; matrix products, arithmetic and copies ran while one was open for 5% -> 28% of each run, Pallas kernels for 0% -> 0%
where the time goes in v1:
time: 424 us; the launch traced here: 419 us
  waiting for transfers between devices  192 us (45%)
  matrix products  116 us (27%)
  starting transfers between devices  46.9 us (11%)
  local copies, waits for them, and re-layouts  33.6 us (8%)
  other arithmetic  29.1 us (7%)
    ppermute x18, waiting for transfers between devices, ring_up(): lax.ppermute(v, 'expert', [(q, (q + 2) % expert_count) for q in range(exp...  75.5 us
    ppermute x9, waiting for transfers between devices, swap_x(): return lax.ppermute(v, 'dp', [(p, p ^ 2) for p in range(dp_count)])  53.5 us
    ppermute x9, waiting for transfers between devices, swap_y(): return lax.ppermute(v, 'expert', [(q, q ^ 1) for q in range(expert_count)])  35.4 us
    ppermute x9, waiting for transfers between devices, ring_down(): lax.ppermute(v, 'expert', [(q, (q - 2) % expert_count) for q in range(exp...  27.3 us
    dot_general x12, matrix products, pick(): jnp.einsum('ijrct,ijrtd->ijrcd', places, v, preferred_element_type=f32)  20.4 us
    dot_general x1, matrix products, gather_path(): lax.dot_general(c_rows, down_matrix, (((1,), (1,)), ((), ())), preferred_...  14.2 us
    ppermute x9, starting transfers between devices, ring_down(): lax.ppermute(v, 'expert', [(q, (q - 2) % expert_count) for q in range(exp...  13.9 us
    ppermute x9, starting transfers between devices, swap_y(): return lax.ppermute(v, 'expert', [(q, q ^ 1) for q in range(expert_count)])  12.8 us
  transfers between devices with their start and end apart: 54, of which 28 were waited for; matrix products, arithmetic and copies ran while one was open for 28% of the time, Pallas kernels for 0%

profile of v1, /device:TPU:0, one launch (start us, length us, event | category | flops | bytes accessed | tf_op | source)
XLA Modules:
  0.0 418.8 jit_solution(3280335972801284415)
XLA Ops:
  0.6 1.9 slice_bitcast_fusion.28
  6.5 3.1 collective-permute-start
  9.6 7.6 %collective-permute-done = bf16[128,896]{1,0:T(8,128)(2,1)S(1)} collective-permute-done((bf16[128,896]{1,0:T(8,128)(2,1)S(1)}, bf16[128,896]{1,0:T(8,128)(2,1)S(1)}, u32[]{:S(2)}, u32[]{:S(2)}) %collective-permute-start) | collective-permute-done | bytes 229408 | tf_op jit(solution)/shard_map/ppermute | solution.py:187
  21.2 6.3 %collective-permute-done.1 = bf16[128,896]{1,0:T(8,128)(2,1)S(1)} collective-permute-done((bf16[128,896]{1,0:T(8,128)(2,1)S(1)}, bf16[128,896]{1,0:T(8,128)(2,1)S(1)}, u32[]{:S(2)}, u32[]{:S(2)}) %collective-permute-start.1) | collective-permute-done | bytes 229408 | tf_op jit(solution)/shard_map/ppermute | solution.py:187
  28.5 3.3 collective-permute-done.18
  31.8 9.1 %collective-permute-done.2 = bf16[128,896]{1,0:T(8,128)(2,1)S(1)} collective-permute-done((bf16[128,896]{1,0:T(8,128)(2,1)S(1)}, bf16[128,896]{1,0:T(8,128)(2,1)S(1)}, u32[]{:S(2)}, u32[]{:S(2)}) %collective-permute-start.2) | collective-permute-done | bytes 229408 | tf_op jit(solution)/shard_map/ppermute | solution.py:187
  47.1 5.2 %collective-permute-done.25 = bf16[128,768]{1,0:T(8,128)(2,1)S(1)} collective-permute-done((bf16[128,768]{1,0:T(8,128)(2,1)S(1)}, bf16[128,768]{1,0:T(8,128)(2,1)S(1)}, u32[]{:S(2)}, u32[]{:S(2)}) %collective-permute-start.25) | collective-permute-done | bytes 196640 | tf_op jit(solution)/shard_map/ppermute | solution.py:187
  52.3 4.2 %collective-permute-done.20 = bf16[128,768]{1,0:T(8,128)(2,1)S(1)} collective-permute-done((bf16[128,768]{1,0:T(8,128)(2,1)S(1)}, bf16[128,768]{1,0:T(8,128)(2,1)S(1)}, u32[]{:S(2)}, u32[]{:S(2)}) %collective-permute-start.20) | collective-permute-done | bytes 196640 | tf_op jit(solution)/shard_map/ppermute | solution.py:187
  58.2 2.7 collective-permute-done.26
  64.4 2.1 fusion.140
  68.4 15.8 %collective-permute-done.31 = bf16[2,128,512]{2,1,0:T(8,128)(2,1)S(1)} collective-permute-done((bf16[2,128,512]{2,1,0:T(8,128)(2,1)S(1)}, bf16[2,128,512]{2,1,0:T(8,128)(2,1)S(1)}, u32[]{:S(2)}, u32[]{:S(2)}) %collective-permute-start.31) | collective-permute-done | bytes 262176 | tf_op jit(solution)/shard_map/ppermute | solution.py:184
  86.6 1.8 fusion.135
  88.4 4.7 %collective-permute-done.8 = bf16[128,768]{1,0:T(8,128)(2,1)S(1)} collective-permute-done((bf16[128,768]{1,0:T(8,128)(2,1)S(1)}, bf16[128,768]{1,0:T(8,128)(2,1)S(1)}, u32[]{:S(2)}, u32[]{:S(2)}) %collective-permute-start.8) | collective-permute-done | bytes 196640 | tf_op jit(solution)/shard_map/ppermute | solution.py:187
  96.2 1.9 fusion.134
  99.9 2.0 collective-permute-done.32
  102.0 15.1 %collective-permute-done.14 = bf16[2,2,128,512]{3,2,1,0:T(8,128)(2,1)} collective-permute-done((bf16[2,2,128,512]{3,2,1,0:T(8,128)(2,1)S(1)}, bf16[2,2,128,512]{3,2,1,0:T(8,128)(2,1)}, u32[]{:S(2)}, u32[]{:S(2)}) %collective-permute-start.14) | collective-permute-done | bytes 524320 | tf_op jit(solution)/shard_map/ppermute | solution.py:187
  117.0 52.1 %collective-permute-done.9 = bf16[4,128,768]{2,1,0:T(8,128)(2,1)} collective-permute-done((bf16[4,128,768]{2,1,0:T(8,128)(2,1)S(1)}, bf16[4,128,768]{2,1,0:T(8,128)(2,1)}, u32[]{:S(2)}, u32[]{:S(2)}) %collective-permute-start.9) | collective-permute-done | bytes 786464 | tf_op jit(solution)/shard_map/ppermute | solution.py:181
  169.2 1.7 fusion.136
  172.6 9.2 %collective-permute-done.15 = bf16[2,2,128,512]{3,2,1,0:T(8,128)(2,1)} collective-permute-done((bf16[2,2,128,512]{3,2,1,0:T(8,128)(2,1)}, bf16[2,2,128,512]{3,2,1,0:T(8,128)(2,1)}, u32[]{:S(2)}, u32[]{:S(2)}) %collective-permute-start.15) | collective-permute-done | bytes 524320 | tf_op jit(solution)/shard_map/ppermute | solution.py:187
  183.6 2.1 fusion.26
  185.8 2.0 fusion.28
  188.3 2.0 fusion.39
  190.3 2.1 fusion.38
  192.4 4.8 %collective-permute-done.34 = bf16[2,2,128,512]{3,2,1,0:T(8,128)(2,1)S(1)} collective-permute-done((bf16[2,2,128,512]{3,2,1,0:T(8,128)(2,1)}, bf16[2,2,128,512]{3,2,1,0:T(8,128)(2,1)S(1)}, u32[]{:S(2)}, u32[]{:S(2)}) %collective-permute-start.34) | collective-permute-done | bytes 524320 | tf_op jit(solution)/shard_map/ppermute | solution.py:187
  198.9 2.2 fusion.37
  201.2 2.3 fusion.21
  213.3 1.9 pad_maximum_fusion.10
  215.2 1.8 pad_maximum_fusion.11
  218.6 2.7 copy-done.24
  221.3 8.9 %fusion.5 = f32[1792,768]{0,1:T(8,128)} fusion(bf16[1,2048,768]{2,1,0:T(8,128)(2,1)S(1)} %copy-done.24, bf16[1792,512]{1,0:T(8,128)(2,1)S(1)} %bitcast.277, bf16[1792,768]{1,0:T(8,128)(2,1)S(1)} %bitcast.269, bf16[1792,768]{1,0:T(8,128)(2,1)S(1)} %slice.250), kind=kOutput, calls=%fused_computation.28 | convolution fusion | flops 5659164672 | bytes 15990784 | tf_op jit(solution)/shard_map/dot_general | solution.py:280
  230.2 8.7 %fusion.3 = f32[1792,768]{0,1:T(8,128)} fusion(bf16[1,2048,768]{2,1,0:T(8,128)(2,1)S(1)} %copy-done.26, bf16[1792,512]{1,0:T(8,128)(2,1)S(1)} %bitcast.278, bf16[1792,768]{1,0:T(8,128)(2,1)S(1)} %bitcast.270, bf16[1792,768]{1,0:T(8,128)(2,1)S(1)} %slice.250), kind=kOutput, calls=%fused_computation.26 | convolution fusion | flops 5659164672 | bytes 15990784 | tf_op jit(solution)/shard_map/dot_general | solution.py:281
  239.0 2.0 copy.128
  242.2 14.2 %multiply_reduce_fusion = (bf16[1792]{0:T(1024)(128)(2,1)S(1)}, bf16[1792,768]{0,1:T(8,128)(2,1)S(1)}, bf16[1792,768]{0,1:T(8,128)(2,1)}) fusion(f32[1792,768]{0,1:T(8,128)} %fusion.3, f32[1792,768]{0,1:T(8,128)} %fusion.5, f32[1792]{0:T(1024)S(1)} %convert_element_type.297, bf16[1,768,2048]{2,1,0:T(8,128)(2,1)S(1)} %copy-done, ...), kind=kOutput, calls=%fused_computation.7 | convolution fusion | flops 5682558976 | bytes 27011584 | tf_op jit(solution)/shard_map/dot_general | solution.py:282
  257.9 2.3 fusion.50
  260.2 3.6 fusion.58
  264.0 2.3 add_convert_fusion.1
  266.3 1.7 add_convert_fusion.2
  271.5 2.8 copy.98
  276.1 4.5 %fusion.47 = f32[1792,768]{1,0:T(8,128)S(1)} fusion(bf16[1792,768]{0,1:T(8,128)(2,1)} %copy-done.28, bf16[1,2048,768]{2,1,0:T(8,128)(2,1)} %param.11), kind=kOutput, calls=%fused_computation.97 | convolution fusion | flops 2113929216 | bytes 9437184 | tf_op jit(solution)/shard_map/dot_general | solution.py:301
  284.0 3.8 add_convert_fusion
  290.3 7.0 %collective-permute-done.49 = bf16[2,2,128,512]{2,3,0,1:T(8,128)(2,1)S(1)} collective-permute-done((bf16[2,2,128,512]{2,3,0,1:T(8,128)(2,1)S(1)}, bf16[2,2,128,512]{2,3,0,1:T(8,128)(2,1)S(1)}, u32[]{:S(2)}, u32[]{:S(2)}) %collective-permute-start.49) | collective-permute-done | bytes 524320 | tf_op jit(solution)/shard_map/ppermute | solution.py:192
  298.4 2.3 collective-permute-start.50
  300.8 11.9 %fusion.9 = bf16[1,768,2048]{2,1,0:T(8,128)(2,1)} fusion(bf16[1792,512]{1,0:T(8,128)(2,1)S(1)} %bitcast.282, bf16[1792,768]{1,0:T(8,128)(2,1)S(1)} %bitcast.276, bf16[1792,768]{1,0:T(8,128)(2,1)S(1)} %bitcast.274, f32[1792]{0:T(1024)S(1)} %copy-done.23, f32[1792,768]{0,1:T(8,128)} %fusion.3, f32[1792,768]{0,1:T(8,128)} %fusion.5), kind=kOutput, calls=%fused_computation.33 | convolution fusion | flops 5670371328 | bytes 21502976 | tf_op jit(solution)/shard_map/dot_general | solution.py:357
  312.6 2.9 copy.97
  320.6 1.8 collective-permute-start.43
  324.7 6.5 %collective-permute-done.51 = bf16[2,2,128,512]{2,3,0,1:T(8,128)(2,1)S(1)} collective-permute-done((bf16[2,2,128,512]{2,3,0,1:T(8,128)(2,1)S(1)}, bf16[2,2,128,512]{2,3,0,1:T(8,128)(2,1)S(1)}, u32[]{:S(2)}, u32[]{:S(2)}) %collective-permute-start.51) | collective-permute-done | bytes 524320 | tf_op jit(solution)/shard_map/ppermute | solution.py:192
  331.6 1.8 collective-permute-start.52
  333.4 12.2 %fusion.8 = bf16[1,2048,768]{2,1,0:T(8,128)(2,1)} fusion(bf16[1792,768]{0,1:T(8,128)(2,1)} %get-tuple-element.16, bf16[1792,512]{1,0:T(8,128)(2,1)} %bitcast.279, bf16[1792,768]{1,0:T(8,128)(2,1)S(1)} %bitcast.271, bf16[1792,768]{1,0:T(8,128)(2,1)S(1)} %copy-done.6), kind=kOutput, calls=%fused_computation.32 | convolution fusion | flops 5660737536 | bytes 13238272 | tf_op jit(solution)/shard_map/dot_general | solution.py:356
  345.6 16.0 %collective-permute-done.52 = bf16[2,128,512]{1,2,0:T(8,128)(2,1)} collective-permute-done((bf16[2,128,512]{1,2,0:T(8,128)(2,1)S(1)}, bf16[2,128,512]{1,2,0:T(8,128)(2,1)}, u32[]{:S(2)}, u32[]{:S(2)}) %collective-permute-start.52) | collective-permute-done | bytes 262176 | tf_op jit(solution)/shard_map/ppermute | solution.py:184
  364.2 2.2 add_convert_fusion.4
  367.9 2.4 add_convert_fusion.3
  370.4 1.8 collective-permute-start.38
  372.2 12.0 %fusion.7 = bf16[1,2048,768]{2,1,0:T(8,128)(2,1)} fusion(bf16[1792,768]{0,1:T(8,128)(2,1)} %copy-done.28, bf16[1792,512]{1,0:T(8,128)(2,1)S(1)} %bitcast.280, bf16[1792,768]{1,0:T(8,128)(2,1)S(1)} %bitcast.272, bf16[1792,768]{1,0:T(8,128)(2,1)S(1)} %copy-done.6), kind=kOutput, calls=%fused_computation.31 | convolution fusion | flops 5660737536 | bytes 13238272 | tf_op jit(solution)/shard_map/dot_general | solution.py:355
  386.8 3.4 collective-permute-done.38
  391.0 3.1 collective-permute-done.45
  394.1 2.4 collective-permute-start.46
  396.5 2.6 collective-permute-done.39
  399.1 2.2 collective-permute-start.40
  401.3 2.0 collective-permute-done.46
  403.4 2.8 collective-permute-start.47
  406.1 2.1 collective-permute-done.40
  408.3 2.5 collective-permute-start.41
  412.5 2.5 collective-permute-done.41
  415.9 2.0 copy.111
  (216 shorter events, 80.4 us)
Async XLA Ops:
  0.6 241.5 %copy-start = (bf16[1,768,2048]{2,1,0:T(8,128)(2,1)S(1)}, bf16[1,768,2048]{2,1,0:T(8,128)(2,1)}, u32[]{:S(2)}) copy-start(bf16[1,768,2048]{2,1,0:T(8,128)(2,1)} %param.13) | copy-start | bytes 9437188
  5.5 40.2 %copy-start.20 = (bf16[128,768]{1,0:T(8,128)(2,1)S(1)}, bf16[128,768]{1,0:T(8,128)(2,1)}, u32[]{:S(2)}) copy-start(bf16[128,768]{1,0:T(8,128)(2,1)} %get-tuple-element.53) | copy-start | bytes 589828
  6.5 10.7 %collective-permute-start = (bf16[128,896]{1,0:T(8,128)(2,1)S(1)}, bf16[128,896]{1,0:T(8,128)(2,1)S(1)}, u32[]{:S(2)}, u32[]{:S(2)}) collective-permute-start(bf16[128,896]{1,0:T(8,128)(2,1)S(1)} %pad_maximum_fusion.68), channel_id=1, source_target_pairs={{0,2},{1,3},{2,4},{3,5},{4,6},{5,7},{6,0},{7,1},{8,10},{9,11},{10,... | collective-permute-start | bytes 688136 | tf_op jit(solution)/shard_map/ppermute | solution.py:187
  17.2 10.3 %collective-permute-start.1 = (bf16[128,896]{1,0:T(8,128)(2,1)S(1)}, bf16[128,896]{1,0:T(8,128)(2,1)S(1)}, u32[]{:S(2)}, u32[]{:S(2)}) collective-permute-start(bf16[128,896]{1,0:T(8,128)(2,1)S(1)} %collective-permute-done), channel_id=1, source_target_pairs={{0,2},{1,3},{2,4},{3,5},{4,6},{5,7},{6,0},{7,1},{8,10},{9,11},{10,... | collective-permute-start | bytes 688136 | tf_op jit(solution)/shard_map/ppermute | solution.py:187
  18.3 13.5 %collective-permute-start.18 = (bf16[128,768]{1,0:T(8,128)(2,1)S(1)}, bf16[128,768]{1,0:T(8,128)(2,1)S(1)}, u32[]{:S(2)}, u32[]{:S(2)}) collective-permute-start(bf16[128,768]{1,0:T(8,128)(2,1)S(1)} %get-tuple-element.45), channel_id=1, source_target_pairs={{0,2},{1,3},{2,4},{3,5},{4,6},{5,7},{6,0},{7,1},{8,10},{9,11},{10,... | collective-permute-start | bytes 589832 | tf_op jit(solution)/shard_map/ppermute | solution.py:187
  19.7 23.0 %collective-permute-start.24 = (bf16[128,768]{1,0:T(8,128)(2,1)S(1)}, bf16[128,768]{1,0:T(8,128)(2,1)S(1)}, u32[]{:S(2)}, u32[]{:S(2)}) collective-permute-start(bf16[128,768]{1,0:T(8,128)(2,1)S(1)} %get-tuple-element.46), channel_id=1, source_target_pairs={{0,2},{1,3},{2,4},{3,5},{4,6},{5,7},{6,0},{7,1},{8,10},{9,11},{10,... | collective-permute-start | bytes 589832 | tf_op jit(solution)/shard_map/ppermute | solution.py:187
  27.6 13.3 %collective-permute-start.2 = (bf16[128,896]{1,0:T(8,128)(2,1)S(1)}, bf16[128,896]{1,0:T(8,128)(2,1)S(1)}, u32[]{:S(2)}, u32[]{:S(2)}) collective-permute-start(bf16[128,896]{1,0:T(8,128)(2,1)S(1)} %collective-permute-done.1), channel_id=1, source_target_pairs={{0,2},{1,3},{2,4},{3,5},{4,6},{5,7},{6,0},{7,1},{8,10},{9,11},{10,... | collective-permute-start | bytes 688136 | tf_op jit(solution)/shard_map/ppermute | solution.py:187
  31.8 12.0 %collective-permute-start.19 = (bf16[128,768]{1,0:T(8,128)(2,1)S(1)}, bf16[128,768]{1,0:T(8,128)(2,1)S(1)}, u32[]{:S(2)}, u32[]{:S(2)}) collective-permute-start(bf16[128,768]{1,0:T(8,128)(2,1)S(1)} %collective-permute-done.18), channel_id=1, source_target_pairs={{0,2},{1,3},{2,4},{3,5},{4,6},{5,7},{6,0},{7,1},{8,10},{9,11},{10,... | collective-permute-start | bytes 589832 | tf_op jit(solution)/shard_map/ppermute | solution.py:187
  41.1 23.4 %collective-permute-start.3 = (bf16[4,128,896]{2,1,0:T(8,128)(2,1)S(1)}, bf16[4,128,896]{2,1,0:T(8,128)(2,1)S(1)}, u32[]{:S(2)}, u32[]{:S(2)}) collective-permute-start(bf16[4,128,896]{2,1,0:T(8,128)(2,1)S(1)} %get-tuple-element.36), channel_id=1, source_target_pairs={{0,1},{1,0},{2,3},{3,2},{4,5},{5,4},{6,7},{7,6},{8,9},{9,8},{10,11... | collective-permute-start | bytes 2752520 | tf_op jit(solution)/shard_map/ppermute | solution.py:184
  42.7 9.6 %collective-permute-start.25 = (bf16[128,768]{1,0:T(8,128)(2,1)S(1)}, bf16[128,768]{1,0:T(8,128)(2,1)S(1)}, u32[]{:S(2)}, u32[]{:S(2)}) collective-permute-start(bf16[128,768]{1,0:T(8,128)(2,1)S(1)} %collective-permute-done.24), channel_id=1, source_target_pairs={{0,2},{1,3},{2,4},{3,5},{4,6},{5,7},{6,0},{7,1},{8,10},{9,11},{10,... | collective-permute-start | bytes 589832 | tf_op jit(solution)/shard_map/ppermute | solution.py:187
  43.8 12.7 %collective-permute-start.20 = (bf16[128,768]{1,0:T(8,128)(2,1)S(1)}, bf16[128,768]{1,0:T(8,128)(2,1)S(1)}, u32[]{:S(2)}, u32[]{:S(2)}) collective-permute-start(bf16[128,768]{1,0:T(8,128)(2,1)S(1)} %collective-permute-done.19), channel_id=1, source_target_pairs={{0,2},{1,3},{2,4},{3,5},{4,6},{5,7},{6,0},{7,1},{8,10},{9,11},{10,... | collective-permute-start | bytes 589832 | tf_op jit(solution)/shard_map/ppermute | solution.py:187
  44.7 17.3 %collective-permute-start.30 = (bf16[128,512]{1,0:T(8,128)(2,1)S(1)}, bf16[128,512]{1,0:T(8,128)(2,1)S(1)}, u32[]{:S(2)}, u32[]{:S(2)}) collective-permute-start(bf16[128,512]{1,0:T(8,128)(2,1)S(1)} %get-tuple-element.50), channel_id=1, source_target_pairs={{0,16},{8,24},{16,0},{24,8},{1,17},{9,25},{17,1},{25,9},{2,18},{10... | collective-permute-start | bytes 393224 | tf_op jit(solution)/shard_map/ppermute | solution.py:181
  45.8 17.4 %collective-permute-start.6 = (bf16[128,768]{1,0:T(8,128)(2,1)S(1)}, bf16[128,768]{1,0:T(8,128)(2,1)S(1)}, u32[]{:S(2)}, u32[]{:S(2)}) collective-permute-start(bf16[128,768]{1,0:T(8,128)(2,1)S(1)} %copy-done.20), channel_id=1, source_target_pairs={{0,2},{1,3},{2,4},{3,5},{4,6},{5,7},{6,0},{7,1},{8,10},{9,11},{10,... | collective-permute-start | bytes 589832 | tf_op jit(solution)/shard_map/ppermute | solution.py:187
  52.3 8.6 %collective-permute-start.26 = (bf16[128,768]{1,0:T(8,128)(2,1)S(1)}, bf16[128,768]{1,0:T(8,128)(2,1)S(1)}, u32[]{:S(2)}, u32[]{:S(2)}) collective-permute-start(bf16[128,768]{1,0:T(8,128)(2,1)S(1)} %collective-permute-done.25), channel_id=1, source_target_pairs={{0,2},{1,3},{2,4},{3,5},{4,6},{5,7},{6,0},{7,1},{8,10},{9,11},{10,... | collective-permute-start | bytes 589832 | tf_op jit(solution)/shard_map/ppermute | solution.py:187
  56.7 29.9 %collective-permute-start.21 = (bf16[4,128,768]{2,1,0:T(8,128)(2,1)S(1)}, bf16[4,128,768]{2,1,0:T(8,128)(2,1)S(1)}, u32[]{:S(2)}, u32[]{:S(2)}) collective-permute-start(bf16[4,128,768]{2,1,0:T(8,128)(2,1)S(1)} %get-tuple-element.38), channel_id=1, source_target_pairs={{0,1},{1,0},{2,3},{3,2},{4,5},{5,4},{6,7},{7,6},{8,9},{9,8},{10,11... | collective-permute-start | bytes 2359304 | tf_op jit(solution)/shard_map/ppermute | solution.py:184
  60.9 6.4 %collective-permute-start.12 = (bf16[128,512]{1,0:T(8,128)(2,1)S(1)}, bf16[128,512]{1,0:T(8,128)(2,1)S(1)}, u32[]{:S(2)}, u32[]{:S(2)}) collective-permute-start(bf16[128,512]{1,0:T(8,128)(2,1)S(1)} %get-tuple-element.57), channel_id=1, source_target_pairs={{0,16},{8,24},{16,0},{24,8},{1,17},{9,25},{17,1},{25,9},{2,18},{10... | collective-permute-start | bytes 393224 | tf_op jit(solution)/shard_map/ppermute | solution.py:181
  62.0 33.6 %collective-permute-start.27 = (bf16[4,128,768]{2,1,0:T(8,128)(2,1)S(1)}, bf16[4,128,768]{2,1,0:T(8,128)(2,1)S(1)}, u32[]{:S(2)}, u32[]{:S(2)}) collective-permute-start(bf16[4,128,768]{2,1,0:T(8,128)(2,1)S(1)} %get-tuple-element.40), channel_id=1, source_target_pairs={{0,16},{8,24},{16,0},{24,8},{1,17},{9,25},{17,1},{25,9},{2,18},{10... | collective-permute-start | bytes 2359304 | tf_op jit(solution)/shard_map/ppermute | solution.py:181
  63.2 21.0 %collective-permute-start.31 = (bf16[2,128,512]{2,1,0:T(8,128)(2,1)S(1)}, bf16[2,128,512]{2,1,0:T(8,128)(2,1)S(1)}, u32[]{:S(2)}, u32[]{:S(2)}) collective-permute-start(bf16[2,128,512]{2,1,0:T(8,128)(2,1)S(1)} %get-tuple-element.59), channel_id=1, source_target_pairs={{0,1},{1,0},{2,3},{3,2},{4,5},{5,4},{6,7},{7,6},{8,9},{9,8},{10,11... | collective-permute-start | bytes 786440 | tf_op jit(solution)/shard_map/ppermute | solution.py:184
  64.4 21.2 %collective-permute-start.7 = (bf16[128,768]{1,0:T(8,128)(2,1)S(1)}, bf16[128,768]{1,0:T(8,128)(2,1)S(1)}, u32[]{:S(2)}, u32[]{:S(2)}) collective-permute-start(bf16[128,768]{1,0:T(8,128)(2,1)S(1)} %collective-permute-done.6), channel_id=1, source_target_pairs={{0,2},{1,3},{2,4},{3,5},{4,6},{5,7},{6,0},{7,1},{8,10},{9,11},{10,... | collective-permute-start | bytes 589832 | tf_op jit(solution)/shard_map/ppermute | solution.py:187
  67.3 114.4 %collective-permute-start.4 = (bf16[2,4,128,896]{3,2,1,0:T(8,128)(2,1)}, bf16[2,4,128,896]{3,2,1,0:T(8,128)(2,1)}, u32[]{:S(2)}, u32[]{:S(2)}) collective-permute-start(bf16[2,4,128,896]{3,2,1,0:T(8,128)(2,1)} %get-tuple-element.28), channel_id=1, source_target_pairs={{0,16},{8,24},{16,0},{24,8},{1,17},{9,25},{17,1},{25,9},{2,18},{10... | collective-permute-start | bytes 5505032 | tf_op jit(solution)/shard_map/ppermute | solution.py:181
  84.1 13.9 %collective-permute-start.13 = (bf16[2,128,512]{2,1,0:T(8,128)(2,1)S(1)}, bf16[2,128,512]{2,1,0:T(8,128)(2,1)S(1)}, u32[]{:S(2)}, u32[]{:S(2)}) collective-permute-start(bf16[2,128,512]{2,1,0:T(8,128)(2,1)S(1)} %get-tuple-element.61), channel_id=1, source_target_pairs={{0,1},{1,0},{2,3},{3,2},{4,5},{5,4},{6,7},{7,6},{8,9},{9,8},{10,11... | collective-permute-start | bytes 786440 | tf_op jit(solution)/shard_map/ppermute | solution.py:184
  85.7 7.5 %collective-permute-start.8 = (bf16[128,768]{1,0:T(8,128)(2,1)S(1)}, bf16[128,768]{1,0:T(8,128)(2,1)S(1)}, u32[]{:S(2)}, u32[]{:S(2)}) collective-permute-start(bf16[128,768]{1,0:T(8,128)(2,1)S(1)} %collective-permute-done.7), channel_id=1, source_target_pairs={{0,2},{1,3},{2,4},{3,5},{4,6},{5,7},{6,0},{7,1},{8,10},{9,11},{10,... | collective-permute-start | bytes 589832 | tf_op jit(solution)/shard_map/ppermute | solution.py:187
  86.6 15.4 %collective-permute-start.32 = (bf16[2,2,128,512]{3,2,1,0:T(8,128)(2,1)S(1)}, bf16[2,2,128,512]{3,2,1,0:T(8,128)(2,1)}, u32[]{:S(2)}, u32[]{:S(2)}) collective-permute-start(bf16[2,2,128,512]{3,2,1,0:T(8,128)(2,1)S(1)} %get-tuple-element.48), channel_id=1, source_target_pairs={{0,2},{1,3},{2,4},{3,5},{4,6},{5,7},{6,0},{7,1},{8,10},{9,11},{10,... | collective-permute-start | bytes 1572872 | tf_op jit(solution)/shard_map/ppermute | solution.py:187
  93.1 90.4 %collective-permute-start.22 = (bf16[2,4,128,768]{3,2,1,0:T(8,128)(2,1)}, bf16[2,4,128,768]{3,2,1,0:T(8,128)(2,1)}, u32[]{:S(2)}, u32[]{:S(2)}) collective-permute-start(bf16[2,4,128,768]{3,2,1,0:T(8,128)(2,1)} %get-tuple-element.30), channel_id=1, source_target_pairs={{0,16},{8,24},{16,0},{24,8},{1,17},{9,25},{17,1},{25,9},{2,18},{10... | collective-permute-start | bytes 4718600 | tf_op jit(solution)/shard_map/ppermute | solution.py:181
  95.7 73.5 %collective-permute-start.9 = (bf16[4,128,768]{2,1,0:T(8,128)(2,1)S(1)}, bf16[4,128,768]{2,1,0:T(8,128)(2,1)}, u32[]{:S(2)}, u32[]{:S(2)}) collective-permute-start(bf16[4,128,768]{2,1,0:T(8,128)(2,1)S(1)} %get-tuple-element.42), channel_id=1, source_target_pairs={{0,16},{8,24},{16,0},{24,8},{1,17},{9,25},{17,1},{25,9},{2,18},{10... | collective-permute-start | bytes 2359304 | tf_op jit(solution)/shard_map/ppermute | solution.py:181
  98.1 87.7 %collective-permute-start.28 = (bf16[2,4,128,768]{3,2,1,0:T(8,128)(2,1)}, bf16[2,4,128,768]{3,2,1,0:T(8,128)(2,1)}, u32[]{:S(2)}, u32[]{:S(2)}) collective-permute-start(bf16[2,4,128,768]{3,2,1,0:T(8,128)(2,1)} %get-tuple-element.32), channel_id=1, source_target_pairs={{0,1},{1,0},{2,3},{3,2},{4,5},{5,4},{6,7},{7,6},{8,9},{9,8},{10,11... | collective-permute-start | bytes 4718600 | tf_op jit(solution)/shard_map/ppermute | solution.py:184
  102.0 15.1 %collective-permute-start.14 = (bf16[2,2,128,512]{3,2,1,0:T(8,128)(2,1)S(1)}, bf16[2,2,128,512]{3,2,1,0:T(8,128)(2,1)}, u32[]{:S(2)}, u32[]{:S(2)}) collective-permute-start(bf16[2,2,128,512]{3,2,1,0:T(8,128)(2,1)S(1)} %get-tuple-element.55), channel_id=1, source_target_pairs={{0,2},{1,3},{2,4},{3,5},{4,6},{5,7},{6,0},{7,1},{8,10},{9,11},{10,... | collective-permute-start | bytes 1572872 | tf_op jit(solution)/shard_map/ppermute | solution.py:187
  117.0 53.9 %collective-permute-start.33 = (bf16[2,2,128,512]{3,2,1,0:T(8,128)(2,1)}, bf16[2,2,128,512]{3,2,1,0:T(8,128)(2,1)}, u32[]{:S(2)}, u32[]{:S(2)}) collective-permute-start(bf16[2,2,128,512]{3,2,1,0:T(8,128)(2,1)} %collective-permute-done.32), channel_id=1, source_target_pairs={{0,2},{1,3},{2,4},{3,5},{4,6},{5,7},{6,0},{7,1},{8,10},{9,11},{10,... | collective-permute-start | bytes 1572872 | tf_op jit(solution)/shard_map/ppermute | solution.py:187
  169.2 12.6 %collective-permute-start.15 = (bf16[2,2,128,512]{3,2,1,0:T(8,128)(2,1)}, bf16[2,2,128,512]{3,2,1,0:T(8,128)(2,1)}, u32[]{:S(2)}, u32[]{:S(2)}) collective-permute-start(bf16[2,2,128,512]{3,2,1,0:T(8,128)(2,1)} %collective-permute-done.14), channel_id=1, source_target_pairs={{0,2},{1,3},{2,4},{3,5},{4,6},{5,7},{6,0},{7,1},{8,10},{9,11},{10,... | collective-permute-start | bytes 1572872 | tf_op jit(solution)/shard_map/ppermute | solution.py:187
  169.2 13.0 %copy-start.2 = (bf16[1,2,4,128,896]{4,3,2,1,0:T(8,128)(2,1)S(1)}, bf16[1,2,4,128,896]{4,3,2,1,0:T(8,128)(2,1)}, u32[]{:S(2)}) copy-start(bf16[1,2,4,128,896]{4,3,2,1,0:T(8,128)(2,1)} %get-tuple-element.27) | copy-start | bytes 5505028
  170.9 34.8 %collective-permute-start.10 = (bf16[2,4,128,768]{3,2,1,0:T(8,128)(2,1)S(1)}, bf16[2,4,128,768]{3,2,1,0:T(8,128)(2,1)S(1)}, u32[]{:S(2)}, u32[]{:S(2)}) collective-permute-start(bf16[2,4,128,768]{3,2,1,0:T(8,128)(2,1)S(1)} %get-tuple-element.34), channel_id=1, source_target_pairs={{0,1},{1,0},{2,3},{3,2},{4,5},{5,4},{6,7},{7,6},{8,9},{9,8},{10,11... | collective-permute-start | bytes 4718600 | tf_op jit(solution)/shard_map/ppermute | solution.py:184
  181.7 15.5 %collective-permute-start.34 = (bf16[2,2,128,512]{3,2,1,0:T(8,128)(2,1)}, bf16[2,2,128,512]{3,2,1,0:T(8,128)(2,1)S(1)}, u32[]{:S(2)}, u32[]{:S(2)}) collective-permute-start(bf16[2,2,128,512]{3,2,1,0:T(8,128)(2,1)} %collective-permute-done.33), channel_id=1, source_target_pairs={{0,2},{1,3},{2,4},{3,5},{4,6},{5,7},{6,0},{7,1},{8,10},{9,11},{10,... | collective-permute-start | bytes 1572872 | tf_op jit(solution)/shard_map/ppermute | solution.py:187
  181.7 21.7 %collective-permute-start.16 = (bf16[2,2,128,512]{3,2,1,0:T(8,128)(2,1)}, bf16[2,2,128,512]{3,2,1,0:T(8,128)(2,1)S(1)}, u32[]{:S(2)}, u32[]{:S(2)}) collective-permute-start(bf16[2,2,128,512]{3,2,1,0:T(8,128)(2,1)} %collective-permute-done.15), channel_id=1, source_target_pairs={{0,2},{1,3},{2,4},{3,5},{4,6},{5,7},{6,0},{7,1},{8,10},{9,11},{10,... | collective-permute-start | bytes 1572872 | tf_op jit(solution)/shard_map/ppermute | solution.py:187
  185.7 27.6 %collective-permute-start.23 = (bf16[2,2,4,56,768]{4,3,2,1,0:T(8,128)(2,1)S(1)}, bf16[2,2,4,56,768]{4,3,2,1,0:T(8,128)(2,1)S(1)}, u32[]{:S(2)}, u32[]{:S(2)}) collective-permute-start(bf16[2,2,4,56,768]{4,3,2,1,0:T(8,128)(2,1)S(1)} %fusion.26), channel_id=1, source_target_pairs={{0,8},{8,0},{16,24},{24,16},{1,9},{9,1},{17,25},{25,17},{2,10},{10... | collective-permute-start | bytes 4128776 | tf_op jit(solution)/shard_map/ppermute | solution.py:178
  187.8 27.5 %collective-permute-start.29 = (bf16[2,2,4,56,768]{4,3,2,1,0:T(8,128)(2,1)S(1)}, bf16[2,2,4,56,768]{4,3,2,1,0:T(8,128)(2,1)S(1)}, u32[]{:S(2)}, u32[]{:S(2)}) collective-permute-start(bf16[2,2,4,56,768]{4,3,2,1,0:T(8,128)(2,1)S(1)} %fusion.28), channel_id=1, source_target_pairs={{0,8},{8,0},{16,24},{24,16},{1,9},{9,1},{17,25},{25,17},{2,10},{10... | collective-permute-start | bytes 4128776 | tf_op jit(solution)/shard_map/ppermute | solution.py:178
  198.9 8.3 %collective-permute-start.35 = (bf16[2,2,4,56,512]{4,3,2,1,0:T(8,128)(2,1)S(1)}, bf16[2,2,4,56,512]{4,3,2,1,0:T(8,128)(2,1)S(1)}, u32[]{:S(2)}, u32[]{:S(2)}) collective-permute-start(bf16[2,2,4,56,512]{4,3,2,1,0:T(8,128)(2,1)S(1)} %convolution_convert_fusion.5), channel_id=1, source_target_pairs={{0,8},{8,0},{16,24},{24,16},{1,9},{9,1},{17,25},{25,17},{2,10},{10... | collective-permute-start | bytes 2752520 | tf_op jit(solution)/shard_map/ppermute | solution.py:178
  203.5 13.8 %collective-permute-start.5 = (bf16[2,2,4,56,896]{4,3,2,1,0:T(8,128)(2,1)S(1)}, bf16[2,2,4,56,896]{4,3,2,1,0:T(8,128)(2,1)S(1)}, u32[]{:S(2)}, u32[]{:S(2)}) collective-permute-start(bf16[2,2,4,56,896]{4,3,2,1,0:T(8,128)(2,1)S(1)} %fusion.21), channel_id=1, source_target_pairs={{0,8},{8,0},{16,24},{24,16},{1,9},{9,1},{17,25},{25,17},{2,10},{10... | collective-permute-start | bytes 4816904 | tf_op jit(solution)/shard_map/ppermute | solution.py:178
  205.7 7.4 %collective-permute-start.17 = (bf16[2,2,4,56,512]{4,3,2,1,0:T(8,128)(2,1)S(1)}, bf16[2,2,4,56,512]{4,3,2,1,0:T(8,128)(2,1)S(1)}, u32[]{:S(2)}, u32[]{:S(2)}) collective-permute-start(bf16[2,2,4,56,512]{4,3,2,1,0:T(8,128)(2,1)S(1)} %convolution_convert_fusion.7), channel_id=1, source_target_pairs={{0,8},{8,0},{16,24},{24,16},{1,9},{9,1},{17,25},{25,17},{2,10},{10... | collective-permute-start | bytes 2752520 | tf_op jit(solution)/shard_map/ppermute | solution.py:178
  207.2 9.9 %collective-permute-start.11 = (bf16[2,2,4,56,768]{4,3,2,1,0:T(8,128)(2,1)S(1)}, bf16[2,2,4,56,768]{4,3,2,1,0:T(8,128)(2,1)S(1)}, u32[]{:S(2)}, u32[]{:S(2)}) collective-permute-start(bf16[2,2,4,56,768]{4,3,2,1,0:T(8,128)(2,1)S(1)} %fusion.24), channel_id=1, source_target_pairs={{0,8},{8,0},{16,24},{24,16},{1,9},{9,1},{17,25},{25,17},{2,10},{10... | collective-permute-start | bytes 4128776 | tf_op jit(solution)/shard_map/ppermute | solution.py:178
  213.3 16.9 %copy-start.9 = (bf16[2,2,2,4,56,512]{5,4,3,2,1,0:T(8,128)(2,1)}, bf16[2,2,2,4,56,512]{5,4,3,2,1,0:T(8,128)(2,1)S(1)}, u32[]{:S(2)}) copy-start(bf16[2,2,2,4,56,512]{5,4,3,2,1,0:T(8,128)(2,1)S(1)} %pad_maximum_fusion.23) | copy-start | bytes 5505028
  217.3 12.9 %copy-start.3 = (bf16[2,2,2,4,56,768]{5,4,3,2,1,0:T(8,128)(2,1)}, bf16[2,2,2,4,56,768]{5,4,3,2,1,0:T(8,128)(2,1)S(1)}, u32[]{:S(2)}) copy-start(bf16[2,2,2,4,56,768]{5,4,3,2,1,0:T(8,128)(2,1)S(1)} %pad_maximum_fusion.9) | copy-start | bytes 8257540
  242.2 14.2 %copy-start.22 = (f32[1792]{0:T(1024)}, f32[1792]{0:T(1024)S(1)}, u32[]{:S(2)}) copy-start(f32[1792]{0:T(1024)S(1)} %convert_element_type.297) | copy-start | bytes 21508
  242.2 15.7 %copy-start.25 = (bf16[1,2048,768]{2,1,0:T(8,128)(2,1)S(1)}, bf16[1,2048,768]{2,1,0:T(8,128)(2,1)}, u32[]{:S(2)}) copy-start(bf16[1,2048,768]{2,1,0:T(8,128)(2,1)} %param.11) | copy-start | bytes 9437188
  270.1 10.6 %collective-permute-start.48 = (bf16[2,2,4,56,512]{4,3,1,0,2:T(8,128)(2,1)}, bf16[2,2,4,56,512]{4,3,1,0,2:T(8,128)(2,1)}, u32[]{:S(2)}, u32[]{:S(2)}) collective-permute-start(bf16[2,2,4,56,512]{4,3,1,0,2:T(8,128)(2,1)} %copy.105), channel_id=1, source_target_pairs={{0,8},{8,0},{16,24},{24,16},{1,9},{9,1},{17,25},{25,17},{2,10},{10... | collective-permute-start | bytes 2752520 | tf_op jit(solution)/shard_map/ppermute | solution.py:178
  274.3 48.1 %collective-permute-start.36 = (bf16[2,2,4,56,896]{4,3,2,1,0:T(8,128)(2,1)}, bf16[2,2,4,56,896]{4,3,2,1,0:T(8,128)(2,1)S(1)}, u32[]{:S(2)}, u32[]{:S(2)}) collective-permute-start(bf16[2,2,4,56,896]{4,3,2,1,0:T(8,128)(2,1)} %bitcast.283), channel_id=1, source_target_pairs={{0,8},{8,0},{16,24},{24,16},{1,9},{9,1},{17,25},{25,17},{2,10},{10... | collective-permute-start | bytes 4816904 | tf_op jit(solution)/shard_map/ppermute | solution.py:178
  283.4 13.9 %collective-permute-start.49 = (bf16[2,2,128,512]{2,3,0,1:T(8,128)(2,1)S(1)}, bf16[2,2,128,512]{2,3,0,1:T(8,128)(2,1)S(1)}, u32[]{:S(2)}, u32[]{:S(2)}) collective-permute-start(bf16[2,2,128,512]{2,3,0,1:T(8,128)(2,1)S(1)} %convolution_convert_fusion.9), channel_id=1, source_target_pairs={{0,6},{1,7},{2,0},{3,1},{4,2},{5,3},{6,4},{7,5},{8,14},{9,15},{10,... | collective-permute-start | bytes 1572872 | tf_op jit(solution)/shard_map/ppermute | solution.py:192
  287.8 12.9 %copy-start.8 = (bf16[2,2,2,4,56,768]{5,4,3,2,1,0:T(8,128)(2,1)S(1)}, bf16[2,2,2,4,56,768]{5,4,3,2,1,0:T(8,128)(2,1)}, u32[]{:S(2)}) copy-start(bf16[2,2,2,4,56,768]{5,4,3,2,1,0:T(8,128)(2,1)} %pad_maximum_fusion.11) | copy-start | bytes 8257540
  290.3 28.2 %collective-permute-start.42 = (bf16[2,2,4,56,768]{4,3,2,0,1:T(8,128)(2,1)}, bf16[2,2,4,56,768]{4,3,2,0,1:T(8,128)(2,1)}, u32[]{:S(2)}, u32[]{:S(2)}) collective-permute-start(bf16[2,2,4,56,768]{4,3,2,0,1:T(8,128)(2,1)} %copy.101), channel_id=1, source_target_pairs={{0,8},{8,0},{16,24},{24,16},{1,9},{9,1},{17,25},{25,17},{2,10},{10... | collective-permute-start | bytes 4128776 | tf_op jit(solution)/shard_map/ppermute | solution.py:178
  298.4 18.6 %collective-permute-start.50 = (bf16[2,2,128,512]{2,3,0,1:T(8,128)(2,1)}, bf16[2,2,128,512]{2,3,0,1:T(8,128)(2,1)}, u32[]{:S(2)}, u32[]{:S(2)}) collective-permute-start(bf16[2,2,128,512]{2,3,0,1:T(8,128)(2,1)} %fusion.45), channel_id=1, source_target_pairs={{0,6},{1,7},{2,0},{3,1},{4,2},{5,3},{6,4},{7,5},{8,14},{9,15},{10,... | collective-permute-start | bytes 1572872 | tf_op jit(solution)/shard_map/ppermute | solution.py:192
  318.4 12.8 %collective-permute-start.51 = (bf16[2,2,128,512]{2,3,0,1:T(8,128)(2,1)S(1)}, bf16[2,2,128,512]{2,3,0,1:T(8,128)(2,1)S(1)}, u32[]{:S(2)}, u32[]{:S(2)}) collective-permute-start(bf16[2,2,128,512]{2,3,0,1:T(8,128)(2,1)S(1)} %fusion.44), channel_id=1, source_target_pairs={{0,6},{1,7},{2,0},{3,1},{4,2},{5,3},{6,4},{7,5},{8,14},{9,15},{10,... | collective-permute-start | bytes 1572872 | tf_op jit(solution)/shard_map/ppermute | solution.py:192
  320.6 43.6 %collective-permute-start.43 = (bf16[2,4,128,768]{2,3,1,0:T(8,128)(2,1)S(1)}, bf16[2,4,128,768]{2,3,1,0:T(8,128)(2,1)}, u32[]{:S(2)}, u32[]{:S(2)}) collective-permute-start(bf16[2,4,128,768]{2,3,1,0:T(8,128)(2,1)S(1)} %convolution_convert_fusion.4), channel_id=1, source_target_pairs={{0,1},{1,0},{2,3},{3,2},{4,5},{5,4},{6,7},{7,6},{8,9},{9,8},{10,11... | collective-permute-start | bytes 4718600 | tf_op jit(solution)/shard_map/ppermute | solution.py:184
  323.2 44.7 %collective-permute-start.37 = (bf16[2,4,128,896]{2,3,1,0:T(8,128)(2,1)S(1)}, bf16[2,4,128,896]{2,3,1,0:T(8,128)(2,1)}, u32[]{:S(2)}, u32[]{:S(2)}) collective-permute-start(bf16[2,4,128,896]{2,3,1,0:T(8,128)(2,1)S(1)} %convolution_convert_fusion.3), channel_id=1, source_target_pairs={{0,16},{8,24},{16,0},{24,8},{1,17},{9,25},{17,1},{25,9},{2,18},{10... | collective-permute-start | bytes 5505032 | tf_op jit(solution)/shard_map/ppermute | solution.py:181
  331.6 30.0 %collective-permute-start.52 = (bf16[2,128,512]{1,2,0:T(8,128)(2,1)S(1)}, bf16[2,128,512]{1,2,0:T(8,128)(2,1)}, u32[]{:S(2)}, u32[]{:S(2)}) collective-permute-start(bf16[2,128,512]{1,2,0:T(8,128)(2,1)S(1)} %slice_bitcast_fusion.12), channel_id=1, source_target_pairs={{0,1},{1,0},{2,3},{3,2},{4,5},{5,4},{6,7},{7,6},{8,9},{9,8},{10,11... | collective-permute-start | bytes 786440 | tf_op jit(solution)/shard_map/ppermute | solution.py:184
  362.7 21.5 %collective-permute-start.53 = (bf16[128,512]{0,1:T(8,128)(2,1)S(1)}, bf16[128,512]{0,1:T(8,128)(2,1)S(1)}, u32[]{:S(2)}, u32[]{:S(2)}) collective-permute-start(bf16[128,512]{0,1:T(8,128)(2,1)S(1)} %slice_bitcast_fusion.22), channel_id=1, source_target_pairs={{0,16},{8,24},{16,0},{24,8},{1,17},{9,25},{17,1},{25,9},{2,18},{10... | collective-permute-start | bytes 393224 | tf_op jit(solution)/shard_map/ppermute | solution.py:181
  367.4 17.5 %collective-permute-start.44 = (bf16[4,128,768]{1,2,0:T(8,128)(2,1)}, bf16[4,128,768]{1,2,0:T(8,128)(2,1)}, u32[]{:S(2)}, u32[]{:S(2)}) collective-permute-start(bf16[4,128,768]{1,2,0:T(8,128)(2,1)} %slice_bitcast_fusion.6), channel_id=1, source_target_pairs={{0,16},{8,24},{16,0},{24,8},{1,17},{9,25},{17,1},{25,9},{2,18},{10... | collective-permute-start | bytes 2359304 | tf_op jit(solution)/shard_map/ppermute | solution.py:181
  370.4 19.8 %collective-permute-start.38 = (bf16[4,128,896]{1,2,0:T(8,128)(2,1)S(1)}, bf16[4,128,896]{1,2,0:T(8,128)(2,1)S(1)}, u32[]{:S(2)}, u32[]{:S(2)}) collective-permute-start(bf16[4,128,896]{1,2,0:T(8,128)(2,1)S(1)} %slice_bitcast_fusion.4), channel_id=1, source_target_pairs={{0,1},{1,0},{2,3},{3,2},{4,5},{5,4},{6,7},{7,6},{8,9},{9,8},{10,11... | collective-permute-start | bytes 2752520 | tf_op jit(solution)/shard_map/ppermute | solution.py:184
  386.2 7.8 %collective-permute-start.45 = (bf16[128,768]{0,1:T(8,128)(2,1)S(1)}, bf16[128,768]{0,1:T(8,128)(2,1)S(1)}, u32[]{:S(2)}, u32[]{:S(2)}) collective-permute-start(bf16[128,768]{0,1:T(8,128)(2,1)S(1)} %slice_bitcast_fusion.18), channel_id=1, source_target_pairs={{0,6},{1,7},{2,0},{3,1},{4,2},{5,3},{6,4},{7,5},{8,14},{9,15},{10,... | collective-permute-start | bytes 589832 | tf_op jit(solution)/shard_map/ppermute | solution.py:192
  390.5 8.6 %collective-permute-start.39 = (bf16[128,896]{0,1:T(8,128)(2,1)S(1)}, bf16[128,896]{0,1:T(8,128)(2,1)S(1)}, u32[]{:S(2)}, u32[]{:S(2)}) collective-permute-start(bf16[128,896]{0,1:T(8,128)(2,1)S(1)} %slice_bitcast_fusion.14), channel_id=1, source_target_pairs={{0,6},{1,7},{2,0},{3,1},{4,2},{5,3},{6,4},{7,5},{8,14},{9,15},{10,... | collective-permute-start | bytes 688136 | tf_op jit(solution)/shard_map/ppermute | solution.py:192
  394.0 24.6 %copy-start.1 = (bf16[1,768,2048]{2,1,0:T(8,128)(2,1)S(1)}, bf16[1,768,2048]{2,1,0:T(8,128)(2,1)}, u32[]{:S(2)}) copy-start(bf16[1,768,2048]{2,1,0:T(8,128)(2,1)} %param.13) | copy-start | bytes 9437188
  394.1 23.9 %copy-start.21 = (s32[128,8]{0,1:T(8,128)S(1)}, s32[128,8]{0,1:T(8,128)}, u32[]{:S(2)}) copy-start(s32[128,8]{0,1:T(8,128)} %param.9) | copy-start | bytes 12292
  394.1 9.2 %collective-permute-start.46 = (bf16[128,768]{0,1:T(8,128)(2,1)S(1)}, bf16[128,768]{0,1:T(8,128)(2,1)S(1)}, u32[]{:S(2)}, u32[]{:S(2)}) collective-permute-start(bf16[128,768]{0,1:T(8,128)(2,1)S(1)} %fusion.82), channel_id=1, source_target_pairs={{0,6},{1,7},{2,0},{3,1},{4,2},{5,3},{6,4},{7,5},{8,14},{9,15},{10,... | collective-permute-start | bytes 589832 | tf_op jit(solution)/shard_map/ppermute | solution.py:192
  399.1 9.1 %collective-permute-start.40 = (bf16[128,896]{0,1:T(8,128)(2,1)S(1)}, bf16[128,896]{0,1:T(8,128)(2,1)S(1)}, u32[]{:S(2)}, u32[]{:S(2)}) collective-permute-start(bf16[128,896]{0,1:T(8,128)(2,1)S(1)} %fusion.63), channel_id=1, source_target_pairs={{0,6},{1,7},{2,0},{3,1},{4,2},{5,3},{6,4},{7,5},{8,14},{9,15},{10,... | collective-permute-start | bytes 688136 | tf_op jit(solution)/shard_map/ppermute | solution.py:192
  403.4 9.1 %collective-permute-start.47 = (bf16[128,768]{0,1:T(8,128)(2,1)S(1)}, bf16[128,768]{0,1:T(8,128)(2,1)S(1)}, u32[]{:S(2)}, u32[]{:S(2)}) collective-permute-start(bf16[128,768]{0,1:T(8,128)(2,1)S(1)} %fusion.83), channel_id=1, source_target_pairs={{0,6},{1,7},{2,0},{3,1},{4,2},{5,3},{6,4},{7,5},{8,14},{9,15},{10,... | collective-permute-start | bytes 589832 | tf_op jit(solution)/shard_map/ppermute | solution.py:192
  408.3 6.7 %collective-permute-start.41 = (bf16[128,896]{0,1:T(8,128)(2,1)S(1)}, bf16[128,896]{0,1:T(8,128)(2,1)S(1)}, u32[]{:S(2)}, u32[]{:S(2)}) collective-permute-start(bf16[128,896]{0,1:T(8,128)(2,1)S(1)} %fusion.64), channel_id=1, source_target_pairs={{0,6},{1,7},{2,0},{3,1},{4,2},{5,3},{6,4},{7,5},{8,14},{9,15},{10,... | collective-permute-start | bytes 688136 | tf_op jit(solution)/shard_map/ppermute | solution.py:192
  (21 other events, 147.6 us)

commit v2 on v0

--- a/solution.py
+++ b/solution.py
@@ -1,9 +1,12 @@
 import jax
 import jax.numpy as jnp
 from jax import lax
+from jax.experimental import pallas as pl
+from jax.experimental.pallas import tpu as pltpu
 from jax.sharding import PartitionSpec as P
 
 block_rows = 256
+gather_limit = 32 * 2**20
 
 
 def expert_parts(inputs, cotangent_rows, router_weight, gate_matrix, up_matrix, down_matrix):
@@ -48,7 +51,7 @@
     return (gate_term, up_term, down_term)
 
 
-def on_device(tokens, cotangent, routes, gates, w_gate, w_up, w_down):
+def exchange_path(tokens, cotangent, routes, gates, w_gate, w_up, w_down):
     dp_count = lax.axis_size("dp")
     expert_count = lax.axis_size("expert")
     device_count = dp_count * expert_count
@@ -158,6 +161,362 @@
     )
 
 
+def gather_path(tokens, cotangent, routes, gates, w_gate, w_up, w_down):
+    dp_count = lax.axis_size("dp")
+    expert_count = lax.axis_size("expert")
+    device_count = dp_count * expert_count
+    tok_local, model_width = tokens.shape
+    hidden_width = w_gate.shape[2]
+    top_count = routes.shape[1]
+    most_rows = 7 * tok_local * top_count // (4 * device_count)
+    source_count = 16
+    half_rows = source_count * most_rows
+    bf16, f32 = jnp.bfloat16, jnp.float32
+
+    def swap_core(v):
+        return lax.ppermute(v, "dp", [(p, p ^ 1) for p in range(dp_count)])
+
+    def swap_x(v):
+        return lax.ppermute(v, "dp", [(p, p ^ 2) for p in range(dp_count)])
+
+    def swap_y(v):
+        return lax.ppermute(v, "expert", [(q, q ^ 1) for q in range(expert_count)])
+
+    def ring_up(v):
+        return lax.ppermute(
+            v, "expert", [(q, (q + 2) % expert_count) for q in range(expert_count)]
+        )
+
+    def ring_down(v):
+        return lax.ppermute(
+            v, "expert", [(q, (q - 2) % expert_count) for q in range(expert_count)]
+        )
+
+    dp_index = lax.axis_index("dp")
+    expert_index = lax.axis_index("expert")
+    mine = dp_index * expert_count + expert_index
+    other = (dp_index ^ 1) * expert_count + expert_index
+
+    hit = routes[:, :, None] == jnp.arange(device_count, dtype=jnp.int32)[None, None, :]
+    gate_dense = jnp.sum(jnp.where(hit, gates[:, :, None].astype(f32), 0.0), axis=1)
+    named = jnp.sum(hit.astype(f32), axis=1)
+    token_iota = jnp.arange(tok_local)
+    before = (token_iota[None, :] < token_iota[:, None]).astype(bf16)
+    rank = jnp.dot(before, named.astype(bf16), preferred_element_type=f32)
+    rank = jnp.where(named > 0.0, rank, -1.0)
+    info_width = -(-2 * device_count // 128) * 128
+    info = jnp.concatenate(
+        [
+            gate_dense.astype(bf16),
+            rank.astype(bf16),
+            jnp.zeros((tok_local, info_width - 2 * device_count), bf16),
+        ],
+        axis=1,
+    )
+
+    cuts = (0, 3 * model_width // 8, 3 * model_width // 4, model_width)
+
+    def part_of(v, n):
+        return v[:, cuts[n] : cuts[n + 1]]
+
+    def gather_zyx(v, near_axis, far_axis, a_first, hold=None):
+        hops = [v]
+        for _ in range(3):
+            hops.append(ring_up(hops[-1]))
+        blocks, where = [], {}
+        for g in range(2):
+            near = jnp.stack([hops[2 * g], hops[2 * g + 1]])
+            both = jnp.concatenate([near, near_axis(near)])
+            if g == 1 and hold is not None:
+                both = hold(both)
+            blocks += [both, far_axis(both)]
+            for far in range(2):
+                for mid in range(2):
+                    for s in range(2):
+                        i, j = (far, mid) if a_first else (mid, far)
+                        where[g, i, j, s] = (2 * g + far, 2 * mid + s)
+        return blocks, where
+
+    def gather_xyz(v, hold=None):
+        pair = jnp.stack([v, swap_x(v)])
+        quad = jnp.concatenate([pair, swap_y(pair)])
+        hops = [quad]
+        for _ in range(3):
+            hops.append(ring_up(hops[-1]))
+        where = {}
+        for r in range(4):
+            for j in range(2):
+                for i in range(2):
+                    where[r // 2, i, j, r % 2] = (r, 2 * j + i)
+        return hops, where
+
+    gathers = (
+        lambda v, hold=None: gather_zyx(v, swap_y, swap_x, True, hold),
+        lambda v, hold=None: gather_zyx(v, swap_x, swap_y, False, hold),
+        gather_xyz,
+    )
+    order = [(g, i, j, s) for g in range(2) for i in range(2) for j in range(2) for s in range(2)]
+
+    def compact(gathered):
+        blocks, where = gathered
+        width = blocks[0].shape[-1]
+
+        def body(places, *refs):
+            ins, keep, give = refs[: len(blocks)], refs[-2], refs[-1]
+            for n, source in enumerate(order):
+                block, at = where[source]
+                picked = jnp.dot(places[n], ins[block][at], preferred_element_type=f32)
+                keep[n] = picked[:most_rows].astype(bf16)
+                give[n] = picked[most_rows:].astype(bf16)
+
+        shape = jax.ShapeDtypeStruct((source_count, most_rows, width), bf16)
+        keep, give = pl.pallas_call(
+            body,
+            out_shape=(shape, shape),
+            in_specs=[pl.BlockSpec(memory_space=pltpu.VMEM)] * (1 + len(blocks)),
+            out_specs=(pl.BlockSpec(memory_space=pltpu.VMEM),) * 2,
+            compiler_params=pltpu.CompilerParams(vmem_limit_bytes=24 * 2**20),
+            cost_estimate=pl.CostEstimate(
+                flops=2 * source_count * 2 * most_rows * tok_local * width,
+                bytes_accessed=12 * 2**20,
+                transcendentals=0,
+            ),
+        )(place_both, *blocks)
+        return keep.reshape(half_rows, width), swap_core(give).reshape(half_rows, width)
+
+    def row_call(body, ins, whole, outs, flops):
+        block = half_rows // 4
+        in_specs = []
+        for v in ins:
+            if v.ndim == 2:
+                in_specs.append(pl.BlockSpec((block, v.shape[1]), lambda b: (b, 0)))
+            else:
+                in_specs.append(pl.BlockSpec((2, block, v.shape[2]), lambda b: (0, b, 0)))
+        for v, shape, place in whole:
+            in_specs.append(pl.BlockSpec(shape, lambda b, place=place: place))
+        return pl.pallas_call(
+            body,
+            grid=(4,),
+            out_shape=tuple(jax.ShapeDtypeStruct((2, half_rows, w), d) for w, d in outs),
+            in_specs=in_specs,
+            out_specs=tuple(pl.BlockSpec((2, block, w), lambda b: (0, b, 0)) for w, _ in outs),
+            compiler_params=pltpu.CompilerParams(vmem_limit_bytes=48 * 2**20),
+            cost_estimate=pl.CostEstimate(
+                flops=flops, bytes_accessed=24 * 2**20, transcendentals=0
+            ),
+        )(*ins, *[v for v, _, _ in whole])
+
+    nt = (((1,), (1,)), ((), ()))
+    gate_matrix, up_matrix, down_matrix = w_gate[0], w_up[0], w_down[0]
+    lanes = lax.broadcasted_iota(jnp.int32, (1, info_width), 1)
+    lane_mask = (lanes == mine).astype(f32)
+    mask_spec = (lane_mask, (1, info_width), (0, 0))
+    unit = 2 * 2 * half_rows * model_width * hidden_width
+
+    token_parts = [part_of(tokens, n) for n in range(3)]
+    token_parts[0] = jnp.concatenate([info, token_parts[0]], axis=1)
+    got = [gathers[n](token_parts[n]) for n in range(3)]
+    blocks, where = got[0]
+    got_info = jnp.stack([blocks[where[k][0]][where[k][1], :, :info_width] for k in order])
+    slots = jnp.arange(most_rows, dtype=f32)
+
+    def places_of(index):
+        at = lax.broadcasted_iota(jnp.int32, got_info.shape, 2) == device_count + index
+        ranks = jnp.sum(jnp.where(at, got_info, jnp.zeros((), bf16)).astype(f32), axis=-1)
+        return (ranks[:, None, :] == slots[:, None]).astype(bf16)
+
+    place_both = jnp.concatenate([places_of(mine), places_of(other)], axis=1)
+    rows = [half for n in range(3) for half in compact(got[n])]
+
+    def forward(*refs):
+        halves, (gates_at, wg, wu), outs = refs[:6], refs[6:9], refs[9:]
+        gated, slope, silu, weighted = outs
+        for h in range(2):
+            parts = [halves[h][:, info_width:], halves[2 + h][...], halves[4 + h][...]]
+            row_gate = jnp.sum(
+                halves[h][:, :info_width].astype(f32) * gates_at[...], axis=1, keepdims=True
+            )
+            pre_gate, pre_up = 0.0, 0.0
+            for n in range(3):
+                pre_gate += jnp.dot(
+                    parts[n], wg[cuts[n] : cuts[n + 1]], preferred_element_type=f32
+                )
+                pre_up += jnp.dot(parts[n], wu[cuts[n] : cuts[n + 1]], preferred_element_type=f32)
+            sigmoid_gate = 1.0 / (1.0 + jnp.exp(-pre_gate))
+            silu_gate = pre_gate * sigmoid_gate
+            hidden = silu_gate * pre_up
+            gated[h] = hidden
+            slope[h] = row_gate * pre_up * sigmoid_gate * (1.0 + pre_gate * (1.0 - sigmoid_gate))
+            silu[h] = row_gate * silu_gate
+            weighted[h] = (row_gate * hidden).astype(bf16)
+
+    square = (model_width, hidden_width)
+    hidden, slope, silu, weighted = row_call(
+        forward,
+        rows,
+        [mask_spec, (gate_matrix, square, (0, 0)), (up_matrix, square, (0, 0))],
+        [(hidden_width, f32)] * 3 + [(hidden_width, bf16)],
+        2 * unit,
+    )
+
+    held = [hidden]
+
+    def hold(v):
+        v, held[0] = lax.optimization_barrier((v, held[0]))
+        return v
+
+    got_cot = [gathers[n](part_of(cotangent, n), hold if n < 2 else None) for n in range(3)]
+    hidden = held[0]
+    cot_rows = [half for n in (2, 1, 0) for half in compact(got_cot[n])]
+    cot_rows = cot_rows[4:] + cot_rows[2:4] + cot_rows[:2]
+
+    def row_grad(pgg, pug, wg, wu):
+        return lax.dot_general(pgg, wg, nt, preferred_element_type=f32) + lax.dot_general(
+            pug, wu, nt, preferred_element_type=f32
+        )
+
+    def backward(*refs):
+        halves, (gated, slope, silu) = refs[:6], refs[6:9]
+        (gates_at, wd, wg, wu), (pgg, pug, gate_lanes, last_grad) = refs[9:13], refs[13:]
+        for h in range(2):
+            back = 0.0
+            for n in range(3):
+                back += lax.dot_general(
+                    halves[2 * n + h][...],
+                    wd[:, cuts[n] : cuts[n + 1]],
+                    nt,
+                    preferred_element_type=f32,
+                )
+            gate_grad = jnp.sum(gated[h] * back, axis=1, keepdims=True)
+            gate_lanes[h] = (gate_grad * gates_at[...]).astype(bf16)
+            gate_side = (back * slope[h]).astype(bf16)
+            up_side = (back * silu[h]).astype(bf16)
+            pgg[h] = gate_side
+            pug[h] = up_side
+            last_grad[h] = row_grad(gate_side, up_side, wg[...], wu[...]).astype(bf16)
+
+    last = (cuts[3] - cuts[2], hidden_width)
+    third = (cuts[1], hidden_width)
+    last_at = cuts[2] // last[0]
+    pre_gate_grad, pre_up_grad, gate_lanes, grad_last = row_call(
+        backward,
+        cot_rows + [hidden, slope, silu],
+        [
+            mask_spec,
+            (down_matrix, (hidden_width, model_width), (0, 0)),
+            (gate_matrix, last, (last_at, 0)),
+            (up_matrix, last, (last_at, 0)),
+        ],
+        [(hidden_width, bf16)] * 2 + [(info_width, bf16), (last[0], bf16)],
+        3 * unit // 2,
+    )
+
+    def first_grad(pgg, pug, gate_lanes, wg, wu, out):
+        for h in range(2):
+            out[h, :, :info_width] = gate_lanes[h]
+            out[h, :, info_width:] = row_grad(pgg[h], pug[h], wg[...], wu[...]).astype(bf16)
+
+    def second_grad(pgg, pug, wg, wu, out):
+        for h in range(2):
+            out[h] = row_grad(pgg[h], pug[h], wg[...], wu[...]).astype(bf16)
+
+    (grad_first,) = row_call(
+        first_grad,
+        [pre_gate_grad, pre_up_grad, gate_lanes],
+        [(gate_matrix, third, (0, 0)), (up_matrix, third, (0, 0))],
+        [(info_width + third[0], bf16)],
+        3 * unit // 4,
+    )
+    (grad_second,) = row_call(
+        second_grad,
+        [pre_gate_grad, pre_up_grad],
+        [(gate_matrix, third, (1, 0)), (up_matrix, third, (1, 0))],
+        [(third[0], bf16)],
+        3 * unit // 4,
+    )
+
+    place_grid = place_both.reshape(2, 2, 2, 2, 2 * most_rows, tok_local)
+
+    def pair_rows(v):
+        width = v.shape[-1]
+        own = v[0].reshape(source_count, most_rows, width)
+        given = swap_core(v[1]).reshape(source_count, most_rows, width)
+        return jnp.concatenate([own, given], axis=1).reshape(2, 2, 2, 2, 2 * most_rows, width)
+
+    def spread(places, v):
+        return jnp.einsum("...ct,...cd->...td", places, v, preferred_element_type=f32)
+
+    def add(own, arrived):
+        return (own.astype(f32) + arrived.astype(f32)).astype(bf16)
+
+    def sum_two(v, take, far_axis, near_axis):
+        blocks = [None] * 4
+        for g in (1, 0):
+            moved = far_axis(spread(take(place_grid[g], 1), take(v[g], 1)).astype(bf16))
+            near = add(spread(take(place_grid[g], 0), take(v[g], 0)), moved)
+            pair = add(near[0], near_axis(near[1]))
+            blocks[2 * g], blocks[2 * g + 1] = pair[0], pair[1]
+        moving = blocks[3]
+        for r in (2, 1, 0):
+            moving = add(blocks[r], ring_down(moving))
+        return moving
+
+    def sum_xyz(v):
+        return sum_two(v, lambda u, i: u[i], swap_x, swap_y)
+
+    def sum_yxz(v):
+        return sum_two(v, lambda u, j: u[:, j], swap_y, swap_x)
+
+    def sum_zyx(v):
+        def block(r):
+            g, s = r // 2, r % 2
+            return spread(place_grid[g, :, :, s], v[g, :, :, s])
+
+        moving = block(3).astype(bf16)
+        for r in (2, 1, 0):
+            moving = add(block(r), ring_down(moving))
+        pair = add(moving[:, 0], swap_y(moving[:, 1]))
+        return add(pair[0], swap_x(pair[1]))
+
+    sum_last = sum_zyx(pair_rows(grad_last))
+    sum_first = sum_xyz(pair_rows(grad_first))
+    sum_second = sum_yxz(pair_rows(grad_second))
+    gate_back = sum_first[:, :device_count].astype(f32)
+    input_grad = jnp.concatenate([sum_first[:, info_width:], sum_second, sum_last], axis=1)
+    gate_grad_out = jnp.sum(jnp.where(hit, gate_back[:, None, :], 0.0), axis=2).astype(bf16)
+
+    def whole(halves, skip):
+        parts = [jnp.concatenate(halves[2 * n : 2 * n + 2]) for n in range(3)]
+        return jnp.concatenate([parts[0][:, skip:], parts[1], parts[2]], axis=1)
+
+    tn = (((0,), (0,)), ((), ()))
+    x_rows = whole(rows, info_width)
+    c_rows = whole(cot_rows, 0)
+
+    def flat(v):
+        return v.reshape(2 * half_rows, v.shape[-1])
+
+    w_gate_grad = lax.dot_general(x_rows, flat(pre_gate_grad), tn, preferred_element_type=f32)
+    w_up_grad = lax.dot_general(x_rows, flat(pre_up_grad), tn, preferred_element_type=f32)
+    w_down_grad = lax.dot_general(flat(weighted), c_rows, tn, preferred_element_type=f32)
+    return (
+        input_grad,
+        gate_grad_out,
+        w_gate_grad.astype(bf16)[None],
+        w_up_grad.astype(bf16)[None],
+        w_down_grad.astype(bf16)[None],
+    )
+
+
+def on_device(tokens, cotangent, routes, gates, w_gate, w_up, w_down):
+    dp_count = lax.axis_size("dp")
+    expert_count = lax.axis_size("expert")
+    gathered_bytes = dp_count * expert_count * tokens.size * 2
+    if dp_count == 4 and expert_count == 8 and gathered_bytes <= gather_limit:
+        return gather_path(tokens, cotangent, routes, gates, w_gate, w_up, w_down)
+    return exchange_path(tokens, cotangent, routes, gates, w_gate, w_up, w_down)
+
+
 def solution(mesh):
     in_specs = (
         P(("dp", "expert"), None),

time: 1060 us -> 457 us (0.43)
  blocking collectives: 362 us -> 0 us
  local copies, waits for them, and re-layouts: 187 us -> 18.9 us
  waiting for transfers between devices: 304 us -> 197 us
  Pallas kernels: 0 us -> 60.6 us
  starting transfers between devices: 14.7 us -> 56.7 us
  matrix products: 135 us -> 101 us
  other arithmetic: 39.9 us -> 12.9 us
    all_to_all x2 -> x0, blocking collectives: 362 us -> none  [the longest x1 193 us: on_device(): lax.all_to_all(gate_out, ('dp', 'expert'), split_axis=0, concat_axis=0, t...]
    all_to_all x3 -> x0, waiting for transfers between devices: 304 us -> none  [the longest x1 157 us: on_device(): lax.all_to_all(send_tokens, ('dp', 'expert'), split_axis=0, concat_axis=0...]
    ppermute x0 -> x66, waiting for transfers between devices: none -> 197 us  [the longest x18 65.2 us: ring_up(): lax.ppermute(v, 'expert', [(q, (q + 2) % expert_count) for q in range(exp...]
    gather x17 -> x0, local copies, waits for them, and re-layouts: 106 us -> none  [the longest x4 25.6 us: block_step(): got_tokens[safe_pick]]
    scatter x10 -> x0, local copies, waits for them, and re-layouts: 61.3 us -> none  [the longest x4 41.1 us: block_step(): grad_slots = grad_slots.at[target].set(row_grad, mode='drop')]
    pallas_call x0 -> x10, Pallas kernels: none -> 60.6 us  [the longest x4 55.6 us: row_call(): pl.pallas_call(body, grid=(4,), out_shape=tuple((jax.ShapeDtypeStruct((2,...]
    ppermute x0 -> x66, starting transfers between devices: none -> 56.7 us  [the longest x15 19.4 us: swap_y(): return lax.ppermute(v, 'expert', [(q, q ^ 1) for q in range(expert_count)])]
    dot_general x36 -> x16, matrix products: 135 us -> 101 us  [the longest x1 50.5 us: gather_path(): lax.dot_general(flat(weighted), c_rows, tn, preferred_element_type=f32)]
  transfers between devices with their start and end apart: 3 -> 66, of which waited for: 2 -> 33; matrix products, arithmetic and copies ran while one was open for 5% -> 27% of each run, Pallas kernels for 0% -> 9%
where the time goes in v2:
time: 457 us; the launch traced here: 449 us
  waiting for transfers between devices  197 us (43%)
  matrix products  101 us (22%)
  Pallas kernels  60.6 us (13%)
  starting transfers between devices  56.7 us (12%)
  local copies, waits for them, and re-layouts  18.9 us (4%)
  other arithmetic  12.9 us (3%)
    ppermute x18, waiting for transfers between devices, ring_up(): lax.ppermute(v, 'expert', [(q, (q + 2) % expert_count) for q in range(exp...  65.2 us
    ppermute x15, waiting for transfers between devices, swap_x(): return lax.ppermute(v, 'dp', [(p, p ^ 2) for p in range(dp_count)])  57.8 us
    pallas_call x4, Pallas kernels, row_call(): pl.pallas_call(body, grid=(4,), out_shape=tuple((jax.ShapeDtypeStruct((2,...  55.6 us
    dot_general x1, matrix products, gather_path(): lax.dot_general(flat(weighted), c_rows, tn, preferred_element_type=f32)  50.5 us
    ppermute x15, waiting for transfers between devices, swap_y(): return lax.ppermute(v, 'expert', [(q, q ^ 1) for q in range(expert_count)])  39.9 us
    ppermute x9, waiting for transfers between devices, ring_down(): lax.ppermute(v, 'expert', [(q, (q - 2) % expert_count) for q in range(exp...  33.4 us
    dot_general x1, matrix products, gather_path(): lax.dot_general(x_rows, flat(pre_gate_grad), tn, preferred_element_type=f32)  22.6 us
    dot_general x1, matrix products, gather_path(): lax.dot_general(x_rows, flat(pre_up_grad), tn, preferred_element_type=f32)  22.6 us
  transfers between devices with their start and end apart: 66, of which 33 were waited for; matrix products, arithmetic and copies ran while one was open for 27% of the time, Pallas kernels for 9%

profile of v2, /device:TPU:0, one launch (start us, length us, event | category | flops | bytes accessed | tf_op | source)
XLA Modules:
  0.0 448.6 jit_solution(16435259386942796029)
XLA Ops:
  0.6 1.7 slice_bitcast_fusion.46
  4.3 3.1 collective-permute-start
  7.4 1.6 collective-permute-start.14
  9.9 1.6 collective-permute-start.22
  11.5 1.6 slice_bitcast_fusion.43
  13.1 1.8 collective-permute-done.22
  15.0 1.6 collective-permute-start.23
  20.6 1.6 collective-permute-start.15
  22.1 2.2 collective-permute-done.23
  25.4 1.6 collective-permute-start.24
  27.0 1.9 collective-permute-done.17
  28.9 4.9 %collective-permute-done.3 = bf16[128,896]{1,0:T(8,128)(2,1)S(1)} collective-permute-done((bf16[128,896]{1,0:T(8,128)(2,1)S(1)}, bf16[128,896]{1,0:T(8,128)(2,1)S(1)}, u32[]{:S(2)}, u32[]{:S(2)}) %collective-permute-start.3) | collective-permute-done | bytes 229408 | tf_op jit(solution)/shard_map/ppermute | solution.py:186
  33.9 1.6 collective-permute-start.2
  35.5 16.9 %collective-permute-done.4 = bf16[128,896]{1,0:T(8,128)(2,1)S(1)} collective-permute-done((bf16[128,896]{1,0:T(8,128)(2,1)S(1)}, bf16[128,896]{1,0:T(8,128)(2,1)S(1)}, u32[]{:S(2)}, u32[]{:S(2)}) %collective-permute-start.4) | collective-permute-done | bytes 229408 | tf_op jit(solution)/shard_map/ppermute | solution.py:186
  53.7 1.6 collective-permute-start.5
  56.1 8.4 %collective-permute-done.5 = bf16[2,128,896]{2,1,0:T(8,128)(2,1)S(1)} collective-permute-done((bf16[2,128,896]{2,1,0:T(8,128)(2,1)S(1)}, bf16[2,128,896]{2,1,0:T(8,128)(2,1)S(1)}, u32[]{:S(2)}, u32[]{:S(2)}) %collective-permute-start.5) | collective-permute-done | bytes 458784 | tf_op jit(solution)/shard_map/ppermute | solution.py:183
  66.8 2.1 collective-permute-done.25.refs_2_
  69.9 15.7 %collective-permute-done.6.refs_3_ = bf16[4,128,896]{2,1,0:T(8,128)(2,1)S(1)} collective-permute-done((bf16[4,128,896]{2,1,0:T(8,128)(2,1)S(1)}, bf16[4,128,896]{2,1,0:T(8,128)(2,1)S(1)}, u32[]{:S(2)}, u32[]{:S(2)}) %collective-permute-start.6) | collective-permute-done | bytes 917536 | tf_op jit(solution)/shard_map/ppermute | solution.py:180
  87.8 11.2 %collective-permute-done.20.refs_3_ = bf16[4,128,768]{2,1,0:T(8,128)(2,1)S(1)} collective-permute-done((bf16[4,128,768]{2,1,0:T(8,128)(2,1)S(1)}, bf16[4,128,768]{2,1,0:T(8,128)(2,1)S(1)}, u32[]{:S(2)}, u32[]{:S(2)}) %collective-permute-start.20) | collective-permute-done | bytes 786464 | tf_op jit(solution)/shard_map/ppermute | solution.py:183
  102.1 4.0 collective-permute-done.39
  106.8 7.3 %collective-permute-done.10 = bf16[128,768]{1,0:T(8,128)(2,1)S(1)} collective-permute-done((bf16[128,768]{1,0:T(8,128)(2,1)S(1)}, bf16[128,768]{1,0:T(8,128)(2,1)S(1)}, u32[]{:S(2)}, u32[]{:S(2)}) %collective-permute-start.10) | collective-permute-done | bytes 196640 | tf_op jit(solution)/shard_map/ppermute | solution.py:186
  114.0 3.8 collective-permute-done.33
  117.9 3.6 collective-permute-done.11
  122.6 4.3 collective-permute-done.34
  126.9 2.5 collective-permute-start.12
  129.8 8.6 %collective-permute-done.12 = bf16[2,128,768]{2,1,0:T(8,128)(2,1)S(1)} collective-permute-done((bf16[2,128,768]{2,1,0:T(8,128)(2,1)S(1)}, bf16[2,128,768]{2,1,0:T(8,128)(2,1)S(1)}, u32[]{:S(2)}, u32[]{:S(2)}) %collective-permute-start.12) | collective-permute-done | bytes 393248 | tf_op jit(solution)/shard_map/ppermute | solution.py:183
  138.7 1.8 collective-permute-start.32
  140.5 1.8 collective-permute-start.35
  143.5 18.4 %shard_map.113 = (f32[2,896,768]{2,1,0:T(8,128)}, f32[2,896,768]{2,1,0:T(8,128)}, f32[2,896,768]{2,1,0:T(8,128)}, bf16[2,896,768]{2,1,0:T(8,128)(2,1)}) custom-call(bf16[896,896]{1,0:T(8,128)(2,1)S(1)} %bitcast.243, bf16[896,896]{1,0:T(8,128)(2,1)} %bitcast.321, bf16[896,768]{1,0:T(8,128)(2,1)S(1)} %bitcast.246, bf16[896,768]{1,0:T(8,128)(2,1)S(1)} %bitcast.249, ...), custom_call_target="tpu_custom_call" | custom-call | flops 11274289152 | bytes 25165824 | tf_op jit(solution)/shard_map/pallas_call | solution.py:297
  162.4 4.8 %collective-permute-done.35 = bf16[2,128,768]{2,1,0:T(8,128)(2,1)S(1)} collective-permute-done((bf16[2,128,768]{2,1,0:T(8,128)(2,1)S(1)}, bf16[2,128,768]{2,1,0:T(8,128)(2,1)S(1)}, u32[]{:S(2)}, u32[]{:S(2)}) %collective-permute-start.35) | collective-permute-done | bytes 393248 | tf_op jit(solution)/shard_map/ppermute | solution.py:180
  167.3 1.8 collective-permute-start.36
  169.1 12.2 %collective-permute-done.41.refs_2_ = bf16[4,128,512]{2,1,0:T(8,128)(2,1)S(1)} collective-permute-done((bf16[4,128,512]{2,1,0:T(8,128)(2,1)S(1)}, bf16[4,128,512]{2,1,0:T(8,128)(2,1)S(1)}, u32[]{:S(2)}, u32[]{:S(2)}) %collective-permute-start.41) | collective-permute-done | bytes 524320 | tf_op jit(solution)/shard_map/ppermute | solution.py:186
  185.6 6.9 %collective-permute-done.42.refs_3_ = bf16[4,128,512]{2,1,0:T(8,128)(2,1)S(1)} collective-permute-done((bf16[4,128,512]{2,1,0:T(8,128)(2,1)S(1)}, bf16[4,128,512]{2,1,0:T(8,128)(2,1)S(1)}, u32[]{:S(2)}, u32[]{:S(2)}) %collective-permute-start.42) | collective-permute-done | bytes 524320 | tf_op jit(solution)/shard_map/ppermute | solution.py:186
  196.8 19.7 %shard_map.117 = (bf16[2,896,768]{2,1,0:T(8,128)(2,1)}, bf16[2,896,768]{2,1,0:T(8,128)(2,1)}, bf16[2,896,128]{2,1,0:T(8,128)(2,1)S(1)}, bf16[2,896,512]{2,1,0:T(8,128)(2,1)}) custom-call(bf16[896,768]{1,0:T(8,128)(2,1)S(1)} %bitcast.231, bf16[896,768]{1,0:T(8,128)(2,1)S(1)} %bitcast.233, bf16[896,768]{1,0:T(8,128)(2,1)} %bitcast.235, ...), custom_call_target="tpu_custom_call" | custom-call | flops 8455716864 | bytes 25165824 | tf_op jit(solution)/shard_map/pallas_call | solution.py:297
  216.6 3.0 fusion.84
  219.9 8.3 %shard_map.119 = bf16[2,896,768]{2,1,0:T(8,128)(2,1)S(1)} custom-call(bf16[2,896,768]{2,1,0:T(8,128)(2,1)S(1)} %copy-done.3, bf16[2,896,768]{2,1,0:T(8,128)(2,1)} %get-tuple-element.49.pug, bf16[2048,768]{1,0:T(8,128)(2,1)} %bitcast.272, bf16[2048,768]{1,0:T(8,128)(2,1)} %bitcast.276), custom_call_target="tpu_custom_call" | custom-call | flops 4227858432 | bytes 25165824 | tf_op jit(solution)/shard_map/pallas_call | solution.py:297
  228.3 1.8 fusion.83
  231.1 9.1 %shard_map.118 = bf16[2,896,896]{2,1,0:T(8,128)(2,1)} custom-call(bf16[2,896,768]{2,1,0:T(8,128)(2,1)S(1)} %copy-done.3, bf16[2,896,768]{2,1,0:T(8,128)(2,1)S(1)} %copy-done.2, bf16[2,896,128]{2,1,0:T(8,128)(2,1)S(1)} %get-tuple-element.50.gate_lanes, bf16[2048,768]{1,0:T(8,128)(2,1)} %bitcast.273, bf16[2048,768]{1,0:T(8,128)(2,1)} %bitcast.277), custom_call_target="tpu_custom_call" | custom-call | flops 4227858432 | bytes 25165824 | tf_op jit(solution)/shard_map/pallas_call | solution.py:297
  240.2 3.8 slice_bitcast_fusion
  244.2 22.6 %fusion.17 = bf16[1,2048,768]{2,1,0:T(8,128)(2,1)} fusion(bf16[1792,768]{1,0:T(8,128)(2,1)S(1)} %bitcast.242, bf16[896,896]{1,0:T(8,128)(2,1)} %bitcast.322, bf16[896,896]{1,0:T(8,128)(2,1)S(1)} %bitcast.244, bf16[896,512]{1,0:T(8,128)(2,1)} %bitcast.256, bf16[896,512]{1,0:T(8,128)(2,1)} %bitcast.253, bf16[896,768]{1,0:T(8,128)(2,1)} %bitcast.250, ...), kind=kOutput, calls=%fused_computation.24 | convolution fusion | flops 5682757632 | bytes 13697024 | tf_op jit(solution)/shard_map/dot_general | solution.py:499
  266.8 22.6 %fusion.18 = bf16[1,2048,768]{2,1,0:T(8,128)(2,1)} fusion(bf16[1792,768]{1,0:T(8,128)(2,1)S(1)} %bitcast.241, bf16[896,896]{1,0:T(8,128)(2,1)} %bitcast.323, bf16[896,896]{1,0:T(8,128)(2,1)S(1)} %bitcast.245, bf16[896,512]{1,0:T(8,128)(2,1)} %bitcast.257, bf16[896,512]{1,0:T(8,128)(2,1)} %bitcast.254, bf16[896,768]{1,0:T(8,128)(2,1)} %bitcast.251, ...), kind=kOutput, calls=%fused_computation.25 | convolution fusion | flops 5682757632 | bytes 13697024 | tf_op jit(solution)/shard_map/dot_general | solution.py:500
  289.5 50.5 %fusion.19 = bf16[1,768,2048]{2,1,0:T(8,128)(2,1)} fusion(bf16[1792,768]{1,0:T(8,128)(2,1)} %bitcast.324, bf16[896,512]{1,0:T(8,128)(2,1)S(1)} %bitcast.240, bf16[896,512]{1,0:T(8,128)(2,1)S(1)} %bitcast.238, bf16[896,768]{1,0:T(8,128)(2,1)S(1)} %bitcast.279, bf16[896,768]{1,0:T(8,128)(2,1)S(1)} %bitcast.236, bf16[896,768]{1,0:T(8,128)(2,1)S(1)} %bitcast.234, ...), kind=kOutput, calls=%fused_computation.26 | convolution fusion | flops 5682757632 | bytes 13238272 | tf_op jit(solution)/shard_map/dot_general | solution.py:501
  340.0 1.6 fusion.38
  342.0 1.5 fusion.22
  344.6 2.1 collective-permute-start.53
  346.6 9.5 %collective-permute-done.61 = bf16[2,2,128,512]{2,3,0,1:T(8,128)(2,1)S(1)} collective-permute-done((bf16[2,2,128,512]{2,3,0,1:T(8,128)(2,1)S(1)}, bf16[2,2,128,512]{2,3,0,1:T(8,128)(2,1)S(1)}, u32[]{:S(2)}, u32[]{:S(2)}) %collective-permute-start.61) | collective-permute-done | bytes 524320 | tf_op jit(solution)/shard_map/ppermute | solution.py:191
  356.4 2.1 collective-permute-start.62
  358.6 1.7 fusion.29
  361.6 1.9 collective-permute-start.45
  363.4 6.4 %collective-permute-done.62 = bf16[2,2,128,512]{2,3,0,1:T(8,128)(2,1)S(1)} collective-permute-done((bf16[2,2,128,512]{2,3,0,1:T(8,128)(2,1)S(1)}, bf16[2,2,128,512]{2,3,0,1:T(8,128)(2,1)S(1)}, u32[]{:S(2)}, u32[]{:S(2)}) %collective-permute-start.62) | collective-permute-done | bytes 524320 | tf_op jit(solution)/shard_map/ppermute | solution.py:191
  370.2 4.2 collective-permute-start.63
  375.2 5.5 %collective-permute-done.53 = bf16[2,2,128,768]{2,3,1,0:T(8,128)(2,1)S(1)} collective-permute-done((bf16[2,2,128,768]{2,3,1,0:T(8,128)(2,1)S(1)}, bf16[2,2,128,768]{2,3,1,0:T(8,128)(2,1)S(1)}, u32[]{:S(2)}, u32[]{:S(2)}) %collective-permute-start.53) | collective-permute-done | bytes 786464 | tf_op jit(solution)/shard_map/ppermute | solution.py:183
  381.5 3.2 collective-permute-done.63
  385.8 2.1 collective-permute-start.48
  387.8 16.0 %collective-permute-done.45 = bf16[2,2,128,896]{2,3,1,0:T(8,128)(2,1)S(1)} collective-permute-done((bf16[2,2,128,896]{2,3,1,0:T(8,128)(2,1)S(1)}, bf16[2,2,128,896]{2,3,1,0:T(8,128)(2,1)S(1)}, u32[]{:S(2)}, u32[]{:S(2)}) %collective-permute-start.45) | collective-permute-done | bytes 917536 | tf_op jit(solution)/shard_map/ppermute | solution.py:180
  404.4 7.8 %collective-permute-done.56 = bf16[2,128,768]{1,2,0:T(8,128)(2,1)S(1)} collective-permute-done((bf16[2,128,768]{1,2,0:T(8,128)(2,1)S(1)}, bf16[2,128,768]{1,2,0:T(8,128)(2,1)S(1)}, u32[]{:S(2)}, u32[]{:S(2)}) %collective-permute-start.56) | collective-permute-done | bytes 393248 | tf_op jit(solution)/shard_map/ppermute | solution.py:180
  412.4 6.7 %collective-permute-done.54 = bf16[2,128,768]{1,2,0:T(8,128)(2,1)S(1)} collective-permute-done((bf16[2,128,768]{1,2,0:T(8,128)(2,1)S(1)}, bf16[2,128,768]{1,2,0:T(8,128)(2,1)S(1)}, u32[]{:S(2)}, u32[]{:S(2)}) %collective-permute-start.54) | collective-permute-done | bytes 393248 | tf_op jit(solution)/shard_map/ppermute | solution.py:180
  420.1 4.3 collective-permute-done.65
  426.3 1.8 collective-permute-start.59
  428.1 5.1 %collective-permute-done.49 = bf16[128,896]{0,1:T(8,128)(2,1)S(1)} collective-permute-done((bf16[128,896]{0,1:T(8,128)(2,1)S(1)}, bf16[128,896]{0,1:T(8,128)(2,1)S(1)}, u32[]{:S(2)}, u32[]{:S(2)}) %collective-permute-start.49) | collective-permute-done | bytes 229408 | tf_op jit(solution)/shard_map/ppermute | solution.py:191
  433.3 1.6 collective-permute-start.50
  435.0 4.5 %collective-permute-done.50 = bf16[128,896]{0,1:T(8,128)(2,1)S(1)} collective-permute-done((bf16[128,896]{0,1:T(8,128)(2,1)S(1)}, bf16[128,896]{0,1:T(8,128)(2,1)S(1)}, u32[]{:S(2)}, u32[]{:S(2)}) %collective-permute-start.50) | collective-permute-done | bytes 229408 | tf_op jit(solution)/shard_map/ppermute | solution.py:191
  439.6 3.2 collective-permute-start.51
  442.9 3.5 collective-permute-done.51
  (229 shorter events, 44.5 us)
Async XLA Ops:
  4.3 12.2 %collective-permute-start = (bf16[128,896]{1,0:T(8,128)(2,1)S(1)}, bf16[128,896]{1,0:T(8,128)(2,1)S(1)}, u32[]{:S(2)}, u32[]{:S(2)}) collective-permute-start(bf16[128,896]{1,0:T(8,128)(2,1)S(1)} %pad_maximum_fusion.25), channel_id=1, source_target_pairs={{0,2},{1,3},{2,4},{3,5},{4,6},{5,7},{6,0},{7,1},{8,10},{9,11},{10,... | collective-permute-start | bytes 688136 | tf_op jit(solution)/shard_map/ppermute | solution.py:186
  7.4 11.8 %collective-permute-start.14 = (bf16[128,768]{1,0:T(8,128)(2,1)}, bf16[128,768]{1,0:T(8,128)(2,1)S(1)}, u32[]{:S(2)}, u32[]{:S(2)}) collective-permute-start(bf16[128,768]{1,0:T(8,128)(2,1)} %get-tuple-element.88), channel_id=1, source_target_pairs={{0,2},{1,3},{2,4},{3,5},{4,6},{5,7},{6,0},{7,1},{8,10},{9,11},{10,... | collective-permute-start | bytes 589832 | tf_op jit(solution)/shard_map/ppermute | solution.py:186
  15.0 9.4 %collective-permute-start.23 = (bf16[2,128,512]{2,1,0:T(8,128)(2,1)S(1)}, bf16[2,128,512]{2,1,0:T(8,128)(2,1)}, u32[]{:S(2)}, u32[]{:S(2)}) collective-permute-start(bf16[2,128,512]{2,1,0:T(8,128)(2,1)S(1)} %pad_maximum_fusion.23), channel_id=1, source_target_pairs={{0,1},{1,0},{2,3},{3,2},{4,5},{5,4},{6,7},{7,6},{8,9},{9,8},{10,11... | collective-permute-start | bytes 786440 | tf_op jit(solution)/shard_map/ppermute | solution.py:183
  16.6 17.2 %collective-permute-start.1 = (bf16[2,128,896]{2,1,0:T(8,128)(2,1)S(1)}, bf16[2,128,896]{2,1,0:T(8,128)(2,1)S(1)}, u32[]{:S(2)}, u32[]{:S(2)}) collective-permute-start(bf16[2,128,896]{2,1,0:T(8,128)(2,1)S(1)} %pad_maximum_fusion.15), channel_id=1, source_target_pairs={{0,1},{1,0},{2,3},{3,2},{4,5},{5,4},{6,7},{7,6},{8,9},{9,8},{10,11... | collective-permute-start | bytes 1376264 | tf_op jit(solution)/shard_map/ppermute | solution.py:183
  19.2 9.6 %collective-permute-start.17 = (bf16[128,768]{1,0:T(8,128)(2,1)S(1)}, bf16[128,768]{1,0:T(8,128)(2,1)S(1)}, u32[]{:S(2)}, u32[]{:S(2)}) collective-permute-start(bf16[128,768]{1,0:T(8,128)(2,1)S(1)} %collective-permute-done.14), channel_id=1, source_target_pairs={{0,2},{1,3},{2,4},{3,5},{4,6},{5,7},{6,0},{7,1},{8,10},{9,11},{10,... | collective-permute-start | bytes 589832 | tf_op jit(solution)/shard_map/ppermute | solution.py:186
  19.2 14.5 %collective-permute-start.3 = (bf16[128,896]{1,0:T(8,128)(2,1)S(1)}, bf16[128,896]{1,0:T(8,128)(2,1)S(1)}, u32[]{:S(2)}, u32[]{:S(2)}) collective-permute-start(bf16[128,896]{1,0:T(8,128)(2,1)S(1)} %collective-permute-done), channel_id=1, source_target_pairs={{0,2},{1,3},{2,4},{3,5},{4,6},{5,7},{6,0},{7,1},{8,10},{9,11},{10,... | collective-permute-start | bytes 688136 | tf_op jit(solution)/shard_map/ppermute | solution.py:186
  20.6 34.8 %collective-permute-start.15 = (bf16[2,128,768]{2,1,0:T(8,128)(2,1)S(1)}, bf16[2,128,768]{2,1,0:T(8,128)(2,1)S(1)}, u32[]{:S(2)}, u32[]{:S(2)}) collective-permute-start(bf16[2,128,768]{2,1,0:T(8,128)(2,1)S(1)} %pad_maximum_fusion.19), channel_id=1, source_target_pairs={{0,16},{8,24},{16,0},{24,8},{1,17},{9,25},{17,1},{25,9},{2,18},{10... | collective-permute-start | bytes 1179656 | tf_op jit(solution)/shard_map/ppermute | solution.py:180
  25.4 30.6 %collective-permute-start.24 = (bf16[4,128,512]{2,1,0:T(8,128)(2,1)S(1)}, bf16[4,128,512]{2,1,0:T(8,128)(2,1)S(1)}, u32[]{:S(2)}, u32[]{:S(2)}) collective-permute-start(bf16[4,128,512]{2,1,0:T(8,128)(2,1)S(1)} %pad_maximum_fusion.11.refs_0_), channel_id=1, source_target_pairs={{0,2},{1,3},{2,4},{3,5},{4,6},{5,7},{6,0},{7,1},{8,10},{9,11},{10,... | collective-permute-start | bytes 1572872 | tf_op jit(solution)/shard_map/ppermute | solution.py:186
  28.9 24.8 %collective-permute-start.18 = (bf16[128,768]{1,0:T(8,128)(2,1)S(1)}, bf16[128,768]{1,0:T(8,128)(2,1)S(1)}, u32[]{:S(2)}, u32[]{:S(2)}) collective-permute-start(bf16[128,768]{1,0:T(8,128)(2,1)S(1)} %collective-permute-done.17), channel_id=1, source_target_pairs={{0,2},{1,3},{2,4},{3,5},{4,6},{5,7},{6,0},{7,1},{8,10},{9,11},{10,... | collective-permute-start | bytes 589832 | tf_op jit(solution)/shard_map/ppermute | solution.py:186
  33.8 18.6 %collective-permute-start.4 = (bf16[128,896]{1,0:T(8,128)(2,1)S(1)}, bf16[128,896]{1,0:T(8,128)(2,1)S(1)}, u32[]{:S(2)}, u32[]{:S(2)}) collective-permute-start(bf16[128,896]{1,0:T(8,128)(2,1)S(1)} %collective-permute-done.3), channel_id=1, source_target_pairs={{0,2},{1,3},{2,4},{3,5},{4,6},{5,7},{6,0},{7,1},{8,10},{9,11},{10,... | collective-permute-start | bytes 688136 | tf_op jit(solution)/shard_map/ppermute | solution.py:186
  33.9 35.9 %collective-permute-start.2 = (bf16[4,128,896]{2,1,0:T(8,128)(2,1)S(1)}, bf16[4,128,896]{2,1,0:T(8,128)(2,1)S(1)}, u32[]{:S(2)}, u32[]{:S(2)}) collective-permute-start(bf16[4,128,896]{2,1,0:T(8,128)(2,1)S(1)} %pad_maximum_fusion.2.refs_0_), channel_id=1, source_target_pairs={{0,16},{8,24},{16,0},{24,8},{1,17},{9,25},{17,1},{25,9},{2,18},{10... | collective-permute-start | bytes 2752520 | tf_op jit(solution)/shard_map/ppermute | solution.py:180
  52.4 35.2 %collective-permute-start.38 = (bf16[128,512]{1,0:T(8,128)(2,1)S(1)}, bf16[128,512]{1,0:T(8,128)(2,1)S(1)}, u32[]{:S(2)}, u32[]{:S(2)}) collective-permute-start(bf16[128,512]{1,0:T(8,128)(2,1)S(1)} %copy-done.23), channel_id=1, source_target_pairs={{0,16},{8,24},{16,0},{24,8},{1,17},{9,25},{17,1},{25,9},{2,18},{10... | collective-permute-start | bytes 393224 | tf_op jit(solution)/shard_map/ppermute | solution.py:180
  53.7 10.8 %collective-permute-start.5 = (bf16[2,128,896]{2,1,0:T(8,128)(2,1)S(1)}, bf16[2,128,896]{2,1,0:T(8,128)(2,1)S(1)}, u32[]{:S(2)}, u32[]{:S(2)}) collective-permute-start(bf16[2,128,896]{2,1,0:T(8,128)(2,1)S(1)} %pad_maximum_fusion.16), channel_id=1, source_target_pairs={{0,1},{1,0},{2,3},{3,2},{4,5},{5,4},{6,7},{7,6},{8,9},{9,8},{10,11... | collective-permute-start | bytes 1376264 | tf_op jit(solution)/shard_map/ppermute | solution.py:183
  55.3 10.8 %collective-permute-start.19 = (bf16[2,128,768]{2,1,0:T(8,128)(2,1)S(1)}, bf16[2,128,768]{2,1,0:T(8,128)(2,1)S(1)}, u32[]{:S(2)}, u32[]{:S(2)}) collective-permute-start(bf16[2,128,768]{2,1,0:T(8,128)(2,1)S(1)} %pad_maximum_fusion.20), channel_id=1, source_target_pairs={{0,16},{8,24},{16,0},{24,8},{1,17},{9,25},{17,1},{25,9},{2,18},{10... | collective-permute-start | bytes 1179656 | tf_op jit(solution)/shard_map/ppermute | solution.py:180
  55.9 12.9 %collective-permute-start.25 = (bf16[4,128,512]{2,1,0:T(8,128)(2,1)S(1)}, bf16[4,128,512]{2,1,0:T(8,128)(2,1)S(1)}, u32[]{:S(2)}, u32[]{:S(2)}) collective-permute-start(bf16[4,128,512]{2,1,0:T(8,128)(2,1)S(1)} %collective-permute-done.24.refs_1_), channel_id=1, source_target_pairs={{0,2},{1,3},{2,4},{3,5},{4,6},{5,7},{6,0},{7,1},{8,10},{9,11},{10,... | collective-permute-start | bytes 1572872 | tf_op jit(solution)/shard_map/ppermute | solution.py:186
  64.5 23.2 %collective-permute-start.16 = (bf16[4,128,768]{2,1,0:T(8,128)(2,1)S(1)}, bf16[4,128,768]{2,1,0:T(8,128)(2,1)S(1)}, u32[]{:S(2)}, u32[]{:S(2)}) collective-permute-start(bf16[4,128,768]{2,1,0:T(8,128)(2,1)S(1)} %pad_maximum_fusion.7.refs_0_), channel_id=1, source_target_pairs={{0,1},{1,0},{2,3},{3,2},{4,5},{5,4},{6,7},{7,6},{8,9},{9,8},{10,11... | collective-permute-start | bytes 2359304 | tf_op jit(solution)/shard_map/ppermute | solution.py:183
  66.1 19.6 %collective-permute-start.6 = (bf16[4,128,896]{2,1,0:T(8,128)(2,1)S(1)}, bf16[4,128,896]{2,1,0:T(8,128)(2,1)S(1)}, u32[]{:S(2)}, u32[]{:S(2)}) collective-permute-start(bf16[4,128,896]{2,1,0:T(8,128)(2,1)S(1)} %pad_maximum_fusion.3.refs_2_), channel_id=1, source_target_pairs={{0,16},{8,24},{16,0},{24,8},{1,17},{9,25},{17,1},{25,9},{2,18},{10... | collective-permute-start | bytes 2752520 | tf_op jit(solution)/shard_map/ppermute | solution.py:180
  68.8 30.2 %collective-permute-start.20 = (bf16[4,128,768]{2,1,0:T(8,128)(2,1)S(1)}, bf16[4,128,768]{2,1,0:T(8,128)(2,1)S(1)}, u32[]{:S(2)}, u32[]{:S(2)}) collective-permute-start(bf16[4,128,768]{2,1,0:T(8,128)(2,1)S(1)} %pad_maximum_fusion.8.refs_2_), channel_id=1, source_target_pairs={{0,1},{1,0},{2,3},{3,2},{4,5},{5,4},{6,7},{7,6},{8,9},{9,8},{10,11... | collective-permute-start | bytes 2359304 | tf_op jit(solution)/shard_map/ppermute | solution.py:183
  69.9 36.3 %collective-permute-start.26 = (bf16[4,128,512]{2,1,0:T(8,128)(2,1)S(1)}, bf16[4,128,512]{2,1,0:T(8,128)(2,1)S(1)}, u32[]{:S(2)}, u32[]{:S(2)}) collective-permute-start(bf16[4,128,512]{2,1,0:T(8,128)(2,1)S(1)} %collective-permute-done.25.refs_2_), channel_id=1, source_target_pairs={{0,2},{1,3},{2,4},{3,5},{4,6},{5,7},{6,0},{7,1},{8,10},{9,11},{10,... | collective-permute-start | bytes 1572872 | tf_op jit(solution)/shard_map/ppermute | solution.py:186
  87.5 54.8 %collective-permute-start.13 = (bf16[16,56,896]{2,1,0:T(8,128)(2,1)S(1)}, bf16[16,56,896]{2,1,0:T(8,128)(2,1)S(1)}, u32[]{:S(2)}, u32[]{:S(2)}) collective-permute-start(bf16[16,56,896]{2,1,0:T(8,128)(2,1)S(1)} %get-tuple-element.30), channel_id=1, source_target_pairs={{0,8},{8,0},{16,24},{24,16},{1,9},{9,1},{17,25},{25,17},{2,10},{10... | collective-permute-start | bytes 4816904 | tf_op jit(solution)/shard_map/ppermute | solution.py:177
  87.6 13.8 %collective-permute-start.7 = (bf16[128,768]{1,0:T(8,128)(2,1)S(1)}, bf16[128,768]{1,0:T(8,128)(2,1)S(1)}, u32[]{:S(2)}, u32[]{:S(2)}) collective-permute-start(bf16[128,768]{1,0:T(8,128)(2,1)S(1)} %get-tuple-element.82), channel_id=1, source_target_pairs={{0,2},{1,3},{2,4},{3,5},{4,6},{5,7},{6,0},{7,1},{8,10},{9,11},{10,... | collective-permute-start | bytes 589832 | tf_op jit(solution)/shard_map/ppermute | solution.py:186
  87.7 13.9 %collective-permute-start.30 = (bf16[128,768]{1,0:T(8,128)(2,1)S(1)}, bf16[128,768]{1,0:T(8,128)(2,1)S(1)}, u32[]{:S(2)}, u32[]{:S(2)}) collective-permute-start(bf16[128,768]{1,0:T(8,128)(2,1)S(1)} %get-tuple-element.83), channel_id=1, source_target_pairs={{0,2},{1,3},{2,4},{3,5},{4,6},{5,7},{6,0},{7,1},{8,10},{9,11},{10,... | collective-permute-start | bytes 589832 | tf_op jit(solution)/shard_map/ppermute | solution.py:186
  99.0 7.1 %collective-permute-start.39 = (bf16[2,128,512]{2,1,0:T(8,128)(2,1)S(1)}, bf16[2,128,512]{2,1,0:T(8,128)(2,1)S(1)}, u32[]{:S(2)}, u32[]{:S(2)}) collective-permute-start(bf16[2,128,512]{2,1,0:T(8,128)(2,1)S(1)} %pad_maximum_fusion.24), channel_id=1, source_target_pairs={{0,1},{1,0},{2,3},{3,2},{4,5},{5,4},{6,7},{7,6},{8,9},{9,8},{10,11... | collective-permute-start | bytes 786440 | tf_op jit(solution)/shard_map/ppermute | solution.py:183
  101.4 39.1 %collective-permute-start.21 = (bf16[16,56,768]{2,1,0:T(8,128)(2,1)S(1)}, bf16[16,56,768]{2,1,0:T(8,128)(2,1)S(1)}, u32[]{:S(2)}, u32[]{:S(2)}) collective-permute-start(bf16[16,56,768]{2,1,0:T(8,128)(2,1)S(1)} %get-tuple-element.32), channel_id=1, source_target_pairs={{0,8},{8,0},{16,24},{24,16},{1,9},{9,1},{17,25},{25,17},{2,10},{10... | collective-permute-start | bytes 4128776 | tf_op jit(solution)/shard_map/ppermute | solution.py:177
  101.6 16.2 %collective-permute-start.8 = (bf16[2,128,768]{2,1,0:T(8,128)(2,1)S(1)}, bf16[2,128,768]{2,1,0:T(8,128)(2,1)S(1)}, u32[]{:S(2)}, u32[]{:S(2)}) collective-permute-start(bf16[2,128,768]{2,1,0:T(8,128)(2,1)S(1)} %pad_maximum_fusion.17), channel_id=1, source_target_pairs={{0,1},{1,0},{2,3},{3,2},{4,5},{5,4},{6,7},{7,6},{8,9},{9,8},{10,11... | collective-permute-start | bytes 1179656 | tf_op jit(solution)/shard_map/ppermute | solution.py:183
  106.1 7.9 %collective-permute-start.10 = (bf16[128,768]{1,0:T(8,128)(2,1)S(1)}, bf16[128,768]{1,0:T(8,128)(2,1)S(1)}, u32[]{:S(2)}, u32[]{:S(2)}) collective-permute-start(bf16[128,768]{1,0:T(8,128)(2,1)S(1)} %collective-permute-done.7), channel_id=1, source_target_pairs={{0,2},{1,3},{2,4},{3,5},{4,6},{5,7},{6,0},{7,1},{8,10},{9,11},{10,... | collective-permute-start | bytes 589832 | tf_op jit(solution)/shard_map/ppermute | solution.py:186
  106.1 11.7 %collective-permute-start.33 = (bf16[128,768]{1,0:T(8,128)(2,1)S(1)}, bf16[128,768]{1,0:T(8,128)(2,1)S(1)}, u32[]{:S(2)}, u32[]{:S(2)}) collective-permute-start(bf16[128,768]{1,0:T(8,128)(2,1)S(1)} %collective-permute-done.30), channel_id=1, source_target_pairs={{0,2},{1,3},{2,4},{3,5},{4,6},{5,7},{6,0},{7,1},{8,10},{9,11},{10,... | collective-permute-start | bytes 589832 | tf_op jit(solution)/shard_map/ppermute | solution.py:186
  114.0 7.5 %collective-permute-start.11 = (bf16[128,768]{1,0:T(8,128)(2,1)S(1)}, bf16[128,768]{1,0:T(8,128)(2,1)S(1)}, u32[]{:S(2)}, u32[]{:S(2)}) collective-permute-start(bf16[128,768]{1,0:T(8,128)(2,1)S(1)} %collective-permute-done.10), channel_id=1, source_target_pairs={{0,2},{1,3},{2,4},{3,5},{4,6},{5,7},{6,0},{7,1},{8,10},{9,11},{10,... | collective-permute-start | bytes 589832 | tf_op jit(solution)/shard_map/ppermute | solution.py:186
  117.8 20.9 %collective-permute-start.27 = (bf16[16,56,512]{2,1,0:T(8,128)(2,1)S(1)}, bf16[16,56,512]{2,1,0:T(8,128)(2,1)S(1)}, u32[]{:S(2)}, u32[]{:S(2)}) collective-permute-start(bf16[16,56,512]{2,1,0:T(8,128)(2,1)S(1)} %get-tuple-element.34), channel_id=1, source_target_pairs={{0,8},{8,0},{16,24},{24,16},{1,9},{9,1},{17,25},{25,17},{2,10},{10... | collective-permute-start | bytes 2752520 | tf_op jit(solution)/shard_map/ppermute | solution.py:177
  117.8 9.1 %collective-permute-start.34 = (bf16[128,768]{1,0:T(8,128)(2,1)S(1)}, bf16[128,768]{1,0:T(8,128)(2,1)S(1)}, u32[]{:S(2)}, u32[]{:S(2)}) collective-permute-start(bf16[128,768]{1,0:T(8,128)(2,1)S(1)} %collective-permute-done.33), channel_id=1, source_target_pairs={{0,2},{1,3},{2,4},{3,5},{4,6},{5,7},{6,0},{7,1},{8,10},{9,11},{10,... | collective-permute-start | bytes 589832 | tf_op jit(solution)/shard_map/ppermute | solution.py:186
  121.5 8.1 %collective-permute-start.31 = (bf16[2,128,768]{2,1,0:T(8,128)(2,1)S(1)}, bf16[2,128,768]{2,1,0:T(8,128)(2,1)S(1)}, u32[]{:S(2)}, u32[]{:S(2)}) collective-permute-start(bf16[2,128,768]{2,1,0:T(8,128)(2,1)S(1)} %pad_maximum_fusion.21), channel_id=1, source_target_pairs={{0,16},{8,24},{16,0},{24,8},{1,17},{9,25},{17,1},{25,9},{2,18},{10... | collective-permute-start | bytes 1179656 | tf_op jit(solution)/shard_map/ppermute | solution.py:180
  126.9 11.4 %collective-permute-start.12 = (bf16[2,128,768]{2,1,0:T(8,128)(2,1)S(1)}, bf16[2,128,768]{2,1,0:T(8,128)(2,1)S(1)}, u32[]{:S(2)}, u32[]{:S(2)}) collective-permute-start(bf16[2,128,768]{2,1,0:T(8,128)(2,1)S(1)} %pad_maximum_fusion.18), channel_id=1, source_target_pairs={{0,1},{1,0},{2,3},{3,2},{4,5},{5,4},{6,7},{7,6},{8,9},{9,8},{10,11... | collective-permute-start | bytes 1179656 | tf_op jit(solution)/shard_map/ppermute | solution.py:183
  129.6 39.5 %collective-permute-start.40 = (bf16[4,128,512]{2,1,0:T(8,128)(2,1)S(1)}, bf16[4,128,512]{2,1,0:T(8,128)(2,1)S(1)}, u32[]{:S(2)}, u32[]{:S(2)}) collective-permute-start(bf16[4,128,512]{2,1,0:T(8,128)(2,1)S(1)} %pad_maximum_fusion.12.refs_0_), channel_id=1, source_target_pairs={{0,2},{1,3},{2,4},{3,5},{4,6},{5,7},{6,0},{7,1},{8,10},{9,11},{10,... | collective-permute-start | bytes 1572872 | tf_op jit(solution)/shard_map/ppermute | solution.py:186
  138.3 43.2 %collective-permute-start.9 = (bf16[4,128,768]{2,1,0:T(8,128)(2,1)S(1)}, bf16[4,128,768]{2,1,0:T(8,128)(2,1)S(1)}, u32[]{:S(2)}, u32[]{:S(2)}) collective-permute-start(bf16[4,128,768]{2,1,0:T(8,128)(2,1)S(1)} %pad_maximum_fusion.5.refs_0_), channel_id=1, source_target_pairs={{0,16},{8,24},{16,0},{24,8},{1,17},{9,25},{17,1},{25,9},{2,18},{10... | collective-permute-start | bytes 2359304 | tf_op jit(solution)/shard_map/ppermute | solution.py:180
  138.7 44.4 %collective-permute-start.32 = (bf16[4,128,768]{2,1,0:T(8,128)(2,1)S(1)}, bf16[4,128,768]{2,1,0:T(8,128)(2,1)S(1)}, u32[]{:S(2)}, u32[]{:S(2)}) collective-permute-start(bf16[4,128,768]{2,1,0:T(8,128)(2,1)S(1)} %pad_maximum_fusion.9.refs_0_), channel_id=1, source_target_pairs={{0,1},{1,0},{2,3},{3,2},{4,5},{5,4},{6,7},{7,6},{8,9},{9,8},{10,11... | collective-permute-start | bytes 2359304 | tf_op jit(solution)/shard_map/ppermute | solution.py:183
  140.5 26.7 %collective-permute-start.35 = (bf16[2,128,768]{2,1,0:T(8,128)(2,1)S(1)}, bf16[2,128,768]{2,1,0:T(8,128)(2,1)S(1)}, u32[]{:S(2)}, u32[]{:S(2)}) collective-permute-start(bf16[2,128,768]{2,1,0:T(8,128)(2,1)S(1)} %pad_maximum_fusion.22), channel_id=1, source_target_pairs={{0,16},{8,24},{16,0},{24,8},{1,17},{9,25},{17,1},{25,9},{2,18},{10... | collective-permute-start | bytes 1179656 | tf_op jit(solution)/shard_map/ppermute | solution.py:180
  161.9 20.3 %collective-permute-start.28 = (bf16[4,128,768]{2,1,0:T(8,128)(2,1)S(1)}, bf16[4,128,768]{2,1,0:T(8,128)(2,1)S(1)}, u32[]{:S(2)}, u32[]{:S(2)}) collective-permute-start(bf16[4,128,768]{2,1,0:T(8,128)(2,1)S(1)} %pad_maximum_fusion.6.refs_2_), channel_id=1, source_target_pairs={{0,16},{8,24},{16,0},{24,8},{1,17},{9,25},{17,1},{25,9},{2,18},{10... | collective-permute-start | bytes 2359304 | tf_op jit(solution)/shard_map/ppermute | solution.py:180
  167.3 15.8 %collective-permute-start.36 = (bf16[4,128,768]{2,1,0:T(8,128)(2,1)S(1)}, bf16[4,128,768]{2,1,0:T(8,128)(2,1)S(1)}, u32[]{:S(2)}, u32[]{:S(2)}) collective-permute-start(bf16[4,128,768]{2,1,0:T(8,128)(2,1)S(1)} %pad_maximum_fusion.10.refs_2_), channel_id=1, source_target_pairs={{0,1},{1,0},{2,3},{3,2},{4,5},{5,4},{6,7},{7,6},{8,9},{9,8},{10,11... | collective-permute-start | bytes 2359304 | tf_op jit(solution)/shard_map/ppermute | solution.py:183
  169.1 12.2 %collective-permute-start.41 = (bf16[4,128,512]{2,1,0:T(8,128)(2,1)S(1)}, bf16[4,128,512]{2,1,0:T(8,128)(2,1)S(1)}, u32[]{:S(2)}, u32[]{:S(2)}) collective-permute-start(bf16[4,128,512]{2,1,0:T(8,128)(2,1)S(1)} %collective-permute-done.40.refs_1_), channel_id=1, source_target_pairs={{0,2},{1,3},{2,4},{3,5},{4,6},{5,7},{6,0},{7,1},{8,10},{9,11},{10,... | collective-permute-start | bytes 1572872 | tf_op jit(solution)/shard_map/ppermute | solution.py:186
  181.3 11.2 %collective-permute-start.42 = (bf16[4,128,512]{2,1,0:T(8,128)(2,1)S(1)}, bf16[4,128,512]{2,1,0:T(8,128)(2,1)S(1)}, u32[]{:S(2)}, u32[]{:S(2)}) collective-permute-start(bf16[4,128,512]{2,1,0:T(8,128)(2,1)S(1)} %collective-permute-done.41.refs_2_), channel_id=1, source_target_pairs={{0,2},{1,3},{2,4},{3,5},{4,6},{5,7},{6,0},{7,1},{8,10},{9,11},{10,... | collective-permute-start | bytes 1572872 | tf_op jit(solution)/shard_map/ppermute | solution.py:186
  183.0 12.6 %collective-permute-start.29 = (bf16[16,56,768]{2,1,0:T(8,128)(2,1)S(1)}, bf16[16,56,768]{2,1,0:T(8,128)(2,1)S(1)}, u32[]{:S(2)}, u32[]{:S(2)}) collective-permute-start(bf16[16,56,768]{2,1,0:T(8,128)(2,1)S(1)} %get-tuple-element.38), channel_id=1, source_target_pairs={{0,8},{8,0},{16,24},{24,16},{1,9},{9,1},{17,25},{25,17},{2,10},{10... | collective-permute-start | bytes 4128776 | tf_op jit(solution)/shard_map/ppermute | solution.py:177
  185.1 10.5 %collective-permute-start.37 = (bf16[16,56,768]{2,1,0:T(8,128)(2,1)S(1)}, bf16[16,56,768]{2,1,0:T(8,128)(2,1)S(1)}, u32[]{:S(2)}, u32[]{:S(2)}) collective-permute-start(bf16[16,56,768]{2,1,0:T(8,128)(2,1)S(1)} %get-tuple-element.42), channel_id=1, source_target_pairs={{0,8},{8,0},{16,24},{24,16},{1,9},{9,1},{17,25},{25,17},{2,10},{10... | collective-permute-start | bytes 4128776 | tf_op jit(solution)/shard_map/ppermute | solution.py:177
  219.6 120.3 %collective-permute-start.60 = (bf16[896,512]{1,0:T(8,128)(2,1)}, bf16[896,512]{1,0:T(8,128)(2,1)}, u32[]{:S(2)}, u32[]{:S(2)}) collective-permute-start(bf16[896,512]{1,0:T(8,128)(2,1)} %get-tuple-element.77), channel_id=1, source_target_pairs={{0,8},{8,0},{16,24},{24,16},{1,9},{9,1},{17,25},{25,17},{2,10},{10... | collective-permute-start | bytes 2752520 | tf_op jit(solution)/shard_map/ppermute | solution.py:177
  230.1 111.9 %collective-permute-start.52 = (bf16[896,768]{1,0:T(8,128)(2,1)}, bf16[896,768]{1,0:T(8,128)(2,1)}, u32[]{:S(2)}, u32[]{:S(2)}) collective-permute-start(bf16[896,768]{1,0:T(8,128)(2,1)} %get-tuple-element.71), channel_id=1, source_target_pairs={{0,8},{8,0},{16,24},{24,16},{1,9},{9,1},{17,25},{25,17},{2,10},{10... | collective-permute-start | bytes 4128776 | tf_op jit(solution)/shard_map/ppermute | solution.py:177
  244.0 114.6 %collective-permute-start.44 = (bf16[896,896]{1,0:T(8,128)(2,1)}, bf16[896,896]{1,0:T(8,128)(2,1)}, u32[]{:S(2)}, u32[]{:S(2)}) collective-permute-start(bf16[896,896]{1,0:T(8,128)(2,1)} %get-tuple-element.66), channel_id=1, source_target_pairs={{0,8},{8,0},{16,24},{24,16},{1,9},{9,1},{17,25},{25,17},{2,10},{10... | collective-permute-start | bytes 4816904 | tf_op jit(solution)/shard_map/ppermute | solution.py:177
  341.9 14.2 %collective-permute-start.61 = (bf16[2,2,128,512]{2,3,0,1:T(8,128)(2,1)S(1)}, bf16[2,2,128,512]{2,3,0,1:T(8,128)(2,1)S(1)}, u32[]{:S(2)}, u32[]{:S(2)}) collective-permute-start(bf16[2,2,128,512]{2,3,0,1:T(8,128)(2,1)S(1)} %convolution_convert_fusion.6), channel_id=1, source_target_pairs={{0,6},{1,7},{2,0},{3,1},{4,2},{5,3},{6,4},{7,5},{8,14},{9,15},{10,... | collective-permute-start | bytes 1572872 | tf_op jit(solution)/shard_map/ppermute | solution.py:191
  344.0 30.4 %collective-permute-start.55 = (bf16[2,2,128,768]{2,3,1,0:T(8,128)(2,1)S(1)}, bf16[2,2,128,768]{2,3,1,0:T(8,128)(2,1)S(1)}, u32[]{:S(2)}, u32[]{:S(2)}) collective-permute-start(bf16[2,2,128,768]{2,3,1,0:T(8,128)(2,1)S(1)} %convolution_convert_fusion.4), channel_id=1, source_target_pairs={{0,1},{1,0},{2,3},{3,2},{4,5},{5,4},{6,7},{7,6},{8,9},{9,8},{10,11... | collective-permute-start | bytes 2359304 | tf_op jit(solution)/shard_map/ppermute | solution.py:183
  344.6 36.1 %collective-permute-start.53 = (bf16[2,2,128,768]{2,3,1,0:T(8,128)(2,1)S(1)}, bf16[2,2,128,768]{2,3,1,0:T(8,128)(2,1)S(1)}, u32[]{:S(2)}, u32[]{:S(2)}) collective-permute-start(bf16[2,2,128,768]{2,3,1,0:T(8,128)(2,1)S(1)} %convolution_convert_fusion.5), channel_id=1, source_target_pairs={{0,1},{1,0},{2,3},{3,2},{4,5},{5,4},{6,7},{7,6},{8,9},{9,8},{10,11... | collective-permute-start | bytes 2359304 | tf_op jit(solution)/shard_map/ppermute | solution.py:183
  356.4 13.4 %collective-permute-start.62 = (bf16[2,2,128,512]{2,3,0,1:T(8,128)(2,1)S(1)}, bf16[2,2,128,512]{2,3,0,1:T(8,128)(2,1)S(1)}, u32[]{:S(2)}, u32[]{:S(2)}) collective-permute-start(bf16[2,2,128,512]{2,3,0,1:T(8,128)(2,1)S(1)} %add_convert_fusion.6), channel_id=1, source_target_pairs={{0,6},{1,7},{2,0},{3,1},{4,2},{5,3},{6,4},{7,5},{8,14},{9,15},{10,... | collective-permute-start | bytes 1572872 | tf_op jit(solution)/shard_map/ppermute | solution.py:191
  360.8 24.4 %collective-permute-start.47 = (bf16[2,2,128,896]{2,3,1,0:T(8,128)(2,1)S(1)}, bf16[2,2,128,896]{2,3,1,0:T(8,128)(2,1)S(1)}, u32[]{:S(2)}, u32[]{:S(2)}) collective-permute-start(bf16[2,2,128,896]{2,3,1,0:T(8,128)(2,1)S(1)} %convolution_convert_fusion.2), channel_id=1, source_target_pairs={{0,16},{8,24},{16,0},{24,8},{1,17},{9,25},{17,1},{25,9},{2,18},{10... | collective-permute-start | bytes 2752520 | tf_op jit(solution)/shard_map/ppermute | solution.py:180
  361.6 42.2 %collective-permute-start.45 = (bf16[2,2,128,896]{2,3,1,0:T(8,128)(2,1)S(1)}, bf16[2,2,128,896]{2,3,1,0:T(8,128)(2,1)S(1)}, u32[]{:S(2)}, u32[]{:S(2)}) collective-permute-start(bf16[2,2,128,896]{2,3,1,0:T(8,128)(2,1)S(1)} %convolution_convert_fusion.3), channel_id=1, source_target_pairs={{0,16},{8,24},{16,0},{24,8},{1,17},{9,25},{17,1},{25,9},{2,18},{10... | collective-permute-start | bytes 2752520 | tf_op jit(solution)/shard_map/ppermute | solution.py:180
  370.2 14.5 %collective-permute-start.63 = (bf16[2,2,128,512]{2,3,0,1:T(8,128)(2,1)S(1)}, bf16[2,2,128,512]{2,3,0,1:T(8,128)(2,1)S(1)}, u32[]{:S(2)}, u32[]{:S(2)}) collective-permute-start(bf16[2,2,128,512]{2,3,0,1:T(8,128)(2,1)S(1)} %add_convert_fusion.5), channel_id=1, source_target_pairs={{0,6},{1,7},{2,0},{3,1},{4,2},{5,3},{6,4},{7,5},{8,14},{9,15},{10,... | collective-permute-start | bytes 1572872 | tf_op jit(solution)/shard_map/ppermute | solution.py:191
  374.9 37.3 %collective-permute-start.56 = (bf16[2,128,768]{1,2,0:T(8,128)(2,1)S(1)}, bf16[2,128,768]{1,2,0:T(8,128)(2,1)S(1)}, u32[]{:S(2)}, u32[]{:S(2)}) collective-permute-start(bf16[2,128,768]{1,2,0:T(8,128)(2,1)S(1)} %slice_bitcast_fusion.19), channel_id=1, source_target_pairs={{0,16},{8,24},{16,0},{24,8},{1,17},{9,25},{17,1},{25,9},{2,18},{10... | collective-permute-start | bytes 1179656 | tf_op jit(solution)/shard_map/ppermute | solution.py:180
  381.2 38.0 %collective-permute-start.54 = (bf16[2,128,768]{1,2,0:T(8,128)(2,1)S(1)}, bf16[2,128,768]{1,2,0:T(8,128)(2,1)S(1)}, u32[]{:S(2)}, u32[]{:S(2)}) collective-permute-start(bf16[2,128,768]{1,2,0:T(8,128)(2,1)S(1)} %slice_bitcast_fusion.21), channel_id=1, source_target_pairs={{0,16},{8,24},{16,0},{24,8},{1,17},{9,25},{17,1},{25,9},{2,18},{10... | collective-permute-start | bytes 1179656 | tf_op jit(solution)/shard_map/ppermute | solution.py:180
  385.1 34.1 %collective-permute-start.64 = (bf16[2,128,512]{1,2,0:T(8,128)(2,1)S(1)}, bf16[2,128,512]{1,2,0:T(8,128)(2,1)S(1)}, u32[]{:S(2)}, u32[]{:S(2)}) collective-permute-start(bf16[2,128,512]{1,2,0:T(8,128)(2,1)S(1)} %slice_bitcast_fusion.23), channel_id=1, source_target_pairs={{0,1},{1,0},{2,3},{3,2},{4,5},{5,4},{6,7},{7,6},{8,9},{9,8},{10,11... | collective-permute-start | bytes 786440 | tf_op jit(solution)/shard_map/ppermute | solution.py:183
  385.8 38.7 %collective-permute-start.48 = (bf16[2,128,896]{1,2,0:T(8,128)(2,1)S(1)}, bf16[2,128,896]{1,2,0:T(8,128)(2,1)S(1)}, u32[]{:S(2)}, u32[]{:S(2)}) collective-permute-start(bf16[2,128,896]{1,2,0:T(8,128)(2,1)S(1)} %slice_bitcast_fusion.15), channel_id=1, source_target_pairs={{0,1},{1,0},{2,3},{3,2},{4,5},{5,4},{6,7},{7,6},{8,9},{9,8},{10,11... | collective-permute-start | bytes 1376264 | tf_op jit(solution)/shard_map/ppermute | solution.py:183
  404.3 30.6 %collective-permute-start.46 = (bf16[2,128,896]{1,2,0:T(8,128)(2,1)S(1)}, bf16[2,128,896]{1,2,0:T(8,128)(2,1)S(1)}, u32[]{:S(2)}, u32[]{:S(2)}) collective-permute-start(bf16[2,128,896]{1,2,0:T(8,128)(2,1)S(1)} %slice_bitcast_fusion.17), channel_id=1, source_target_pairs={{0,1},{1,0},{2,3},{3,2},{4,5},{5,4},{6,7},{7,6},{8,9},{9,8},{10,11... | collective-permute-start | bytes 1376264 | tf_op jit(solution)/shard_map/ppermute | solution.py:183
  412.3 7.4 %collective-permute-start.57 = (bf16[128,768]{0,1:T(8,128)(2,1)S(1)}, bf16[128,768]{0,1:T(8,128)(2,1)S(1)}, u32[]{:S(2)}, u32[]{:S(2)}) collective-permute-start(bf16[128,768]{0,1:T(8,128)(2,1)S(1)} %slice_bitcast_fusion.37), channel_id=1, source_target_pairs={{0,6},{1,7},{2,0},{3,1},{4,2},{5,3},{6,4},{7,5},{8,14},{9,15},{10,... | collective-permute-start | bytes 589832 | tf_op jit(solution)/shard_map/ppermute | solution.py:191
  419.4 5.0 %collective-permute-start.65 = (bf16[128,512]{0,1:T(8,128)(2,1)S(1)}, bf16[128,512]{0,1:T(8,128)(2,1)S(1)}, u32[]{:S(2)}, u32[]{:S(2)}) collective-permute-start(bf16[128,512]{0,1:T(8,128)(2,1)S(1)} %slice_bitcast_fusion.41), channel_id=1, source_target_pairs={{0,16},{8,24},{16,0},{24,8},{1,17},{9,25},{17,1},{25,9},{2,18},{10... | collective-permute-start | bytes 393224 | tf_op jit(solution)/shard_map/ppermute | solution.py:180
  419.8 6.5 %collective-permute-start.58 = (bf16[128,768]{0,1:T(8,128)(2,1)S(1)}, bf16[128,768]{0,1:T(8,128)(2,1)S(1)}, u32[]{:S(2)}, u32[]{:S(2)}) collective-permute-start(bf16[128,768]{0,1:T(8,128)(2,1)S(1)} %fusion.60), channel_id=1, source_target_pairs={{0,6},{1,7},{2,0},{3,1},{4,2},{5,3},{6,4},{7,5},{8,14},{9,15},{10,... | collective-permute-start | bytes 589832 | tf_op jit(solution)/shard_map/ppermute | solution.py:191
  424.6 8.6 %collective-permute-start.49 = (bf16[128,896]{0,1:T(8,128)(2,1)S(1)}, bf16[128,896]{0,1:T(8,128)(2,1)S(1)}, u32[]{:S(2)}, u32[]{:S(2)}) collective-permute-start(bf16[128,896]{0,1:T(8,128)(2,1)S(1)} %slice_bitcast_fusion.25), channel_id=1, source_target_pairs={{0,6},{1,7},{2,0},{3,1},{4,2},{5,3},{6,4},{7,5},{8,14},{9,15},{10,... | collective-permute-start | bytes 688136 | tf_op jit(solution)/shard_map/ppermute | solution.py:191
  426.3 16.6 %collective-permute-start.59 = (bf16[128,768]{0,1:T(8,128)(2,1)S(1)}, bf16[128,768]{0,1:T(8,128)(2,1)S(1)}, u32[]{:S(2)}, u32[]{:S(2)}) collective-permute-start(bf16[128,768]{0,1:T(8,128)(2,1)S(1)} %fusion.61), channel_id=1, source_target_pairs={{0,6},{1,7},{2,0},{3,1},{4,2},{5,3},{6,4},{7,5},{8,14},{9,15},{10,... | collective-permute-start | bytes 589832 | tf_op jit(solution)/shard_map/ppermute | solution.py:191
  433.3 6.3 %collective-permute-start.50 = (bf16[128,896]{0,1:T(8,128)(2,1)S(1)}, bf16[128,896]{0,1:T(8,128)(2,1)S(1)}, u32[]{:S(2)}, u32[]{:S(2)}) collective-permute-start(bf16[128,896]{0,1:T(8,128)(2,1)S(1)} %fusion.42), channel_id=1, source_target_pairs={{0,6},{1,7},{2,0},{3,1},{4,2},{5,3},{6,4},{7,5},{8,14},{9,15},{10,... | collective-permute-start | bytes 688136 | tf_op jit(solution)/shard_map/ppermute | solution.py:191
  439.6 6.8 %collective-permute-start.51 = (bf16[128,896]{0,1:T(8,128)(2,1)S(1)}, bf16[128,896]{0,1:T(8,128)(2,1)S(1)}, u32[]{:S(2)}, u32[]{:S(2)}) collective-permute-start(bf16[128,896]{0,1:T(8,128)(2,1)S(1)} %fusion.43), channel_id=1, source_target_pairs={{0,6},{1,7},{2,0},{3,1},{4,2},{5,3},{6,4},{7,5},{8,14},{9,15},{10,... | collective-permute-start | bytes 688136 | tf_op jit(solution)/shard_map/ppermute | solution.py:191
  (28 other events, 337.5 us)

commit v3 on v0

--- a/solution.py
+++ b/solution.py
@@ -1,9 +1,12 @@
 import jax
 import jax.numpy as jnp
 from jax import lax
+from jax.experimental import pallas as pl
+from jax.experimental.pallas import tpu as pltpu
 from jax.sharding import PartitionSpec as P
 
 block_rows = 256
+gather_limit = 32 * 2**20
 
 
 def expert_parts(inputs, cotangent_rows, router_weight, gate_matrix, up_matrix, down_matrix):
@@ -48,7 +51,7 @@
     return (gate_term, up_term, down_term)
 
 
-def on_device(tokens, cotangent, routes, gates, w_gate, w_up, w_down):
+def exchange_path(tokens, cotangent, routes, gates, w_gate, w_up, w_down):
     dp_count = lax.axis_size("dp")
     expert_count = lax.axis_size("expert")
     device_count = dp_count * expert_count
@@ -158,6 +161,448 @@
     )
 
 
+def gather_path(tokens, cotangent, routes, gates, w_gate, w_up, w_down):
+    dp_count = lax.axis_size("dp")
+    expert_count = lax.axis_size("expert")
+    device_count = dp_count * expert_count
+    tok_local, model_width = tokens.shape
+    hidden_width = w_gate.shape[2]
+    top_count = routes.shape[1]
+    most_rows = 7 * tok_local * top_count // (4 * device_count)
+    source_count = 16
+    half_rows = source_count * most_rows
+    bf16, f32 = jnp.bfloat16, jnp.float32
+
+    def swap_core(v):
+        return lax.ppermute(v, "dp", [(p, p ^ 1) for p in range(dp_count)])
+
+    def swap_x(v):
+        return lax.ppermute(v, "dp", [(p, p ^ 2) for p in range(dp_count)])
+
+    def swap_y(v):
+        return lax.ppermute(v, "expert", [(q, q ^ 1) for q in range(expert_count)])
+
+    def ring_up(v):
+        return lax.ppermute(
+            v, "expert", [(q, (q + 2) % expert_count) for q in range(expert_count)]
+        )
+
+    def ring_down(v):
+        return lax.ppermute(
+            v, "expert", [(q, (q - 2) % expert_count) for q in range(expert_count)]
+        )
+
+    dp_index = lax.axis_index("dp")
+    expert_index = lax.axis_index("expert")
+    mine = dp_index * expert_count + expert_index
+    other = (dp_index ^ 1) * expert_count + expert_index
+
+    hit = routes[:, :, None] == jnp.arange(device_count, dtype=jnp.int32)[None, None, :]
+    gate_dense = jnp.sum(jnp.where(hit, gates[:, :, None].astype(f32), 0.0), axis=1)
+    named = jnp.sum(hit.astype(f32), axis=1)
+    token_iota = jnp.arange(tok_local)
+    before = (token_iota[None, :] < token_iota[:, None]).astype(bf16)
+    rank = jnp.dot(before, named.astype(bf16), preferred_element_type=f32)
+    rank = jnp.where(named > 0.0, rank, -1.0)
+    info_width = -(-2 * device_count // 128) * 128
+    info = jnp.concatenate(
+        [
+            gate_dense.astype(bf16),
+            rank.astype(bf16),
+            jnp.zeros((tok_local, info_width - 2 * device_count), bf16),
+        ],
+        axis=1,
+    )
+
+    cuts = (0, 3 * model_width // 8, 3 * model_width // 4, model_width)
+
+    def part_of(v, n):
+        return v[:, cuts[n] : cuts[n + 1]]
+
+    links = {"x": [], "y": [], "z": []}
+    ways = {"x": swap_x, "y": swap_y, "z": ring_up, "d": ring_down}
+
+    def send(way, v):
+        queue = links["z" if way == "d" else way]
+        if len(queue) >= 2:
+            v, _ = lax.optimization_barrier((v, queue[-2]))
+        queue.append(ways[way](v))
+        return queue[-1]
+
+    order = [(g, i, j, s) for g in range(2) for i in range(2) for j in range(2) for s in range(2)]
+    where = [{}, {}, {}]
+    for g, i, j, s in order:
+        where[0][g, i, j, s] = (2 * g + i, 2 * j + s)
+        where[1][g, i, j, s] = (2 * g + j, 2 * i + s)
+        where[2][g, i, j, s] = (2 * g + s, 2 * j + i)
+
+    def with_other(way, v):
+        return jnp.concatenate([v, send(way, v)])
+
+    def compact(blocks, where):
+        width = blocks[0].shape[-1]
+
+        def body(places, *refs):
+            ins, keep, give = refs[: len(blocks)], refs[-2], refs[-1]
+            for n, source in enumerate(order):
+                block, at = where[source]
+                picked = jnp.dot(places[n], ins[block][at], preferred_element_type=f32)
+                keep[n] = picked[:most_rows].astype(bf16)
+                give[n] = picked[most_rows:].astype(bf16)
+
+        shape = jax.ShapeDtypeStruct((source_count, most_rows, width), bf16)
+        keep, give = pl.pallas_call(
+            body,
+            out_shape=(shape, shape),
+            in_specs=[pl.BlockSpec(memory_space=pltpu.VMEM)] * (1 + len(blocks)),
+            out_specs=(pl.BlockSpec(memory_space=pltpu.VMEM),) * 2,
+            compiler_params=pltpu.CompilerParams(vmem_limit_bytes=24 * 2**20),
+            cost_estimate=pl.CostEstimate(
+                flops=2 * source_count * 2 * most_rows * tok_local * width,
+                bytes_accessed=12 * 2**20,
+                transcendentals=0,
+            ),
+        )(place_both, *blocks)
+        return keep.reshape(half_rows, width), swap_core(give).reshape(half_rows, width)
+
+    block_rows_here = half_rows // 4
+
+    def row_call(body, ins, whole, outs, flops):
+        row_spec = [pl.BlockSpec((block_rows_here, v.shape[1]), lambda b: (b, 0)) for v in ins]
+        whole_spec = [
+            pl.BlockSpec(shape, lambda b, place=place: place, pipeline_mode=pl.Buffered(1))
+            for _, shape, place in whole
+        ]
+        outs = [out for out in outs for _ in range(2)]
+        return pl.pallas_call(
+            body,
+            grid=(4,),
+            out_shape=tuple(jax.ShapeDtypeStruct((half_rows, w), d) for w, d in outs),
+            in_specs=row_spec + whole_spec,
+            out_specs=tuple(pl.BlockSpec((block_rows_here, w), lambda b: (b, 0)) for w, _ in outs),
+            compiler_params=pltpu.CompilerParams(vmem_limit_bytes=44 * 2**20),
+            cost_estimate=pl.CostEstimate(
+                flops=flops, bytes_accessed=24 * 2**20, transcendentals=0
+            ),
+        )(*ins, *[v for v, _, _ in whole])
+
+    def both_halves(refs, at=slice(None)):
+        return jnp.concatenate([refs[0][:, at], refs[1][:, at]])
+
+    def put(refs, v, at=slice(None)):
+        refs[0][:, at] = v[:block_rows_here]
+        refs[1][:, at] = v[block_rows_here:]
+
+    nt = (((1,), (1,)), ((), ()))
+    gate_matrix, up_matrix, down_matrix = w_gate[0], w_up[0], w_down[0]
+    lanes = lax.broadcasted_iota(jnp.int32, (1, info_width), 1)
+    lane_mask = (lanes == mine).astype(f32)
+    mask_spec = (lane_mask, (1, info_width), (0, 0))
+    unit = 2 * 2 * half_rows * model_width * hidden_width
+
+    t0 = jnp.concatenate([part_of(tokens, 0), info], axis=1)
+    t1, t2 = part_of(tokens, 1), part_of(tokens, 2)
+    c0, c1, c2 = (part_of(cotangent, n) for n in range(3))
+    t0_hops, t1_hops, c0_hops, c1_hops = [t0], [t1], [c0], [c1]
+
+    def hop(hops):
+        hops.append(send("z", hops[-1]))
+
+    def near(way, hops, g):
+        return with_other(way, jnp.stack([hops[2 * g], hops[2 * g + 1]]))
+
+    hop(t0_hops)
+    hop(t1_hops)
+    t2_hops = [with_other("y", with_other("x", t2[None]))]
+    t0_near = [near("y", t0_hops, 0)]
+    t1_near = [near("x", t1_hops, 0)]
+    hop(t0_hops)
+    hop(t1_hops)
+    t0_far = [send("x", t0_near[0])]
+    t1_far = [send("y", t1_near[0])]
+    hop(t0_hops)
+    hop(t1_hops)
+    t1_near.append(near("x", t1_hops, 1))
+    t0_near.append(near("y", t0_hops, 1))
+    hop(t2_hops)
+    hop(c0_hops)
+    hop(c1_hops)
+    t0_far.append(send("x", t0_near[1]))
+    t1_far.append(send("y", t1_near[1]))
+    hop(t2_hops)
+    c2_hops = [with_other("y", with_other("x", c2[None]))]
+    c0_near = [near("y", c0_hops, 0)]
+    c1_near = [near("x", c1_hops, 0)]
+    hop(c0_hops)
+    hop(c1_hops)
+    hop(t2_hops)
+    c0_far = [send("x", c0_near[0])]
+    c1_far = [send("y", c1_near[0])]
+    hop(c0_hops)
+    hop(c1_hops)
+    c1_near.append(near("x", c1_hops, 1))
+    c0_near.append(near("y", c0_hops, 1))
+    hop(c2_hops)
+    c0_far.append(send("x", c0_near[1]))
+    c1_far.append(send("y", c1_near[1]))
+    hop(c2_hops)
+
+    t0_blocks = [t0_near[0], t0_far[0], t0_near[1], t0_far[1]]
+    t1_blocks = [t1_near[0], t1_far[0], t1_near[1], t1_far[1]]
+    got_info = jnp.stack(
+        [t0_blocks[where[0][k][0]][where[0][k][1], :, cuts[1] :] for k in order]
+    )
+    slots = jnp.arange(most_rows, dtype=f32)
+
+    def places_of(index):
+        at = lax.broadcasted_iota(jnp.int32, got_info.shape, 2) == device_count + index
+        ranks = jnp.sum(jnp.where(at, got_info, jnp.zeros((), bf16)).astype(f32), axis=-1)
+        return (ranks[:, None, :] == slots[:, None]).astype(bf16)
+
+    place_both = jnp.concatenate([places_of(mine), places_of(other)], axis=1)
+    rows = [
+        half
+        for n, blocks in enumerate((t0_blocks, t1_blocks, t2_hops))
+        for half in compact(blocks, where[n])
+    ]
+
+    def forward(*refs):
+        halves, (gates_at, wg, wu), outs = refs[:6], refs[6:9], refs[9:]
+        parts = [both_halves(halves[2 * n : 2 * n + 2], slice(0, cuts[n + 1] - cuts[n])) for n in range(3)]
+        sent = both_halves(halves[:2], slice(cuts[1], None))
+        row_gate = jnp.sum(sent.astype(f32) * gates_at[...], axis=1, keepdims=True)
+        pre_gate, pre_up = 0.0, 0.0
+        for n in range(3):
+            rows_at = slice(cuts[n], cuts[n + 1])
+            pre_gate += jnp.dot(parts[n], wg[rows_at], preferred_element_type=f32)
+            pre_up += jnp.dot(parts[n], wu[rows_at], preferred_element_type=f32)
+        sigmoid_gate = 1.0 / (1.0 + jnp.exp(-pre_gate))
+        silu_gate = pre_gate * sigmoid_gate
+        hidden = silu_gate * pre_up
+        put(outs[0:2], hidden)
+        slope = pre_up * sigmoid_gate * (1.0 + pre_gate * (1.0 - sigmoid_gate))
+        put(outs[2:4], row_gate * slope)
+        put(outs[4:6], row_gate * silu_gate)
+        put(outs[6:8], (row_gate * hidden).astype(bf16))
+
+    square = (model_width, hidden_width)
+    forward_out = row_call(
+        forward,
+        rows,
+        [mask_spec, (gate_matrix, square, (0, 0)), (up_matrix, square, (0, 0))],
+        [(hidden_width, f32)] * 3 + [(hidden_width, bf16)],
+        2 * unit,
+    )
+    before_last, held = lax.optimization_barrier((c2_hops[-1], forward_out[0]))
+    c2_hops.append(send("z", before_last))
+    kept, weighted = (held,) + forward_out[1:6], forward_out[6:]
+    c1_rows = compact([c1_near[0], c1_far[0], c1_near[1], c1_far[1]], where[1])
+    c0_rows = compact([c0_near[0], c0_far[0], c0_near[1], c0_far[1]], where[0])
+    cot_rows = [*c0_rows, *c1_rows, *compact(c2_hops, where[2])]
+
+    def row_grad(pgg, pug, wg, wu):
+        return lax.dot_general(pgg, wg, nt, preferred_element_type=f32) + lax.dot_general(
+            pug, wu, nt, preferred_element_type=f32
+        )
+
+    def backward(*refs):
+        halves, gated, slope, silu = refs[:6], refs[6:8], refs[8:10], refs[10:12]
+        (gates_at, wd, wg, wu), outs = refs[12:16], refs[16:]
+        back = 0.0
+        for n in range(3):
+            back += lax.dot_general(
+                both_halves(halves[2 * n : 2 * n + 2]),
+                wd[:, cuts[n] : cuts[n + 1]],
+                nt,
+                preferred_element_type=f32,
+            )
+        gate_grad = jnp.sum(both_halves(gated) * back, axis=1, keepdims=True)
+        gate_side = (back * both_halves(slope)).astype(bf16)
+        up_side = (back * both_halves(silu)).astype(bf16)
+        put(outs[0:2], gate_side)
+        put(outs[2:4], up_side)
+        put(outs[4:6], (gate_grad * gates_at[...]).astype(bf16))
+        put(outs[6:8], row_grad(gate_side, up_side, wg[...], wu[...]).astype(bf16))
+
+    last = (cuts[3] - cuts[2], hidden_width)
+    third = (cuts[1], hidden_width)
+    last_at = cuts[2] // last[0]
+    backward_out = row_call(
+        backward,
+        cot_rows + list(kept),
+        [
+            mask_spec,
+            (down_matrix, (hidden_width, model_width), (0, 0)),
+            (gate_matrix, last, (last_at, 0)),
+            (up_matrix, last, (last_at, 0)),
+        ],
+        [(hidden_width, bf16)] * 2 + [(info_width, bf16), (last[0], bf16)],
+        3 * unit // 2,
+    )
+    sides, gate_lanes, grad_last = backward_out[:4], backward_out[4:6], backward_out[6:]
+
+    def first_grad(*refs):
+        outs = refs[8:]
+        grad = row_grad(both_halves(refs[0:2]), both_halves(refs[2:4]), refs[6][...], refs[7][...])
+        put(outs, grad.astype(bf16), slice(0, cuts[1]))
+        put(outs, both_halves(refs[4:6]), slice(cuts[1], None))
+
+    def second_grad(*refs):
+        grad = row_grad(both_halves(refs[0:2]), both_halves(refs[2:4]), refs[4][...], refs[5][...])
+        put(refs[6:], grad.astype(bf16))
+
+    grad_first = row_call(
+        first_grad,
+        [*sides, *gate_lanes],
+        [(gate_matrix, third, (0, 0)), (up_matrix, third, (0, 0))],
+        [(info_width + third[0], bf16)],
+        3 * unit // 4,
+    )
+    grad_second = row_call(
+        second_grad,
+        [*sides],
+        [(gate_matrix, third, (1, 0)), (up_matrix, third, (1, 0))],
+        [(third[0], bf16)],
+        3 * unit // 4,
+    )
+
+    place_grid = place_both.reshape(2, 2, 2, 2, 2 * most_rows, tok_local)
+
+    def pair_rows(halves):
+        width = halves[0].shape[-1]
+        own = halves[0].reshape(source_count, most_rows, width)
+        given = swap_core(halves[1]).reshape(source_count, most_rows, width)
+        return jnp.concatenate([own, given], axis=1).reshape(2, 2, 2, 2, 2 * most_rows, width)
+
+    def spread(places, v):
+        return jnp.einsum("...ct,...cd->...td", places, v, preferred_element_type=f32)
+
+    def add(own, arrived):
+        return (own.astype(f32) + arrived.astype(f32)).astype(bf16)
+
+    links["x"].clear()
+    links["y"].clear()
+    links["z"].clear()
+    v2 = pair_rows(grad_last)
+    v0 = pair_rows(grad_first)
+    v1 = pair_rows(grad_second)
+
+    def spread_last(r):
+        return spread(place_grid[r // 2, :, :, r % 2], v2[r // 2, :, :, r % 2])
+
+    first_last = spread_last(3).astype(bf16)
+    moving2 = send("d", first_last)
+    far0 = [spread(place_grid[g, 1], v0[g, 1]).astype(bf16) for g in range(2)]
+    far1 = [spread(place_grid[g, :, 1], v1[g, :, 1]).astype(bf16) for g in range(2)]
+    sent0, sent1, half0, half1, near0, near1 = ([None, None] for _ in range(6))
+    sent0[1] = send("x", far0[1])
+    sent1[1] = send("y", far1[1])
+    sides_tied, _, _, _ = lax.optimization_barrier((sides, far0[1], far1[1], first_last))
+    moving2 = send("d", add(spread_last(2), moving2))
+    half1[1] = add(spread(place_grid[1, :, 0], v1[1, :, 0]), sent1[1])
+    near1[1] = send("x", half1[1][1])
+    half0[1] = add(spread(place_grid[1, 0], v0[1, 0]), sent0[1])
+    near0[1] = send("y", half0[1][1])
+    weighted_tied, _, _ = lax.optimization_barrier((weighted, half0[1], half1[1]))
+    sent0[0] = send("x", far0[0])
+    sent1[0] = send("y", far1[0])
+    moving2 = send("d", add(spread_last(1), moving2))
+    sum0_high = add(half0[1][0], near0[1])
+    sum1_high = add(half1[1][0], near1[1])
+    moving0 = send("d", sum0_high[1])
+    moving1 = send("d", sum1_high[1])
+    half1[0] = add(spread(place_grid[0, :, 0], v1[0, :, 0]), sent1[0])
+    near1[0] = send("x", half1[0][1])
+    half0[0] = add(spread(place_grid[0, 0], v0[0, 0]), sent0[0])
+    near0[0] = send("y", half0[0][1])
+    moving0 = send("d", add(sum0_high[0], moving0))
+    moving1 = send("d", add(sum1_high[0], moving1))
+    pair = add(spread_last(0), moving2)
+    pair = add(pair[:, 0], send("y", pair[:, 1]))
+    sum_last = add(pair[0], send("x", pair[1]))
+    sum0_low = add(half0[0][0], near0[0])
+    sum1_low = add(half1[0][0], near1[0])
+    moving0 = send("d", add(sum0_low[1], moving0))
+    moving1 = send("d", add(sum1_low[1], moving1))
+    sum_first = add(sum0_low[0], moving0)
+    sum_second = add(sum1_low[0], moving1)
+    gate_back = sum_first[:, cuts[1] : cuts[1] + device_count].astype(f32)
+    input_grad = jnp.concatenate([sum_first[:, : cuts[1]], sum_second, sum_last], axis=1)
+    gate_grad_out = jnp.sum(jnp.where(hit, gate_back[:, None, :], 0.0), axis=2).astype(bf16)
+
+    tile = 256
+    firsts = [cut // tile for cut in cuts]
+
+    def tile_spec(n):
+        top = firsts[n + 1] - firsts[n] - 1
+        return pl.BlockSpec(
+            (half_rows, tile), lambda b: (0, jnp.clip(b - firsts[n], 0, top))
+        )
+
+    tile_specs = [tile_spec(n) for n in range(3) for _ in range(2)]
+    tn = (((0,), (0,)), ((), ()))
+
+    def tn_dot(a, b):
+        return lax.dot_general(a, b, tn, preferred_element_type=f32)
+
+    def side_weights(*refs):
+        halves, (pgg0, pgg1, pug0, pug1), (gate_out, up_out) = refs[:6], refs[6:10], refs[10:]
+        step = pl.program_id(0)
+        for n in range(3):
+
+            @pl.when((step >= firsts[n]) & (step < firsts[n + 1]))
+            def _(n=n):
+                x0, x1 = halves[2 * n][...], halves[2 * n + 1][...]
+                gate_out[...] = (tn_dot(x0, pgg0[...]) + tn_dot(x1, pgg1[...])).astype(bf16)
+                up_out[...] = (tn_dot(x0, pug0[...]) + tn_dot(x1, pug1[...])).astype(bf16)
+
+    def down_weights(*refs):
+        halves, (w0, w1), out = refs[:6], refs[6:8], refs[8]
+        step = pl.program_id(0)
+        for n in range(3):
+
+            @pl.when((step >= firsts[n]) & (step < firsts[n + 1]))
+            def _(n=n):
+                c0_tile, c1_tile = halves[2 * n][...], halves[2 * n + 1][...]
+                out[...] = (tn_dot(w0[...], c0_tile) + tn_dot(w1[...], c1_tile)).astype(bf16)
+
+    half_spec = pl.BlockSpec(
+        (half_rows, hidden_width), lambda b: (0, 0), pipeline_mode=pl.Buffered(1)
+    )
+    grad_spec = pl.BlockSpec((tile, hidden_width), lambda b: (b, 0))
+    grad_shape = jax.ShapeDtypeStruct((model_width, hidden_width), bf16)
+    w_gate_grad, w_up_grad = pl.pallas_call(
+        side_weights,
+        grid=(firsts[3],),
+        out_shape=(grad_shape, grad_shape),
+        in_specs=tile_specs + [half_spec] * 4,
+        out_specs=(grad_spec, grad_spec),
+        compiler_params=pltpu.CompilerParams(vmem_limit_bytes=28 * 2**20),
+        cost_estimate=pl.CostEstimate(
+            flops=2 * unit, bytes_accessed=20 * 2**20, transcendentals=0
+        ),
+    )(*rows, *sides_tied)
+    w_down_grad = pl.pallas_call(
+        down_weights,
+        grid=(firsts[3],),
+        out_shape=jax.ShapeDtypeStruct((hidden_width, model_width), bf16),
+        in_specs=tile_specs + [half_spec] * 2,
+        out_specs=pl.BlockSpec((hidden_width, tile), lambda b: (0, b)),
+        compiler_params=pltpu.CompilerParams(vmem_limit_bytes=28 * 2**20),
+        cost_estimate=pl.CostEstimate(flops=unit, bytes_accessed=14 * 2**20, transcendentals=0),
+    )(*cot_rows, *weighted_tied)
+    return (input_grad, gate_grad_out, w_gate_grad[None], w_up_grad[None], w_down_grad[None])
+
+
+def on_device(tokens, cotangent, routes, gates, w_gate, w_up, w_down):
+    dp_count = lax.axis_size("dp")
+    expert_count = lax.axis_size("expert")
+    gathered_bytes = dp_count * expert_count * tokens.size * 2
+    if dp_count == 4 and expert_count == 8 and gathered_bytes <= gather_limit:
+        return gather_path(tokens, cotangent, routes, gates, w_gate, w_up, w_down)
+    return exchange_path(tokens, cotangent, routes, gates, w_gate, w_up, w_down)
+
+
 def solution(mesh):
     in_specs = (
         P(("dp", "expert"), None),

time: 1060 us -> 331 us (0.31); the launches traced: 1050 us -> 331 us
  blocking collectives: 362 us -> 0 us
  local copies, waits for them, and re-layouts: 187 us -> 12.9 us
  waiting for transfers between devices: 304 us -> 156 us
  matrix products: 135 us -> 5.27 us
  Pallas kernels: 0 us -> 83.7 us
  starting transfers between devices: 14.7 us -> 64.6 us
  other arithmetic: 39.9 us -> 6.63 us
    all_to_all x2 -> x0, blocking collectives: 362 us -> none  [the longest x1 193 us: on_device(): lax.all_to_all(gate_out, ('dp', 'expert'), split_axis=0, concat_axis=0, t...]
    all_to_all x3 -> x0, waiting for transfers between devices: 304 us -> none  [the longest x1 157 us: on_device(): lax.all_to_all(send_tokens, ('dp', 'expert'), split_axis=0, concat_axis=0...]
    ppermute x0 -> x66, waiting for transfers between devices: none -> 156 us  [the longest x18 70.4 us: ring_up(): lax.ppermute(v, 'expert', [(q, (q + 2) % expert_count) for q in range(exp...]
    dot_general x36 -> x13, matrix products: 135 us -> 5.27 us  [the longest x12 5.14 us: spread(): jnp.einsum('...ct,...cd->...td', places, v, preferred_element_type=f32)]
    gather x17 -> x0, local copies, waits for them, and re-layouts: 106 us -> none  [the longest x4 25.6 us: block_step(): got_tokens[safe_pick]]
    pallas_call x0 -> x12, Pallas kernels: none -> 83.7 us  [the longest x4 51.9 us: row_call(): pl.pallas_call(body, grid=(4,), out_shape=tuple((jax.ShapeDtypeStruct((ha...]
    ppermute x0 -> x66, starting transfers between devices: none -> 64.6 us  [the longest x15 20.5 us: swap_x(): return lax.ppermute(v, 'dp', [(p, p ^ 2) for p in range(dp_count)])]
    scatter x10 -> x0, local copies, waits for them, and re-layouts: 61.3 us -> none  [the longest x4 41.1 us: block_step(): grad_slots = grad_slots.at[target].set(row_grad, mode='drop')]
  transfers between devices with their start and end apart: 3 -> 66, of which waited for: 2 -> 28; matrix products, arithmetic and copies ran while one was open for 5% -> 3% of each run, Pallas kernels for 0% -> 19%
where the time goes in v3:
time: 331 us
  waiting for transfers between devices  156 us (47%)
  Pallas kernels  83.7 us (25%)
  starting transfers between devices  64.6 us (20%)
  local copies, waits for them, and re-layouts  12.9 us (4%)
  other arithmetic  6.63 us (2%)
  matrix products  5.27 us (2%)
    ppermute x18, waiting for transfers between devices, ring_up(): lax.ppermute(v, 'expert', [(q, (q + 2) % expert_count) for q in range(exp...  70.4 us
    pallas_call x4, Pallas kernels, row_call(): pl.pallas_call(body, grid=(4,), out_shape=tuple((jax.ShapeDtypeStruct((ha...  51.9 us
    ppermute x9, waiting for transfers between devices, ring_down(): lax.ppermute(v, 'expert', [(q, (q - 2) % expert_count) for q in range(exp...  33.4 us
    ppermute x15, waiting for transfers between devices, swap_x(): return lax.ppermute(v, 'dp', [(p, p ^ 2) for p in range(dp_count)])  30.5 us
    ppermute x15, starting transfers between devices, swap_x(): return lax.ppermute(v, 'dp', [(p, p ^ 2) for p in range(dp_count)])  20.5 us
    ppermute x15, waiting for transfers between devices, swap_y(): return lax.ppermute(v, 'expert', [(q, q ^ 1) for q in range(expert_count)])  19.5 us
    ppermute x15, starting transfers between devices, swap_y(): return lax.ppermute(v, 'expert', [(q, q ^ 1) for q in range(expert_count)])  17.1 us
    pallas_call x1, Pallas kernels, gather_path(): pl.pallas_call(side_weights, grid=(firsts[3],), out_shape=(grad_shape, gr...  16.8 us
  transfers between devices with their start and end apart: 66, of which 28 were waited for; matrix products, arithmetic and copies ran while one was open for 3% of the time, Pallas kernels for 19%

profile of v3, /device:TPU:0, one launch (start us, length us, event | category | flops | bytes accessed | tf_op | source)
XLA Modules:
  0.0 330.9 jit_solution(13057736205856590031)
XLA Ops:
  2.3 1.7 slice_bitcast_fusion.23
  4.4 3.1 collective-permute-start
  8.4 1.6 collective-permute-start.2
  9.9 1.6 collective-permute-start.8
  11.7 1.6 collective-permute-done.2
  13.4 1.6 collective-permute-start.14
  15.0 4.3 %collective-permute-done.8 = bf16[128,768]{1,0:T(8,128)(2,1)S(1)} collective-permute-done((bf16[128,768]{1,0:T(8,128)(2,1)}, bf16[128,768]{1,0:T(8,128)(2,1)S(1)}, u32[]{:S(2)}, u32[]{:S(2)}) %collective-permute-start.8) | collective-permute-done | bytes 196640 | tf_op jit(solution)/shard_map/ppermute | solution.py:186
  19.3 1.6 collective-permute-start.1
  21.0 1.6 collective-permute-start.12
  22.5 1.3 collective-permute-start.4
  23.8 5.1 %collective-permute-done.9 = bf16[128,768]{1,0:T(8,128)(2,1)S(1)} collective-permute-done((bf16[128,768]{1,0:T(8,128)(2,1)S(1)}, bf16[128,768]{1,0:T(8,128)(2,1)S(1)}, u32[]{:S(2)}, u32[]{:S(2)}) %collective-permute-start.9) | collective-permute-done | bytes 196640 | tf_op jit(solution)/shard_map/ppermute | solution.py:186
  29.0 4.9 %collective-permute-done.4 = bf16[128,896]{1,0:T(8,128)(2,1)S(1)} collective-permute-done((bf16[128,896]{1,0:T(8,128)(2,1)S(1)}, bf16[128,896]{1,0:T(8,128)(2,1)S(1)}, u32[]{:S(2)}, u32[]{:S(2)}) %collective-permute-start.4) | collective-permute-done | bytes 229408 | tf_op jit(solution)/shard_map/ppermute | solution.py:186
  34.0 1.6 collective-permute-start.3
  35.5 2.5 collective-permute-done.10
  38.1 2.0 collective-permute-start.13
  40.0 3.7 %collective-permute-done.5 = bf16[128,896]{1,0:T(8,128)(2,1)S(1)} collective-permute-done((bf16[128,896]{1,0:T(8,128)(2,1)S(1)}, bf16[128,896]{1,0:T(8,128)(2,1)S(1)}, u32[]{:S(2)}, u32[]{:S(2)}) %collective-permute-start.5) | collective-permute-done | bytes 229408 | tf_op jit(solution)/shard_map/ppermute | solution.py:186
  43.8 1.6 collective-permute-start.15
  45.4 4.2 %collective-permute-done.11 = bf16[128,768]{1,0:T(8,128)(2,1)S(1)} collective-permute-done((bf16[128,768]{1,0:T(8,128)(2,1)S(1)}, bf16[128,768]{1,0:T(8,128)(2,1)S(1)}, u32[]{:S(2)}, u32[]{:S(2)}) %collective-permute-start.11) | collective-permute-done | bytes 196640 | tf_op jit(solution)/shard_map/ppermute | solution.py:186
  49.7 1.5 collective-permute-start.6
  51.3 11.5 %collective-permute-done.13 = bf16[2,128,768]{2,1,0:T(8,128)(2,1)S(1)} collective-permute-done((bf16[2,128,768]{2,1,0:T(8,128)(2,1)S(1)}, bf16[2,128,768]{2,1,0:T(8,128)(2,1)S(1)}, u32[]{:S(2)}, u32[]{:S(2)}) %collective-permute-start.13) | collective-permute-done | bytes 393248 | tf_op jit(solution)/shard_map/ppermute | solution.py:180
  63.8 5.1 %collective-permute-done.6 = bf16[2,128,896]{2,1,0:T(8,128)(2,1)S(1)} collective-permute-done((bf16[2,128,896]{2,1,0:T(8,128)(2,1)S(1)}, bf16[2,128,896]{2,1,0:T(8,128)(2,1)S(1)}, u32[]{:S(2)}, u32[]{:S(2)}) %collective-permute-start.6) | collective-permute-done | bytes 458784 | tf_op jit(solution)/shard_map/ppermute | solution.py:183
  69.1 2.6 collective-permute-start.7
  71.6 1.4 collective-permute-start.30
  73.7 5.4 %collective-permute-done.21 = bf16[128,768]{1,0:T(8,128)(2,1)S(1)} collective-permute-done((bf16[128,768]{1,0:T(8,128)(2,1)S(1)}, bf16[128,768]{1,0:T(8,128)(2,1)S(1)}, u32[]{:S(2)}, u32[]{:S(2)}) %collective-permute-start.21) | collective-permute-done | bytes 196640 | tf_op jit(solution)/shard_map/ppermute | solution.py:186
  79.2 9.6 %collective-permute-done.22 = bf16[128,768]{1,0:T(8,128)(2,1)S(1)} collective-permute-done((bf16[128,768]{1,0:T(8,128)(2,1)S(1)}, bf16[128,768]{1,0:T(8,128)(2,1)S(1)}, u32[]{:S(2)}, u32[]{:S(2)}) %collective-permute-start.22) | collective-permute-done | bytes 196640 | tf_op jit(solution)/shard_map/ppermute | solution.py:186
  88.9 17.2 %collective-permute-done.24 = bf16[128,768]{1,0:T(8,128)(2,1)S(1)} collective-permute-done((bf16[128,768]{1,0:T(8,128)(2,1)S(1)}, bf16[128,768]{1,0:T(8,128)(2,1)S(1)}, u32[]{:S(2)}, u32[]{:S(2)}) %collective-permute-start.24) | collective-permute-done | bytes 196640 | tf_op jit(solution)/shard_map/ppermute | solution.py:186
  106.8 1.1 shard_map.112
  108.1 1.6 collective-permute-start.17
  110.5 3.1 collective-permute-done.25
  114.5 1.7 collective-permute-done.33
  116.3 3.4 %collective-permute-done.17 = bf16[2,128,768]{2,1,0:T(8,128)(2,1)S(1)} collective-permute-done((bf16[2,128,768]{2,1,0:T(8,128)(2,1)S(1)}, bf16[2,128,768]{2,1,0:T(8,128)(2,1)S(1)}, u32[]{:S(2)}, u32[]{:S(2)}) %collective-permute-start.17) | collective-permute-done | bytes 393248 | tf_op jit(solution)/shard_map/ppermute | solution.py:183
  119.6 1.5 collective-permute-start.26
  122.7 4.2 %collective-permute-done.37.refs_1_ = bf16[4,128,512]{2,1,0:T(8,128)(2,1)S(1)} collective-permute-done((bf16[4,128,512]{2,1,0:T(8,128)(2,1)S(1)}, bf16[4,128,512]{2,1,0:T(8,128)(2,1)S(1)}, u32[]{:S(2)}, u32[]{:S(2)}) %collective-permute-start.37) | collective-permute-done | bytes 524320 | tf_op jit(solution)/shard_map/ppermute | solution.py:186
  127.0 3.3 %collective-permute-done.26 = bf16[2,128,768]{2,1,0:T(8,128)(2,1)S(1)} collective-permute-done((bf16[2,128,768]{2,1,0:T(8,128)(2,1)S(1)}, bf16[2,128,768]{2,1,0:T(8,128)(2,1)S(1)}, u32[]{:S(2)}, u32[]{:S(2)}) %collective-permute-start.26) | collective-permute-done | bytes 393248 | tf_op jit(solution)/shard_map/ppermute | solution.py:183
  130.4 1.5 collective-permute-start.19
  132.9 15.8 %collective-permute-done.19.refs_1_ = bf16[4,128,768]{2,1,0:T(8,128)(2,1)S(1)} collective-permute-done((bf16[4,128,768]{2,1,0:T(8,128)(2,1)S(1)}, bf16[4,128,768]{2,1,0:T(8,128)(2,1)S(1)}, u32[]{:S(2)}, u32[]{:S(2)}) %collective-permute-start.19) | collective-permute-done | bytes 786464 | tf_op jit(solution)/shard_map/ppermute | solution.py:180
  151.9 1.1 copy-done.10
  153.0 1.1 copy-done.8
  154.2 1.3 copy-done.11
  155.5 18.8 %shard_map.115 = (f32[896,768]{1,0:T(8,128)}, f32[896,768]{1,0:T(8,128)}, f32[896,768]{1,0:T(8,128)}, f32[896,768]{1,0:T(8,128)}, f32[896,768]{1,0:T(8,128)}, /*...) custom-call(bf16[896,896]{1,0:T(8,128)(2,1)S(1)} %bitcast.231, ...), custom_call_target="tpu_custom_call" | custom-call | flops 11274289152 | bytes 25165824 | tf_op jit(solution)/shard_map/pallas_call | solution.py:277
  175.3 4.0 %collective-permute-start.42 = (bf16[4,128,512]{2,1,0:T(8,128)(2,1)S(1)}, bf16[4,128,512]{2,1,0:T(8,128)(2,1)S(1)}, u32[]{:S(2)}, u32[]{:S(2)}) collective-permute-start(bf16[4,128,512]{2,1,0:T(8,128)(2,1)S(1)} %collective-permute-done.38.refs_2_), channel_id=1, source_target_pairs={{0,2},{1,3},{2,4},{3,5},{4,6},{5,7},{6,0},{7,1},{8,10},{9,11},{10,... | collective-permute-start | bytes 1572872 | tf_op jit(solution)/shard_map/ppermute | solution.py:186
  183.7 4.5 %collective-permute-done.42.refs_3_ = bf16[4,128,512]{2,1,0:T(8,128)(2,1)S(1)} collective-permute-done((bf16[4,128,512]{2,1,0:T(8,128)(2,1)S(1)}, bf16[4,128,512]{2,1,0:T(8,128)(2,1)S(1)}, u32[]{:S(2)}, u32[]{:S(2)}) %collective-permute-start.42) | collective-permute-done | bytes 524320 | tf_op jit(solution)/shard_map/ppermute | solution.py:186
  189.0 2.4 collective-permute-done.43
  192.5 19.6 %shard_map.117 = (bf16[896,768]{1,0:T(8,128)(2,1)S(1)}, bf16[896,768]{1,0:T(8,128)(2,1)S(1)}, bf16[896,768]{1,0:T(8,128)(2,1)S(1)}, bf16[896,768]{1,0:T(8,128)(2...) custom-call(bf16[896,768]{1,0:T(8,128)(2,1)} %bitcast.218, ...), custom_call_target="tpu_custom_call" | custom-call | flops 8455716864 | bytes 25165824 | tf_op jit(solution)/shard_map/pallas_call | solution.py:277
  212.3 6.7 %shard_map.119 = (bf16[896,768]{1,0:T(8,128)(2,1)S(1)}, bf16[896,768]{1,0:T(8,128)(2,1)S(1)}) custom-call(bf16[896,768]{1,0:T(8,128)(2,1)S(1)} %get-tuple-element.169.refs_0_.refs_6_, bf16[896,768]{1,0:T(8,128)(2,1)S(1)} %get-tuple-element.170.refs_1_.refs_7_, bf16[896,768]{1,0:T(8,128)(2,1)S(1)} %get-tuple-element.171.refs_2_.refs_8_, ...), custom_call_target="tpu_custom_call" | custom-call | flops 4227858432 | bytes 25165824 | tf_op jit(solution)/shard_map/pallas_call | solution.py:277
  219.5 6.8 %shard_map.118 = (bf16[896,896]{1,0:T(8,128)(2,1)S(1)}, bf16[896,896]{1,0:T(8,128)(2,1)S(1)}) custom-call(bf16[896,768]{1,0:T(8,128)(2,1)S(1)} %get-tuple-element.169.refs_0_.refs_6_, bf16[896,768]{1,0:T(8,128)(2,1)S(1)} %get-tuple-element.170.refs_1_.refs_7_, bf16[896,768]{1,0:T(8,128)(2,1)S(1)} %get-tuple-element.171.refs_2_.refs_8_, ...), custom_call_target="tpu_custom_call" | custom-call | flops 4227858432 | bytes 25165824 | tf_op jit(solution)/shard_map/pallas_call | solution.py:277
  226.7 1.5 fusion.42
  228.5 2.1 collective-permute-start.50
  232.1 10.8 %collective-permute-done.50 = bf16[2,2,128,512]{2,3,0,1:T(8,128)(2,1)S(1)} collective-permute-done((bf16[2,2,128,512]{2,3,0,1:T(8,128)(2,1)S(1)}, bf16[2,2,128,512]{2,3,0,1:T(8,128)(2,1)S(1)}, u32[]{:S(2)}, u32[]{:S(2)}) %collective-permute-start.50) | collective-permute-done | bytes 524320 | tf_op jit(solution)/shard_map/ppermute | solution.py:191
  243.3 3.9 %collective-permute-start.51 = (bf16[2,2,128,512]{2,3,0,1:T(8,128)(2,1)S(1)}, bf16[2,2,128,512]{2,3,0,1:T(8,128)(2,1)S(1)}, u32[]{:S(2)}, u32[]{:S(2)}) collective-permute-start(bf16[2,2,128,512]{2,3,0,1:T(8,128)(2,1)S(1)} %add_convert_fusion.6), channel_id=1, source_target_pairs={{0,6},{1,7},{2,0},{3,1},{4,2},{5,3},{6,4},{7,5},{8,14},{9,15},{10,... | collective-permute-start | bytes 1572872 | tf_op jit(solution)/shard_map/ppermute | solution.py:191
  249.3 16.8 %shard_map.120 = (bf16[2048,768]{1,0:T(8,128)(2,1)}, bf16[2048,768]{1,0:T(8,128)(2,1)}) custom-call(bf16[896,896]{1,0:T(8,128)(2,1)S(1)} %bitcast.232, bf16[896,896]{1,0:T(8,128)(2,1)S(1)} %bitcast.234, bf16[896,768]{1,0:T(8,128)(2,1)S(1)} %bitcast.236, bf16[896,768]{1,0:T(8,128)(2,1)S(1)} %bitcast.238, bf16[896,512]{1,0:T(8,128)(2,1)S(1)} %bitcast.240, ...), custom_call_target="tpu_custom_call" | custom-call | flops 11274289152 | bytes 20971520 | tf_op jit(solution)/shard_map/pallas_call | solution.py:574
  268.2 1.5 collective-permute-start.58
  269.7 9.9 %collective-permute-done.60 = bf16[2,2,128,512]{2,3,0,1:T(8,128)(2,1)S(1)} collective-permute-done((bf16[2,2,128,512]{2,3,0,1:T(8,128)(2,1)S(1)}, bf16[2,2,128,512]{2,3,0,1:T(8,128)(2,1)S(1)}, u32[]{:S(2)}, u32[]{:S(2)}) %collective-permute-start.60) | collective-permute-done | bytes 524320 | tf_op jit(solution)/shard_map/ppermute | solution.py:191
  281.4 1.3 collective-permute-start.47
  282.9 2.2 collective-permute-start.61
  285.1 10.0 %shard_map.121 = bf16[768,2048]{1,0:T(8,128)(2,1)} custom-call(bf16[896,768]{1,0:T(8,128)(2,1)S(1)} %bitcast.219, bf16[896,768]{1,0:T(8,128)(2,1)S(1)} %bitcast.221, bf16[896,768]{1,0:T(8,128)(2,1)S(1)} %bitcast.223, bf16[896,768]{1,0:T(8,128)(2,1)S(1)} %bitcast.225, bf16[896,512]{1,0:T(8,128)(2,1)S(1)} %bitcast.228, bf16[896,512]{1,0:T(8,128)(2,1)S(1)} %bitcast.230, ...), custom_call_target="tpu_custom_call" | custom-call | flops 5637144576 | bytes 14680064 | tf_op jit(solution)/shard_map/pallas_call | solution.py:585
  297.1 1.5 collective-permute-start.59
  298.6 6.4 %collective-permute-done.52 = bf16[128,896]{0,1:T(8,128)(2,1)S(1)} collective-permute-done((bf16[128,896]{0,1:T(8,128)(2,1)S(1)}, bf16[128,896]{0,1:T(8,128)(2,1)S(1)}, u32[]{:S(2)}, u32[]{:S(2)}) %collective-permute-start.52) | collective-permute-done | bytes 229408 | tf_op jit(solution)/shard_map/ppermute | solution.py:191
  305.1 2.9 collective-permute-start.53
  308.1 1.5 collective-permute-done.59
  309.8 2.5 collective-permute-start.63
  313.6 1.5 collective-permute-start.65
  315.8 7.0 %collective-permute-done.48 = bf16[2,128,896]{1,2,0:T(8,128)(2,1)S(1)} collective-permute-done((bf16[2,128,896]{1,2,0:T(8,128)(2,1)S(1)}, bf16[2,128,896]{1,2,0:T(8,128)(2,1)S(1)}, u32[]{:S(2)}, u32[]{:S(2)}) %collective-permute-start.48) | collective-permute-done | bytes 458784 | tf_op jit(solution)/shard_map/ppermute | solution.py:183
  323.5 5.7 %collective-permute-done.54 = bf16[128,896]{0,1:T(8,128)(2,1)S(1)} collective-permute-done((bf16[128,896]{0,1:T(8,128)(2,1)S(1)}, bf16[128,896]{0,1:T(8,128)(2,1)S(1)}, u32[]{:S(2)}, u32[]{:S(2)}) %collective-permute-start.54) | collective-permute-done | bytes 229408 | tf_op jit(solution)/shard_map/ppermute | solution.py:191
  (217 shorter events, 36.9 us)
Async XLA Ops:
  4.4 14.9 %collective-permute-start = (bf16[128,896]{1,0:T(8,128)(2,1)S(1)}, bf16[128,896]{1,0:T(8,128)(2,1)S(1)}, u32[]{:S(2)}, u32[]{:S(2)}) collective-permute-start(bf16[128,896]{1,0:T(8,128)(2,1)S(1)} %maximum_maximum_fusion), channel_id=1, source_target_pairs={{0,2},{1,3},{2,4},{3,5},{4,6},{5,7},{6,0},{7,1},{8,10},{9,11},{10,... | collective-permute-start | bytes 688136 | tf_op jit(solution)/shard_map/ppermute | solution.py:186
  9.9 9.4 %collective-permute-start.8 = (bf16[128,768]{1,0:T(8,128)(2,1)}, bf16[128,768]{1,0:T(8,128)(2,1)S(1)}, u32[]{:S(2)}, u32[]{:S(2)}) collective-permute-start(bf16[128,768]{1,0:T(8,128)(2,1)} %get-tuple-element.198), channel_id=1, source_target_pairs={{0,2},{1,3},{2,4},{3,5},{4,6},{5,7},{6,0},{7,1},{8,10},{9,11},{10,... | collective-permute-start | bytes 589832 | tf_op jit(solution)/shard_map/ppermute | solution.py:186
  13.4 15.5 %collective-permute-start.14 = (bf16[2,128,512]{2,1,0:T(8,128)(2,1)S(1)}, bf16[2,128,512]{2,1,0:T(8,128)(2,1)S(1)}, u32[]{:S(2)}, u32[]{:S(2)}) collective-permute-start(bf16[2,128,512]{2,1,0:T(8,128)(2,1)S(1)} %pad_maximum_fusion.22), channel_id=1, source_target_pairs={{0,1},{1,0},{2,3},{3,2},{4,5},{5,4},{6,7},{7,6},{8,9},{9,8},{10,11... | collective-permute-start | bytes 786440 | tf_op jit(solution)/shard_map/ppermute | solution.py:183
  19.3 9.6 %collective-permute-start.9 = (bf16[128,768]{1,0:T(8,128)(2,1)S(1)}, bf16[128,768]{1,0:T(8,128)(2,1)S(1)}, u32[]{:S(2)}, u32[]{:S(2)}) collective-permute-start(bf16[128,768]{1,0:T(8,128)(2,1)S(1)} %collective-permute-done.8), channel_id=1, source_target_pairs={{0,2},{1,3},{2,4},{3,5},{4,6},{5,7},{6,0},{7,1},{8,10},{9,11},{10,... | collective-permute-start | bytes 589832 | tf_op jit(solution)/shard_map/ppermute | solution.py:186
  19.3 14.5 %collective-permute-start.1 = (bf16[2,128,896]{2,1,0:T(8,128)(2,1)S(1)}, bf16[2,128,896]{2,1,0:T(8,128)(2,1)S(1)}, u32[]{:S(2)}, u32[]{:S(2)}) collective-permute-start(bf16[2,128,896]{2,1,0:T(8,128)(2,1)S(1)} %pad_maximum_fusion.14), channel_id=1, source_target_pairs={{0,1},{1,0},{2,3},{3,2},{4,5},{5,4},{6,7},{7,6},{8,9},{9,8},{10,11... | collective-permute-start | bytes 1376264 | tf_op jit(solution)/shard_map/ppermute | solution.py:183
  21.0 17.1 %collective-permute-start.12 = (bf16[2,128,768]{2,1,0:T(8,128)(2,1)S(1)}, bf16[2,128,768]{2,1,0:T(8,128)(2,1)S(1)}, u32[]{:S(2)}, u32[]{:S(2)}) collective-permute-start(bf16[2,128,768]{2,1,0:T(8,128)(2,1)S(1)} %pad_maximum_fusion.18), channel_id=1, source_target_pairs={{0,16},{8,24},{16,0},{24,8},{1,17},{9,25},{17,1},{25,9},{2,18},{10... | collective-permute-start | bytes 1179656 | tf_op jit(solution)/shard_map/ppermute | solution.py:180
  22.5 11.3 %collective-permute-start.4 = (bf16[128,896]{1,0:T(8,128)(2,1)S(1)}, bf16[128,896]{1,0:T(8,128)(2,1)S(1)}, u32[]{:S(2)}, u32[]{:S(2)}) collective-permute-start(bf16[128,896]{1,0:T(8,128)(2,1)S(1)} %collective-permute-done), channel_id=1, source_target_pairs={{0,2},{1,3},{2,4},{3,5},{4,6},{5,7},{6,0},{7,1},{8,10},{9,11},{10,... | collective-permute-start | bytes 688136 | tf_op jit(solution)/shard_map/ppermute | solution.py:186
  28.9 9.1 %collective-permute-start.10 = (bf16[128,768]{1,0:T(8,128)(2,1)S(1)}, bf16[128,768]{1,0:T(8,128)(2,1)S(1)}, u32[]{:S(2)}, u32[]{:S(2)}) collective-permute-start(bf16[128,768]{1,0:T(8,128)(2,1)S(1)} %collective-permute-done.9), channel_id=1, source_target_pairs={{0,2},{1,3},{2,4},{3,5},{4,6},{5,7},{6,0},{7,1},{8,10},{9,11},{10,... | collective-permute-start | bytes 589832 | tf_op jit(solution)/shard_map/ppermute | solution.py:186
  33.8 9.9 %collective-permute-start.5 = (bf16[128,896]{1,0:T(8,128)(2,1)S(1)}, bf16[128,896]{1,0:T(8,128)(2,1)S(1)}, u32[]{:S(2)}, u32[]{:S(2)}) collective-permute-start(bf16[128,896]{1,0:T(8,128)(2,1)S(1)} %collective-permute-done.4), channel_id=1, source_target_pairs={{0,2},{1,3},{2,4},{3,5},{4,6},{5,7},{6,0},{7,1},{8,10},{9,11},{10,... | collective-permute-start | bytes 688136 | tf_op jit(solution)/shard_map/ppermute | solution.py:186
  34.0 35.1 %collective-permute-start.3 = (bf16[4,128,896]{2,1,0:T(8,128)(2,1)S(1)}, bf16[4,128,896]{2,1,0:T(8,128)(2,1)S(1)}, u32[]{:S(2)}, u32[]{:S(2)}) collective-permute-start(bf16[4,128,896]{2,1,0:T(8,128)(2,1)S(1)} %pad_maximum_fusion.refs_0_), channel_id=1, source_target_pairs={{0,16},{8,24},{16,0},{24,8},{1,17},{9,25},{17,1},{25,9},{2,18},{10... | collective-permute-start | bytes 2752520 | tf_op jit(solution)/shard_map/ppermute | solution.py:180
  38.1 24.7 %collective-permute-start.13 = (bf16[2,128,768]{2,1,0:T(8,128)(2,1)S(1)}, bf16[2,128,768]{2,1,0:T(8,128)(2,1)S(1)}, u32[]{:S(2)}, u32[]{:S(2)}) collective-permute-start(bf16[2,128,768]{2,1,0:T(8,128)(2,1)S(1)} %pad_maximum_fusion.17), channel_id=1, source_target_pairs={{0,16},{8,24},{16,0},{24,8},{1,17},{9,25},{17,1},{25,9},{2,18},{10... | collective-permute-start | bytes 1179656 | tf_op jit(solution)/shard_map/ppermute | solution.py:180
  40.0 9.6 %collective-permute-start.11 = (bf16[128,768]{1,0:T(8,128)(2,1)S(1)}, bf16[128,768]{1,0:T(8,128)(2,1)S(1)}, u32[]{:S(2)}, u32[]{:S(2)}) collective-permute-start(bf16[128,768]{1,0:T(8,128)(2,1)S(1)} %get-tuple-element.99), channel_id=1, source_target_pairs={{0,2},{1,3},{2,4},{3,5},{4,6},{5,7},{6,0},{7,1},{8,10},{9,11},{10,... | collective-permute-start | bytes 589832 | tf_op jit(solution)/shard_map/ppermute | solution.py:186
  43.7 20.0 %collective-permute-start.20 = (bf16[4,128,512]{2,1,0:T(8,128)(2,1)S(1)}, bf16[4,128,512]{2,1,0:T(8,128)(2,1)S(1)}, u32[]{:S(2)}, u32[]{:S(2)}) collective-permute-start(bf16[4,128,512]{2,1,0:T(8,128)(2,1)S(1)} %pad_maximum_fusion.10.refs_0_), channel_id=1, source_target_pairs={{0,2},{1,3},{2,4},{3,5},{4,6},{5,7},{6,0},{7,1},{8,10},{9,11},{10,... | collective-permute-start | bytes 1572872 | tf_op jit(solution)/shard_map/ppermute | solution.py:186
  43.8 29.2 %collective-permute-start.15 = (bf16[4,128,768]{2,1,0:T(8,128)(2,1)S(1)}, bf16[4,128,768]{2,1,0:T(8,128)(2,1)S(1)}, u32[]{:S(2)}, u32[]{:S(2)}) collective-permute-start(bf16[4,128,768]{2,1,0:T(8,128)(2,1)S(1)} %pad_maximum_fusion.4.refs_0_), channel_id=1, source_target_pairs={{0,1},{1,0},{2,3},{3,2},{4,5},{5,4},{6,7},{7,6},{8,9},{9,8},{10,11... | collective-permute-start | bytes 2359304 | tf_op jit(solution)/shard_map/ppermute | solution.py:183
  49.7 19.2 %collective-permute-start.6 = (bf16[2,128,896]{2,1,0:T(8,128)(2,1)S(1)}, bf16[2,128,896]{2,1,0:T(8,128)(2,1)S(1)}, u32[]{:S(2)}, u32[]{:S(2)}) collective-permute-start(bf16[2,128,896]{2,1,0:T(8,128)(2,1)S(1)} %pad_maximum_fusion.15), channel_id=1, source_target_pairs={{0,1},{1,0},{2,3},{3,2},{4,5},{5,4},{6,7},{7,6},{8,9},{9,8},{10,11... | collective-permute-start | bytes 1376264 | tf_op jit(solution)/shard_map/ppermute | solution.py:183
  62.7 8.9 %collective-permute-start.18 = (bf16[1,128,512]{2,1,0:T(8,128)(2,1)S(1)}, bf16[1,128,512]{2,1,0:T(8,128)(2,1)S(1)}, u32[]{:S(2)}, u32[]{:S(2)}) collective-permute-start(bf16[1,128,512]{2,1,0:T(8,128)(2,1)S(1)} %slice_bitcast_fusion.20), channel_id=1, source_target_pairs={{0,16},{8,24},{16,0},{24,8},{1,17},{9,25},{17,1},{25,9},{2,18},{10... | collective-permute-start | bytes 393224 | tf_op jit(solution)/shard_map/ppermute | solution.py:180
  63.7 25.1 %collective-permute-start.23 = (bf16[4,128,512]{2,1,0:T(8,128)(2,1)S(1)}, bf16[4,128,512]{2,1,0:T(8,128)(2,1)S(1)}, u32[]{:S(2)}, u32[]{:S(2)}) collective-permute-start(bf16[4,128,512]{2,1,0:T(8,128)(2,1)S(1)} %collective-permute-done.20.refs_1_), channel_id=1, source_target_pairs={{0,2},{1,3},{2,4},{3,5},{4,6},{5,7},{6,0},{7,1},{8,10},{9,11},{10,... | collective-permute-start | bytes 1572872 | tf_op jit(solution)/shard_map/ppermute | solution.py:186
  68.9 10.3 %collective-permute-start.21 = (bf16[128,768]{1,0:T(8,128)(2,1)S(1)}, bf16[128,768]{1,0:T(8,128)(2,1)S(1)}, u32[]{:S(2)}, u32[]{:S(2)}) collective-permute-start(bf16[128,768]{1,0:T(8,128)(2,1)S(1)} %get-tuple-element.107), channel_id=1, source_target_pairs={{0,2},{1,3},{2,4},{3,5},{4,6},{5,7},{6,0},{7,1},{8,10},{9,11},{10,... | collective-permute-start | bytes 589832 | tf_op jit(solution)/shard_map/ppermute | solution.py:186
  69.1 37.1 %collective-permute-start.7 = (bf16[4,128,896]{2,1,0:T(8,128)(2,1)S(1)}, bf16[4,128,896]{2,1,0:T(8,128)(2,1)S(1)}, u32[]{:S(2)}, u32[]{:S(2)}) collective-permute-start(bf16[4,128,896]{2,1,0:T(8,128)(2,1)S(1)} %pad_maximum_fusion.1.refs_2_), channel_id=1, source_target_pairs={{0,16},{8,24},{16,0},{24,8},{1,17},{9,25},{17,1},{25,9},{2,18},{10... | collective-permute-start | bytes 2752520 | tf_op jit(solution)/shard_map/ppermute | solution.py:180
  71.6 38.0 %collective-permute-start.30 = (bf16[2,128,512]{2,1,0:T(8,128)(2,1)S(1)}, bf16[2,128,512]{2,1,0:T(8,128)(2,1)S(1)}, u32[]{:S(2)}, u32[]{:S(2)}) collective-permute-start(bf16[2,128,512]{2,1,0:T(8,128)(2,1)S(1)} %pad_maximum_fusion.23), channel_id=1, source_target_pairs={{0,1},{1,0},{2,3},{3,2},{4,5},{5,4},{6,7},{7,6},{8,9},{9,8},{10,11... | collective-permute-start | bytes 786440 | tf_op jit(solution)/shard_map/ppermute | solution.py:183
  73.0 35.0 %collective-permute-start.16 = (bf16[4,128,768]{2,1,0:T(8,128)(2,1)S(1)}, bf16[4,128,768]{2,1,0:T(8,128)(2,1)S(1)}, u32[]{:S(2)}, u32[]{:S(2)}) collective-permute-start(bf16[4,128,768]{2,1,0:T(8,128)(2,1)S(1)} %pad_maximum_fusion.3.refs_2_), channel_id=1, source_target_pairs={{0,1},{1,0},{2,3},{3,2},{4,5},{5,4},{6,7},{7,6},{8,9},{9,8},{10,11... | collective-permute-start | bytes 2359304 | tf_op jit(solution)/shard_map/ppermute | solution.py:183
  79.2 9.6 %collective-permute-start.22 = (bf16[128,768]{1,0:T(8,128)(2,1)S(1)}, bf16[128,768]{1,0:T(8,128)(2,1)S(1)}, u32[]{:S(2)}, u32[]{:S(2)}) collective-permute-start(bf16[128,768]{1,0:T(8,128)(2,1)S(1)} %collective-permute-done.11), channel_id=1, source_target_pairs={{0,2},{1,3},{2,4},{3,5},{4,6},{5,7},{6,0},{7,1},{8,10},{9,11},{10,... | collective-permute-start | bytes 589832 | tf_op jit(solution)/shard_map/ppermute | solution.py:186
  88.8 17.3 %collective-permute-start.32 = (bf16[4,128,512]{2,1,0:T(8,128)(2,1)S(1)}, bf16[4,128,512]{2,1,0:T(8,128)(2,1)S(1)}, u32[]{:S(2)}, u32[]{:S(2)}) collective-permute-start(bf16[4,128,512]{2,1,0:T(8,128)(2,1)S(1)} %collective-permute-done.23.refs_2_), channel_id=1, source_target_pairs={{0,2},{1,3},{2,4},{3,5},{4,6},{5,7},{6,0},{7,1},{8,10},{9,11},{10,... | collective-permute-start | bytes 1572872 | tf_op jit(solution)/shard_map/ppermute | solution.py:186
  88.9 17.3 %collective-permute-start.24 = (bf16[128,768]{1,0:T(8,128)(2,1)S(1)}, bf16[128,768]{1,0:T(8,128)(2,1)S(1)}, u32[]{:S(2)}, u32[]{:S(2)}) collective-permute-start(bf16[128,768]{1,0:T(8,128)(2,1)S(1)} %collective-permute-done.21), channel_id=1, source_target_pairs={{0,2},{1,3},{2,4},{3,5},{4,6},{5,7},{6,0},{7,1},{8,10},{9,11},{10,... | collective-permute-start | bytes 589832 | tf_op jit(solution)/shard_map/ppermute | solution.py:186
  106.1 7.5 %collective-permute-start.25 = (bf16[128,768]{1,0:T(8,128)(2,1)S(1)}, bf16[128,768]{1,0:T(8,128)(2,1)S(1)}, u32[]{:S(2)}, u32[]{:S(2)}) collective-permute-start(bf16[128,768]{1,0:T(8,128)(2,1)S(1)} %collective-permute-done.22), channel_id=1, source_target_pairs={{0,2},{1,3},{2,4},{3,5},{4,6},{5,7},{6,0},{7,1},{8,10},{9,11},{10,... | collective-permute-start | bytes 589832 | tf_op jit(solution)/shard_map/ppermute | solution.py:186
  106.1 10.0 %collective-permute-start.33 = (bf16[128,768]{1,0:T(8,128)(2,1)S(1)}, bf16[128,768]{1,0:T(8,128)(2,1)S(1)}, u32[]{:S(2)}, u32[]{:S(2)}) collective-permute-start(bf16[128,768]{1,0:T(8,128)(2,1)S(1)} %collective-permute-done.24), channel_id=1, source_target_pairs={{0,2},{1,3},{2,4},{3,5},{4,6},{5,7},{6,0},{7,1},{8,10},{9,11},{10,... | collective-permute-start | bytes 589832 | tf_op jit(solution)/shard_map/ppermute | solution.py:186
  107.9 45.1 %collective-permute-start.39 = (bf16[16,56,896]{2,1,0:T(8,128)(2,1)S(1)}, bf16[16,56,896]{2,1,0:T(8,128)(2,1)S(1)}, u32[]{:S(2)}, u32[]{:S(2)}) collective-permute-start(bf16[16,56,896]{2,1,0:T(8,128)(2,1)S(1)} %get-tuple-element.128), channel_id=1, source_target_pairs={{0,8},{8,0},{16,24},{24,16},{1,9},{9,1},{17,25},{25,17},{2,10},{10... | collective-permute-start | bytes 4816904 | tf_op jit(solution)/shard_map/ppermute | solution.py:177
  108.1 11.6 %collective-permute-start.17 = (bf16[2,128,768]{2,1,0:T(8,128)(2,1)S(1)}, bf16[2,128,768]{2,1,0:T(8,128)(2,1)S(1)}, u32[]{:S(2)}, u32[]{:S(2)}) collective-permute-start(bf16[2,128,768]{2,1,0:T(8,128)(2,1)S(1)} %pad_maximum_fusion.16), channel_id=1, source_target_pairs={{0,1},{1,0},{2,3},{3,2},{4,5},{5,4},{6,7},{7,6},{8,9},{9,8},{10,11... | collective-permute-start | bytes 1179656 | tf_op jit(solution)/shard_map/ppermute | solution.py:183
  109.7 11.5 %collective-permute-start.29 = (bf16[2,128,768]{2,1,0:T(8,128)(2,1)S(1)}, bf16[2,128,768]{2,1,0:T(8,128)(2,1)S(1)}, u32[]{:S(2)}, u32[]{:S(2)}) collective-permute-start(bf16[2,128,768]{2,1,0:T(8,128)(2,1)S(1)} %pad_maximum_fusion.20), channel_id=1, source_target_pairs={{0,16},{8,24},{16,0},{24,8},{1,17},{9,25},{17,1},{25,9},{2,18},{10... | collective-permute-start | bytes 1179656 | tf_op jit(solution)/shard_map/ppermute | solution.py:180
  113.6 13.3 %collective-permute-start.37 = (bf16[4,128,512]{2,1,0:T(8,128)(2,1)S(1)}, bf16[4,128,512]{2,1,0:T(8,128)(2,1)S(1)}, u32[]{:S(2)}, u32[]{:S(2)}) collective-permute-start(bf16[4,128,512]{2,1,0:T(8,128)(2,1)S(1)} %pad_maximum_fusion.11.refs_0_), channel_id=1, source_target_pairs={{0,2},{1,3},{2,4},{3,5},{4,6},{5,7},{6,0},{7,1},{8,10},{9,11},{10,... | collective-permute-start | bytes 1572872 | tf_op jit(solution)/shard_map/ppermute | solution.py:186
  116.2 35.8 %collective-permute-start.40 = (bf16[16,56,768]{2,1,0:T(8,128)(2,1)S(1)}, bf16[16,56,768]{2,1,0:T(8,128)(2,1)S(1)}, u32[]{:S(2)}, u32[]{:S(2)}) collective-permute-start(bf16[16,56,768]{2,1,0:T(8,128)(2,1)S(1)} %get-tuple-element.130), channel_id=1, source_target_pairs={{0,8},{8,0},{16,24},{24,16},{1,9},{9,1},{17,25},{25,17},{2,10},{10... | collective-permute-start | bytes 4128776 | tf_op jit(solution)/shard_map/ppermute | solution.py:177
  119.6 10.7 %collective-permute-start.26 = (bf16[2,128,768]{2,1,0:T(8,128)(2,1)S(1)}, bf16[2,128,768]{2,1,0:T(8,128)(2,1)S(1)}, u32[]{:S(2)}, u32[]{:S(2)}) collective-permute-start(bf16[2,128,768]{2,1,0:T(8,128)(2,1)S(1)} %pad_maximum_fusion.19), channel_id=1, source_target_pairs={{0,1},{1,0},{2,3},{3,2},{4,5},{5,4},{6,7},{7,6},{8,9},{9,8},{10,11... | collective-permute-start | bytes 1179656 | tf_op jit(solution)/shard_map/ppermute | solution.py:183
  121.2 10.7 %collective-permute-start.34 = (bf16[2,128,768]{2,1,0:T(8,128)(2,1)S(1)}, bf16[2,128,768]{2,1,0:T(8,128)(2,1)S(1)}, u32[]{:S(2)}, u32[]{:S(2)}) collective-permute-start(bf16[2,128,768]{2,1,0:T(8,128)(2,1)S(1)} %pad_maximum_fusion.21), channel_id=1, source_target_pairs={{0,16},{8,24},{16,0},{24,8},{1,17},{9,25},{17,1},{25,9},{2,18},{10... | collective-permute-start | bytes 1179656 | tf_op jit(solution)/shard_map/ppermute | solution.py:180
  126.9 23.9 %collective-permute-start.41 = (bf16[16,56,512]{2,1,0:T(8,128)(2,1)S(1)}, bf16[16,56,512]{2,1,0:T(8,128)(2,1)S(1)}, u32[]{:S(2)}, u32[]{:S(2)}) collective-permute-start(bf16[16,56,512]{2,1,0:T(8,128)(2,1)S(1)} %get-tuple-element.132), channel_id=1, source_target_pairs={{0,8},{8,0},{16,24},{24,16},{1,9},{9,1},{17,25},{25,17},{2,10},{10... | collective-permute-start | bytes 2752520 | tf_op jit(solution)/shard_map/ppermute | solution.py:177
  130.4 18.3 %collective-permute-start.19 = (bf16[4,128,768]{2,1,0:T(8,128)(2,1)S(1)}, bf16[4,128,768]{2,1,0:T(8,128)(2,1)S(1)}, u32[]{:S(2)}, u32[]{:S(2)}) collective-permute-start(bf16[4,128,768]{2,1,0:T(8,128)(2,1)S(1)} %pad_maximum_fusion.5.refs_0_), channel_id=1, source_target_pairs={{0,16},{8,24},{16,0},{24,8},{1,17},{9,25},{17,1},{25,9},{2,18},{10... | collective-permute-start | bytes 2359304 | tf_op jit(solution)/shard_map/ppermute | solution.py:180
  131.9 18.0 %collective-permute-start.31 = (bf16[4,128,768]{2,1,0:T(8,128)(2,1)S(1)}, bf16[4,128,768]{2,1,0:T(8,128)(2,1)S(1)}, u32[]{:S(2)}, u32[]{:S(2)}) collective-permute-start(bf16[4,128,768]{2,1,0:T(8,128)(2,1)S(1)} %pad_maximum_fusion.7.refs_0_), channel_id=1, source_target_pairs={{0,1},{1,0},{2,3},{3,2},{4,5},{5,4},{6,7},{7,6},{8,9},{9,8},{10,11... | collective-permute-start | bytes 2359304 | tf_op jit(solution)/shard_map/ppermute | solution.py:183
  148.6 26.6 %collective-permute-start.38 = (bf16[4,128,512]{2,1,0:T(8,128)(2,1)S(1)}, bf16[4,128,512]{2,1,0:T(8,128)(2,1)S(1)}, u32[]{:S(2)}, u32[]{:S(2)}) collective-permute-start(bf16[4,128,512]{2,1,0:T(8,128)(2,1)S(1)} %collective-permute-done.37.refs_1_), channel_id=1, source_target_pairs={{0,2},{1,3},{2,4},{3,5},{4,6},{5,7},{6,0},{7,1},{8,10},{9,11},{10,... | collective-permute-start | bytes 1572872 | tf_op jit(solution)/shard_map/ppermute | solution.py:186
  149.9 29.4 %collective-permute-start.27 = (bf16[4,128,768]{2,1,0:T(8,128)(2,1)S(1)}, bf16[4,128,768]{2,1,0:T(8,128)(2,1)S(1)}, u32[]{:S(2)}, u32[]{:S(2)}) collective-permute-start(bf16[4,128,768]{2,1,0:T(8,128)(2,1)S(1)} %pad_maximum_fusion.6.refs_2_), channel_id=1, source_target_pairs={{0,16},{8,24},{16,0},{24,8},{1,17},{9,25},{17,1},{25,9},{2,18},{10... | collective-permute-start | bytes 2359304 | tf_op jit(solution)/shard_map/ppermute | solution.py:180
  150.8 30.4 %collective-permute-start.35 = (bf16[4,128,768]{2,1,0:T(8,128)(2,1)S(1)}, bf16[4,128,768]{2,1,0:T(8,128)(2,1)S(1)}, u32[]{:S(2)}, u32[]{:S(2)}) collective-permute-start(bf16[4,128,768]{2,1,0:T(8,128)(2,1)S(1)} %pad_maximum_fusion.8.refs_2_), channel_id=1, source_target_pairs={{0,1},{1,0},{2,3},{3,2},{4,5},{5,4},{6,7},{7,6},{8,9},{9,8},{10,11... | collective-permute-start | bytes 2359304 | tf_op jit(solution)/shard_map/ppermute | solution.py:183
  175.3 13.0 %collective-permute-start.42 = (bf16[4,128,512]{2,1,0:T(8,128)(2,1)S(1)}, bf16[4,128,512]{2,1,0:T(8,128)(2,1)S(1)}, u32[]{:S(2)}, u32[]{:S(2)}) collective-permute-start(bf16[4,128,512]{2,1,0:T(8,128)(2,1)S(1)} %collective-permute-done.38.refs_2_), channel_id=1, source_target_pairs={{0,2},{1,3},{2,4},{3,5},{4,6},{5,7},{6,0},{7,1},{8,10},{9,11},{10,... | collective-permute-start | bytes 1572872 | tf_op jit(solution)/shard_map/ppermute | solution.py:186
  181.2 7.7 %collective-permute-start.28 = (bf16[16,56,768]{2,1,0:T(8,128)(2,1)S(1)}, bf16[16,56,768]{2,1,0:T(8,128)(2,1)S(1)}, u32[]{:S(2)}, u32[]{:S(2)}) collective-permute-start(bf16[16,56,768]{2,1,0:T(8,128)(2,1)S(1)} %get-tuple-element.115), channel_id=1, source_target_pairs={{0,8},{8,0},{16,24},{24,16},{1,9},{9,1},{17,25},{25,17},{2,10},{10... | collective-permute-start | bytes 4128776 | tf_op jit(solution)/shard_map/ppermute | solution.py:177
  183.2 8.2 %collective-permute-start.36 = (bf16[16,56,768]{2,1,0:T(8,128)(2,1)S(1)}, bf16[16,56,768]{2,1,0:T(8,128)(2,1)S(1)}, u32[]{:S(2)}, u32[]{:S(2)}) collective-permute-start(bf16[16,56,768]{2,1,0:T(8,128)(2,1)S(1)} %get-tuple-element.124), channel_id=1, source_target_pairs={{0,8},{8,0},{16,24},{24,16},{1,9},{9,1},{17,25},{25,17},{2,10},{10... | collective-permute-start | bytes 4128776 | tf_op jit(solution)/shard_map/ppermute | solution.py:177
  212.1 14.6 %collective-permute-start.49 = (bf16[896,512]{1,0:T(8,128)(2,1)}, bf16[896,512]{1,0:T(8,128)(2,1)}, u32[]{:S(2)}, u32[]{:S(2)}) collective-permute-start(bf16[896,512]{1,0:T(8,128)(2,1)} %get-tuple-element.155), channel_id=1, source_target_pairs={{0,8},{8,0},{16,24},{24,16},{1,9},{9,1},{17,25},{25,17},{2,10},{10... | collective-permute-start | bytes 2752520 | tf_op jit(solution)/shard_map/ppermute | solution.py:177
  219.1 11.5 %collective-permute-start.55 = (bf16[896,768]{1,0:T(8,128)(2,1)S(1)}, bf16[896,768]{1,0:T(8,128)(2,1)S(1)}, u32[]{:S(2)}, u32[]{:S(2)}) collective-permute-start(bf16[896,768]{1,0:T(8,128)(2,1)S(1)} %get-tuple-element.160), channel_id=1, source_target_pairs={{0,8},{8,0},{16,24},{24,16},{1,9},{9,1},{17,25},{25,17},{2,10},{10... | collective-permute-start | bytes 4128776 | tf_op jit(solution)/shard_map/ppermute | solution.py:177
  226.3 20.9 %collective-permute-start.44 = (bf16[896,896]{1,0:T(8,128)(2,1)S(1)}, bf16[896,896]{1,0:T(8,128)(2,1)S(1)}, u32[]{:S(2)}, u32[]{:S(2)}) collective-permute-start(bf16[896,896]{1,0:T(8,128)(2,1)S(1)} %get-tuple-element.151), channel_id=1, source_target_pairs={{0,8},{8,0},{16,24},{24,16},{1,9},{9,1},{17,25},{25,17},{2,10},{10... | collective-permute-start | bytes 4816904 | tf_op jit(solution)/shard_map/ppermute | solution.py:177
  228.5 14.4 %collective-permute-start.50 = (bf16[2,2,128,512]{2,3,0,1:T(8,128)(2,1)S(1)}, bf16[2,2,128,512]{2,3,0,1:T(8,128)(2,1)S(1)}, u32[]{:S(2)}, u32[]{:S(2)}) collective-permute-start(bf16[2,2,128,512]{2,3,0,1:T(8,128)(2,1)S(1)} %convolution_convert_fusion.4), channel_id=1, source_target_pairs={{0,6},{1,7},{2,0},{3,1},{4,2},{5,3},{6,4},{7,5},{8,14},{9,15},{10,... | collective-permute-start | bytes 1572872 | tf_op jit(solution)/shard_map/ppermute | solution.py:191
  231.0 36.0 %collective-permute-start.56 = (bf16[2,2,128,768]{2,3,1,0:T(8,128)(2,1)S(1)}, bf16[2,2,128,768]{2,3,1,0:T(8,128)(2,1)S(1)}, u32[]{:S(2)}, u32[]{:S(2)}) collective-permute-start(bf16[2,2,128,768]{2,3,1,0:T(8,128)(2,1)S(1)} %convolution_convert_fusion.2), channel_id=1, source_target_pairs={{0,1},{1,0},{2,3},{3,2},{4,5},{5,4},{6,7},{7,6},{8,9},{9,8},{10,11... | collective-permute-start | bytes 2359304 | tf_op jit(solution)/shard_map/ppermute | solution.py:183
  243.3 22.8 %collective-permute-start.51 = (bf16[2,2,128,512]{2,3,0,1:T(8,128)(2,1)S(1)}, bf16[2,2,128,512]{2,3,0,1:T(8,128)(2,1)S(1)}, u32[]{:S(2)}, u32[]{:S(2)}) collective-permute-start(bf16[2,2,128,512]{2,3,0,1:T(8,128)(2,1)S(1)} %add_convert_fusion.6), channel_id=1, source_target_pairs={{0,6},{1,7},{2,0},{3,1},{4,2},{5,3},{6,4},{7,5},{8,14},{9,15},{10,... | collective-permute-start | bytes 1572872 | tf_op jit(solution)/shard_map/ppermute | solution.py:191
  247.7 32.3 %collective-permute-start.45 = (bf16[2,2,128,896]{2,3,1,0:T(8,128)(2,1)S(1)}, bf16[2,2,128,896]{2,3,1,0:T(8,128)(2,1)S(1)}, u32[]{:S(2)}, u32[]{:S(2)}) collective-permute-start(bf16[2,2,128,896]{2,3,1,0:T(8,128)(2,1)S(1)} %convolution_convert_fusion), channel_id=1, source_target_pairs={{0,16},{8,24},{16,0},{24,8},{1,17},{9,25},{17,1},{25,9},{2,18},{10... | collective-permute-start | bytes 2752520 | tf_op jit(solution)/shard_map/ppermute | solution.py:180
  266.4 13.1 %collective-permute-start.60 = (bf16[2,2,128,512]{2,3,0,1:T(8,128)(2,1)S(1)}, bf16[2,2,128,512]{2,3,0,1:T(8,128)(2,1)S(1)}, u32[]{:S(2)}, u32[]{:S(2)}) collective-permute-start(bf16[2,2,128,512]{2,3,0,1:T(8,128)(2,1)S(1)} %add_convert_fusion.5), channel_id=1, source_target_pairs={{0,6},{1,7},{2,0},{3,1},{4,2},{5,3},{6,4},{7,5},{8,14},{9,15},{10,... | collective-permute-start | bytes 1572872 | tf_op jit(solution)/shard_map/ppermute | solution.py:191
  267.1 28.7 %collective-permute-start.57 = (bf16[2,2,128,768]{2,3,1,0:T(8,128)(2,1)S(1)}, bf16[2,2,128,768]{2,3,1,0:T(8,128)(2,1)S(1)}, u32[]{:S(2)}, u32[]{:S(2)}) collective-permute-start(bf16[2,2,128,768]{2,3,1,0:T(8,128)(2,1)S(1)} %convolution_convert_fusion.3), channel_id=1, source_target_pairs={{0,1},{1,0},{2,3},{3,2},{4,5},{5,4},{6,7},{7,6},{8,9},{9,8},{10,11... | collective-permute-start | bytes 2359304 | tf_op jit(solution)/shard_map/ppermute | solution.py:183
  268.2 14.6 %collective-permute-start.58 = (bf16[2,128,768]{1,2,0:T(8,128)(2,1)S(1)}, bf16[2,128,768]{1,2,0:T(8,128)(2,1)S(1)}, u32[]{:S(2)}, u32[]{:S(2)}) collective-permute-start(bf16[2,128,768]{1,2,0:T(8,128)(2,1)S(1)} %slice_bitcast_fusion.5), channel_id=1, source_target_pairs={{0,16},{8,24},{16,0},{24,8},{1,17},{9,25},{17,1},{25,9},{2,18},{10... | collective-permute-start | bytes 1179656 | tf_op jit(solution)/shard_map/ppermute | solution.py:180
  280.5 31.8 %collective-permute-start.46 = (bf16[2,2,128,896]{2,3,1,0:T(8,128)(2,1)S(1)}, bf16[2,2,128,896]{2,3,1,0:T(8,128)(2,1)S(1)}, u32[]{:S(2)}, u32[]{:S(2)}) collective-permute-start(bf16[2,2,128,896]{2,3,1,0:T(8,128)(2,1)S(1)} %convolution_convert_fusion.1), channel_id=1, source_target_pairs={{0,16},{8,24},{16,0},{24,8},{1,17},{9,25},{17,1},{25,9},{2,18},{10... | collective-permute-start | bytes 2752520 | tf_op jit(solution)/shard_map/ppermute | solution.py:180
  281.4 15.3 %collective-permute-start.47 = (bf16[2,128,896]{1,2,0:T(8,128)(2,1)S(1)}, bf16[2,128,896]{1,2,0:T(8,128)(2,1)S(1)}, u32[]{:S(2)}, u32[]{:S(2)}) collective-permute-start(bf16[2,128,896]{1,2,0:T(8,128)(2,1)S(1)} %slice_bitcast_fusion.1), channel_id=1, source_target_pairs={{0,1},{1,0},{2,3},{3,2},{4,5},{5,4},{6,7},{7,6},{8,9},{9,8},{10,11... | collective-permute-start | bytes 1376264 | tf_op jit(solution)/shard_map/ppermute | solution.py:183
  282.9 12.3 %collective-permute-start.61 = (bf16[128,768]{0,1:T(8,128)(2,1)S(1)}, bf16[128,768]{0,1:T(8,128)(2,1)S(1)}, u32[]{:S(2)}, u32[]{:S(2)}) collective-permute-start(bf16[128,768]{0,1:T(8,128)(2,1)S(1)} %slice_bitcast_fusion.14), channel_id=1, source_target_pairs={{0,6},{1,7},{2,0},{3,1},{4,2},{5,3},{6,4},{7,5},{8,14},{9,15},{10,... | collective-permute-start | bytes 589832 | tf_op jit(solution)/shard_map/ppermute | solution.py:191
  295.2 14.5 %collective-permute-start.62 = (bf16[128,768]{0,1:T(8,128)(2,1)S(1)}, bf16[128,768]{0,1:T(8,128)(2,1)S(1)}, u32[]{:S(2)}, u32[]{:S(2)}) collective-permute-start(bf16[128,768]{0,1:T(8,128)(2,1)S(1)} %fusion.59), channel_id=1, source_target_pairs={{0,6},{1,7},{2,0},{3,1},{4,2},{5,3},{6,4},{7,5},{8,14},{9,15},{10,... | collective-permute-start | bytes 589832 | tf_op jit(solution)/shard_map/ppermute | solution.py:191
  295.7 12.3 %collective-permute-start.64 = (bf16[2,128,512]{1,2,0:T(8,128)(2,1)S(1)}, bf16[2,128,512]{1,2,0:T(8,128)(2,1)S(1)}, u32[]{:S(2)}, u32[]{:S(2)}) collective-permute-start(bf16[2,128,512]{1,2,0:T(8,128)(2,1)S(1)} %slice_bitcast_fusion.8), channel_id=1, source_target_pairs={{0,1},{1,0},{2,3},{3,2},{4,5},{5,4},{6,7},{7,6},{8,9},{9,8},{10,11... | collective-permute-start | bytes 786440 | tf_op jit(solution)/shard_map/ppermute | solution.py:183
  296.9 8.1 %collective-permute-start.52 = (bf16[128,896]{0,1:T(8,128)(2,1)S(1)}, bf16[128,896]{0,1:T(8,128)(2,1)S(1)}, u32[]{:S(2)}, u32[]{:S(2)}) collective-permute-start(bf16[128,896]{0,1:T(8,128)(2,1)S(1)} %slice_bitcast_fusion.10), channel_id=1, source_target_pairs={{0,6},{1,7},{2,0},{3,1},{4,2},{5,3},{6,4},{7,5},{8,14},{9,15},{10,... | collective-permute-start | bytes 688136 | tf_op jit(solution)/shard_map/ppermute | solution.py:191
  297.1 12.5 %collective-permute-start.59 = (bf16[2,128,768]{1,2,0:T(8,128)(2,1)S(1)}, bf16[2,128,768]{1,2,0:T(8,128)(2,1)S(1)}, u32[]{:S(2)}, u32[]{:S(2)}) collective-permute-start(bf16[2,128,768]{1,2,0:T(8,128)(2,1)S(1)} %slice_bitcast_fusion.6), channel_id=1, source_target_pairs={{0,16},{8,24},{16,0},{24,8},{1,17},{9,25},{17,1},{25,9},{2,18},{10... | collective-permute-start | bytes 1179656 | tf_op jit(solution)/shard_map/ppermute | solution.py:180
  305.1 17.9 %collective-permute-start.53 = (bf16[128,896]{0,1:T(8,128)(2,1)S(1)}, bf16[128,896]{0,1:T(8,128)(2,1)S(1)}, u32[]{:S(2)}, u32[]{:S(2)}) collective-permute-start(bf16[128,896]{0,1:T(8,128)(2,1)S(1)} %fusion.43), channel_id=1, source_target_pairs={{0,6},{1,7},{2,0},{3,1},{4,2},{5,3},{6,4},{7,5},{8,14},{9,15},{10,... | collective-permute-start | bytes 688136 | tf_op jit(solution)/shard_map/ppermute | solution.py:191
  309.8 6.0 %collective-permute-start.63 = (bf16[128,768]{0,1:T(8,128)(2,1)S(1)}, bf16[128,768]{0,1:T(8,128)(2,1)S(1)}, u32[]{:S(2)}, u32[]{:S(2)}) collective-permute-start(bf16[128,768]{0,1:T(8,128)(2,1)S(1)} %fusion.60), channel_id=1, source_target_pairs={{0,6},{1,7},{2,0},{3,1},{4,2},{5,3},{6,4},{7,5},{8,14},{9,15},{10,... | collective-permute-start | bytes 589832 | tf_op jit(solution)/shard_map/ppermute | solution.py:191
  312.9 9.9 %collective-permute-start.48 = (bf16[2,128,896]{1,2,0:T(8,128)(2,1)S(1)}, bf16[2,128,896]{1,2,0:T(8,128)(2,1)S(1)}, u32[]{:S(2)}, u32[]{:S(2)}) collective-permute-start(bf16[2,128,896]{1,2,0:T(8,128)(2,1)S(1)} %slice_bitcast_fusion.2), channel_id=1, source_target_pairs={{0,1},{1,0},{2,3},{3,2},{4,5},{5,4},{6,7},{7,6},{8,9},{9,8},{10,11... | collective-permute-start | bytes 1376264 | tf_op jit(solution)/shard_map/ppermute | solution.py:183
  313.6 9.9 %collective-permute-start.65 = (bf16[128,512]{0,1:T(8,128)(2,1)S(1)}, bf16[128,512]{0,1:T(8,128)(2,1)S(1)}, u32[]{:S(2)}, u32[]{:S(2)}) collective-permute-start(bf16[128,512]{0,1:T(8,128)(2,1)S(1)} %slice_bitcast_fusion.18), channel_id=1, source_target_pairs={{0,16},{8,24},{16,0},{24,8},{1,17},{9,25},{17,1},{25,9},{2,18},{10... | collective-permute-start | bytes 393224 | tf_op jit(solution)/shard_map/ppermute | solution.py:180
  323.1 6.1 %collective-permute-start.54 = (bf16[128,896]{0,1:T(8,128)(2,1)S(1)}, bf16[128,896]{0,1:T(8,128)(2,1)S(1)}, u32[]{:S(2)}, u32[]{:S(2)}) collective-permute-start(bf16[128,896]{0,1:T(8,128)(2,1)S(1)} %fusion.44), channel_id=1, source_target_pairs={{0,6},{1,7},{2,0},{3,1},{4,2},{5,3},{6,4},{7,5},{8,14},{9,15},{10,... | collective-permute-start | bytes 688136 | tf_op jit(solution)/shard_map/ppermute | solution.py:191
  (27 other events, 162.9 us)

commit v4 on v3

--- a/solution.py
+++ b/solution.py
@@ -214,32 +214,35 @@
         axis=1,
     )
 
+    t_cuts = (0, model_width // 2, model_width)
+    c_cuts = (0, model_width // 4, model_width // 2, model_width)
     cuts = (0, 3 * model_width // 8, 3 * model_width // 4, model_width)
 
-    def part_of(v, n):
-        return v[:, cuts[n] : cuts[n + 1]]
-
     links = {"x": [], "y": [], "z": []}
+    depth = {"x": 2, "y": 2, "z": 3}
     ways = {"x": swap_x, "y": swap_y, "z": ring_up, "d": ring_down}
 
     def send(way, v):
-        queue = links["z" if way == "d" else way]
-        if len(queue) >= 2:
-            v, _ = lax.optimization_barrier((v, queue[-2]))
+        link = "z" if way == "d" else way
+        queue = links[link]
+        if len(queue) >= depth[link]:
+            v, _ = lax.optimization_barrier((v, queue[-depth[link]]))
         queue.append(ways[way](v))
         return queue[-1]
 
     order = [(g, i, j, s) for g in range(2) for i in range(2) for j in range(2) for s in range(2)]
-    where = [{}, {}, {}]
+    where = [{}, {}, {}, {}, {}]
     for g, i, j, s in order:
         where[0][g, i, j, s] = (2 * g + i, 2 * j + s)
         where[1][g, i, j, s] = (2 * g + j, 2 * i + s)
         where[2][g, i, j, s] = (2 * g + s, 2 * j + i)
+        where[3][g, i, j, s] = (i, 4 * j + 2 * g + s)
+        where[4][g, i, j, s] = (j, 4 * i + 2 * g + s)
 
     def with_other(way, v):
         return jnp.concatenate([v, send(way, v)])
 
-    def compact(blocks, where):
+    def compact(place_both, blocks, where):
         width = blocks[0].shape[-1]
 
         def body(places, *refs):
@@ -258,31 +261,28 @@
             out_specs=(pl.BlockSpec(memory_space=pltpu.VMEM),) * 2,
             compiler_params=pltpu.CompilerParams(vmem_limit_bytes=24 * 2**20),
             cost_estimate=pl.CostEstimate(
-                flops=2 * source_count * 2 * most_rows * tok_local * width,
-                bytes_accessed=12 * 2**20,
-                transcendentals=0,
+                flops=2 * source_count * 2 * most_rows * tok_local * width, bytes_accessed=12 * 2**20, transcendentals=0,
             ),
         )(place_both, *blocks)
         return keep.reshape(half_rows, width), swap_core(give).reshape(half_rows, width)
 
-    block_rows_here = half_rows // 4
-
-    def row_call(body, ins, whole, outs, flops):
+    def row_call(body, ins, whole, outs, flops, steps=4, copies=2):
+        block_rows_here = half_rows // steps
         row_spec = [pl.BlockSpec((block_rows_here, v.shape[1]), lambda b: (b, 0)) for v in ins]
         whole_spec = [
             pl.BlockSpec(shape, lambda b, place=place: place, pipeline_mode=pl.Buffered(1))
             for _, shape, place in whole
         ]
-        outs = [out for out in outs for _ in range(2)]
+        outs = [out for out in outs for _ in range(copies)]
         return pl.pallas_call(
             body,
-            grid=(4,),
+            grid=(steps,),
             out_shape=tuple(jax.ShapeDtypeStruct((half_rows, w), d) for w, d in outs),
             in_specs=row_spec + whole_spec,
             out_specs=tuple(pl.BlockSpec((block_rows_here, w), lambda b: (b, 0)) for w, _ in outs),
-            compiler_params=pltpu.CompilerParams(vmem_limit_bytes=44 * 2**20),
+            compiler_params=pltpu.CompilerParams(vmem_limit_bytes=38 * 2**20),
             cost_estimate=pl.CostEstimate(
-                flops=flops, bytes_accessed=24 * 2**20, transcendentals=0
+                flops=flops, bytes_accessed=flops // 200, transcendentals=0
             ),
         )(*ins, *[v for v, _, _ in whole])
 
@@ -290,8 +290,8 @@
         return jnp.concatenate([refs[0][:, at], refs[1][:, at]])
 
     def put(refs, v, at=slice(None)):
-        refs[0][:, at] = v[:block_rows_here]
-        refs[1][:, at] = v[block_rows_here:]
+        refs[0][:, at] = v[: v.shape[0] // 2]
+        refs[1][:, at] = v[v.shape[0] // 2 :]
 
     nt = (((1,), (1,)), ((), ()))
     gate_matrix, up_matrix, down_matrix = w_gate[0], w_up[0], w_down[0]
@@ -300,9 +300,9 @@
     mask_spec = (lane_mask, (1, info_width), (0, 0))
     unit = 2 * 2 * half_rows * model_width * hidden_width
 
-    t0 = jnp.concatenate([part_of(tokens, 0), info], axis=1)
-    t1, t2 = part_of(tokens, 1), part_of(tokens, 2)
-    c0, c1, c2 = (part_of(cotangent, n) for n in range(3))
+    t0 = jnp.concatenate([tokens[:, : t_cuts[1]], info], axis=1)
+    t1 = tokens[:, t_cuts[1] :]
+    c0, c1, c2 = (cotangent[:, c_cuts[n] : c_cuts[n + 1]] for n in range(3))
     t0_hops, t1_hops, c0_hops, c1_hops = [t0], [t1], [c0], [c1]
 
     def hop(hops):
@@ -313,7 +313,7 @@
 
     hop(t0_hops)
     hop(t1_hops)
-    t2_hops = [with_other("y", with_other("x", t2[None]))]
+    c2_hops = [with_other("y", with_other("x", c2[None]))]
     t0_near = [near("y", t0_hops, 0)]
     t1_near = [near("x", t1_hops, 0)]
     hop(t0_hops)
@@ -324,33 +324,22 @@
     hop(t1_hops)
     t1_near.append(near("x", t1_hops, 1))
     t0_near.append(near("y", t0_hops, 1))
-    hop(t2_hops)
     hop(c0_hops)
     hop(c1_hops)
     t0_far.append(send("x", t0_near[1]))
     t1_far.append(send("y", t1_near[1]))
-    hop(t2_hops)
-    c2_hops = [with_other("y", with_other("x", c2[None]))]
-    c0_near = [near("y", c0_hops, 0)]
-    c1_near = [near("x", c1_hops, 0)]
     hop(c0_hops)
     hop(c1_hops)
-    hop(t2_hops)
-    c0_far = [send("x", c0_near[0])]
-    c1_far = [send("y", c1_near[0])]
     hop(c0_hops)
     hop(c1_hops)
-    c1_near.append(near("x", c1_hops, 1))
-    c0_near.append(near("y", c0_hops, 1))
     hop(c2_hops)
-    c0_far.append(send("x", c0_near[1]))
-    c1_far.append(send("y", c1_near[1]))
+    c1_near = with_other("x", jnp.stack(c1_hops))
+    c0_near = with_other("y", jnp.stack(c0_hops))
     hop(c2_hops)
-
     t0_blocks = [t0_near[0], t0_far[0], t0_near[1], t0_far[1]]
     t1_blocks = [t1_near[0], t1_far[0], t1_near[1], t1_far[1]]
     got_info = jnp.stack(
-        [t0_blocks[where[0][k][0]][where[0][k][1], :, cuts[1] :] for k in order]
+        [t0_blocks[where[0][k][0]][where[0][k][1], :, t_cuts[1] :] for k in order]
     )
     slots = jnp.arange(most_rows, dtype=f32)
 
@@ -362,43 +351,76 @@
     place_both = jnp.concatenate([places_of(mine), places_of(other)], axis=1)
     rows = [
         half
-        for n, blocks in enumerate((t0_blocks, t1_blocks, t2_hops))
-        for half in compact(blocks, where[n])
+        for n, blocks in enumerate((t0_blocks, t1_blocks))
+        for half in compact(place_both, blocks, where[n])
     ]
 
     def forward(*refs):
-        halves, (gates_at, wg, wu), outs = refs[:6], refs[6:9], refs[9:]
-        parts = [both_halves(halves[2 * n : 2 * n + 2], slice(0, cuts[n + 1] - cuts[n])) for n in range(3)]
-        sent = both_halves(halves[:2], slice(cuts[1], None))
-        row_gate = jnp.sum(sent.astype(f32) * gates_at[...], axis=1, keepdims=True)
+        (part0, part1), (gates_at, wg, wu), outs = refs[:2], refs[2:5], refs[5:]
+        sent = part0[:, t_cuts[1] :].astype(f32)
+        row_gate = jnp.sum(sent * gates_at[...], axis=1, keepdims=True)
+        parts = (part0[:, : t_cuts[1]], part1[...])
         pre_gate, pre_up = 0.0, 0.0
-        for n in range(3):
-            rows_at = slice(cuts[n], cuts[n + 1])
+        for n in range(2):
+            rows_at = slice(t_cuts[n], t_cuts[n + 1])
             pre_gate += jnp.dot(parts[n], wg[rows_at], preferred_element_type=f32)
             pre_up += jnp.dot(parts[n], wu[rows_at], preferred_element_type=f32)
         sigmoid_gate = 1.0 / (1.0 + jnp.exp(-pre_gate))
         silu_gate = pre_gate * sigmoid_gate
         hidden = silu_gate * pre_up
-        put(outs[0:2], hidden)
+        outs[0][...] = hidden
         slope = pre_up * sigmoid_gate * (1.0 + pre_gate * (1.0 - sigmoid_gate))
-        put(outs[2:4], row_gate * slope)
-        put(outs[4:6], row_gate * silu_gate)
-        put(outs[6:8], (row_gate * hidden).astype(bf16))
+        outs[1][...] = row_gate * slope
+        outs[2][...] = row_gate * silu_gate
+        outs[3][...] = (row_gate * hidden).astype(bf16)
 
     square = (model_width, hidden_width)
-    forward_out = row_call(
-        forward,
-        rows,
-        [mask_spec, (gate_matrix, square, (0, 0)), (up_matrix, square, (0, 0))],
-        [(hidden_width, f32)] * 3 + [(hidden_width, bf16)],
-        2 * unit,
-    )
-    before_last, held = lax.optimization_barrier((c2_hops[-1], forward_out[0]))
-    c2_hops.append(send("z", before_last))
-    kept, weighted = (held,) + forward_out[1:6], forward_out[6:]
-    c1_rows = compact([c1_near[0], c1_far[0], c1_near[1], c1_far[1]], where[1])
-    c0_rows = compact([c0_near[0], c0_far[0], c0_near[1], c0_far[1]], where[0])
-    cot_rows = [*c0_rows, *c1_rows, *compact(c2_hops, where[2])]
+    def forward_half(part0, part1, flops):
+        return row_call(
+            forward,
+            [part0, part1],
+            [mask_spec, (gate_matrix, square, (0, 0)), (up_matrix, square, (0, 0))],
+            [(hidden_width, f32)] * 3 + [(hidden_width, bf16)],
+            flops,
+            2,
+            1,
+        )
+
+    forward_own = forward_half(rows[0], rows[2], 2 * unit)
+    first_kept = forward_own[0]
+    c0_far = send("x", c0_near)
+    c1_far = send("y", c1_near)
+    hop(c2_hops)
+    given_in, _, _ = lax.optimization_barrier((rows[1], c0_near, c2_hops[2]))
+    forward_out = [[first_kept, *forward_own[1:]], forward_half(given_in, rows[3], 2 * unit)]
+    kept = [forward_out[h][n] for n in range(3) for h in range(2)]
+    weighted = [forward_out[h][3] for h in range(2)]
+    place_tied, kept[0], kept[1] = lax.optimization_barrier((place_both, kept[0], kept[1]))
+    c1_rows = compact(place_tied, [c1_near, c1_far], where[4])
+    c0_rows = compact(place_tied, [c0_near, c0_far], where[3])
+
+    def early(*refs):
+        total = 0.0
+        for n in range(2):
+            total += lax.dot_general(
+                both_halves(refs[2 * n : 2 * n + 2]),
+                refs[4][:, c_cuts[n] : c_cuts[n + 1]],
+                nt,
+                preferred_element_type=f32,
+            )
+        put(refs[5:], total)
+
+    early_back = row_call(
+        early,
+        [*c0_rows, *c1_rows],
+        [(down_matrix, (hidden_width, c_cuts[2]), (0, 0))],
+        [(hidden_width, f32)],
+        1024,
+    )
+    place_tied, early_first = lax.optimization_barrier((place_both, early_back[0]))
+    early_back = [early_first, early_back[1]]
+    c2_rows = compact(place_tied, c2_hops, where[2])
+    cot_rows = [*c0_rows, *c1_rows, *c2_rows]
 
     def row_grad(pgg, pug, wg, wu):
         return lax.dot_general(pgg, wg, nt, preferred_element_type=f32) + lax.dot_general(
@@ -406,65 +428,44 @@
         )
 
     def backward(*refs):
-        halves, gated, slope, silu = refs[:6], refs[6:8], refs[8:10], refs[10:12]
-        (gates_at, wd, wg, wu), outs = refs[12:16], refs[16:]
-        back = 0.0
-        for n in range(3):
-            back += lax.dot_general(
-                both_halves(halves[2 * n : 2 * n + 2]),
-                wd[:, cuts[n] : cuts[n + 1]],
-                nt,
-                preferred_element_type=f32,
-            )
-        gate_grad = jnp.sum(both_halves(gated) * back, axis=1, keepdims=True)
-        gate_side = (back * both_halves(slope)).astype(bf16)
-        up_side = (back * both_halves(silu)).astype(bf16)
-        put(outs[0:2], gate_side)
-        put(outs[2:4], up_side)
-        put(outs[4:6], (gate_grad * gates_at[...]).astype(bf16))
-        put(outs[6:8], row_grad(gate_side, up_side, wg[...], wu[...]).astype(bf16))
-
-    last = (cuts[3] - cuts[2], hidden_width)
-    third = (cuts[1], hidden_width)
-    last_at = cuts[2] // last[0]
-    backward_out = row_call(
-        backward,
-        cot_rows + list(kept),
-        [
-            mask_spec,
-            (down_matrix, (hidden_width, model_width), (0, 0)),
-            (gate_matrix, last, (last_at, 0)),
-            (up_matrix, last, (last_at, 0)),
-        ],
-        [(hidden_width, bf16)] * 2 + [(info_width, bf16), (last[0], bf16)],
-        3 * unit // 2,
-    )
-    sides, gate_lanes, grad_last = backward_out[:4], backward_out[4:6], backward_out[6:]
-
-    def first_grad(*refs):
-        outs = refs[8:]
-        grad = row_grad(both_halves(refs[0:2]), both_halves(refs[2:4]), refs[6][...], refs[7][...])
-        put(outs, grad.astype(bf16), slice(0, cuts[1]))
-        put(outs, both_halves(refs[4:6]), slice(cuts[1], None))
-
-    def second_grad(*refs):
-        grad = row_grad(both_halves(refs[0:2]), both_halves(refs[2:4]), refs[4][...], refs[5][...])
-        put(refs[6:], grad.astype(bf16))
-
-    grad_first = row_call(
-        first_grad,
-        [*sides, *gate_lanes],
-        [(gate_matrix, third, (0, 0)), (up_matrix, third, (0, 0))],
-        [(info_width + third[0], bf16)],
-        3 * unit // 4,
-    )
-    grad_second = row_call(
-        second_grad,
-        [*sides],
-        [(gate_matrix, third, (1, 0)), (up_matrix, third, (1, 0))],
-        [(third[0], bf16)],
-        3 * unit // 4,
-    )
+        half, first, gated, slope, silu, gates_at, wd, wg, wu = refs[:9]
+        pgg, pug, grad0, grad1, grad2 = refs[9:]
+        back = first[...] + lax.dot_general(
+            half[...], wd[...], nt, preferred_element_type=f32
+        )
+        gate_grad = jnp.sum(gated[...] * back, axis=1, keepdims=True)
+        gate_side = (back * slope[...]).astype(bf16)
+        up_side = (back * silu[...]).astype(bf16)
+        pgg[...] = gate_side
+        pug[...] = up_side
+        for n, out in ((2, grad2), (0, grad0), (1, grad1)):
+            at = slice(cuts[n], cuts[n + 1])
+            grad = row_grad(gate_side, up_side, wg[at], wu[at])
+            out[:, : cuts[n + 1] - cuts[n]] = grad.astype(bf16)
+        grad0[:, cuts[1] :] = (gate_grad * gates_at[...]).astype(bf16)
+
+    def backward_half(h, half):
+        return row_call(
+            backward,
+            [half, early_back[h], kept[h], kept[2 + h], kept[4 + h]],
+            [
+                mask_spec,
+                (down_matrix, (hidden_width, c_cuts[3] - c_cuts[2]), (0, 1)),
+                (gate_matrix, square, (0, 0)),
+                (up_matrix, square, (0, 0)),
+            ],
+            [(hidden_width, bf16)] * 2
+            + [(info_width + cuts[1], bf16), (cuts[2] - cuts[1], bf16), (cuts[3] - cuts[2], bf16)],
+            1024,
+            2,
+            1,
+        )
+
+    given_out = backward_half(1, c2_rows[1])
+    own_in, tied = lax.optimization_barrier((c2_rows[0], given_out[0]))
+    own_out = backward_half(0, own_in)
+    sides = [own_out[0], tied, own_out[1], given_out[1]]
+    grad_first, grad_second, grad_last = ((own_out[n], given_out[n]) for n in (2, 3, 4))
 
     place_grid = place_both.reshape(2, 2, 2, 2, 2 * most_rows, tok_local)
 
@@ -483,6 +484,7 @@
     links["x"].clear()
     links["y"].clear()
     links["z"].clear()
+    depth.update(x=3, y=3, z=3)
     v2 = pair_rows(grad_last)
     v0 = pair_rows(grad_first)
     v1 = pair_rows(grad_second)
@@ -491,35 +493,40 @@
         return spread(place_grid[r // 2, :, :, r % 2], v2[r // 2, :, :, r % 2])
 
     first_last = spread_last(3).astype(bf16)
-    moving2 = send("d", first_last)
     far0 = [spread(place_grid[g, 1], v0[g, 1]).astype(bf16) for g in range(2)]
     far1 = [spread(place_grid[g, :, 1], v1[g, :, 1]).astype(bf16) for g in range(2)]
+    first_last, far0, far1 = lax.optimization_barrier((first_last, far0, far1))
+    moving2 = send("d", first_last)
     sent0, sent1, half0, half1, near0, near1 = ([None, None] for _ in range(6))
     sent0[1] = send("x", far0[1])
     sent1[1] = send("y", far1[1])
-    sides_tied, _, _, _ = lax.optimization_barrier((sides, far0[1], far1[1], first_last))
-    moving2 = send("d", add(spread_last(2), moving2))
-    half1[1] = add(spread(place_grid[1, :, 0], v1[1, :, 0]), sent1[1])
-    near1[1] = send("x", half1[1][1])
-    half0[1] = add(spread(place_grid[1, 0], v0[1, 0]), sent0[1])
-    near0[1] = send("y", half0[1][1])
-    weighted_tied, _, _ = lax.optimization_barrier((weighted, half0[1], half1[1]))
     sent0[0] = send("x", far0[0])
     sent1[0] = send("y", far1[0])
-    moving2 = send("d", add(spread_last(1), moving2))
+    gate_tied, _, _, _ = lax.optimization_barrier((sides[:2], far0, far1, first_last))
+    moving2 = add(spread_last(2), moving2)
+    up_tied, moving2 = lax.optimization_barrier((sides[2:], moving2))
+    moving2 = send("d", moving2)
+    half1[1] = add(spread(place_grid[1, :, 0], v1[1, :, 0]), sent1[1])
+    half0[1] = add(spread(place_grid[1, 0], v0[1, 0]), sent0[1])
+    moving2 = add(spread_last(1), moving2)
+    half1[1], half0[1], moving2 = lax.optimization_barrier((half1[1], half0[1], moving2))
+    moving2 = send("d", moving2)
+    near1[1] = send("x", half1[1][1])
+    near0[1] = send("y", half0[1][1])
+    half1[0] = add(spread(place_grid[0, :, 0], v1[0, :, 0]), sent1[0])
+    half0[0] = add(spread(place_grid[0, 0], v0[0, 0]), sent0[0])
+    near1[0] = send("x", half1[0][1])
+    near0[0] = send("y", half0[0][1])
     sum0_high = add(half0[1][0], near0[1])
     sum1_high = add(half1[1][0], near1[1])
+    weighted_tied, _, _ = lax.optimization_barrier((weighted, half0[0], half1[0]))
     moving0 = send("d", sum0_high[1])
     moving1 = send("d", sum1_high[1])
-    half1[0] = add(spread(place_grid[0, :, 0], v1[0, :, 0]), sent1[0])
-    near1[0] = send("x", half1[0][1])
-    half0[0] = add(spread(place_grid[0, 0], v0[0, 0]), sent0[0])
-    near0[0] = send("y", half0[0][1])
-    moving0 = send("d", add(sum0_high[0], moving0))
-    moving1 = send("d", add(sum1_high[0], moving1))
     pair = add(spread_last(0), moving2)
     pair = add(pair[:, 0], send("y", pair[:, 1]))
     sum_last = add(pair[0], send("x", pair[1]))
+    moving0 = send("d", add(sum0_high[0], moving0))
+    moving1 = send("d", add(sum1_high[0], moving1))
     sum0_low = add(half0[0][0], near0[0])
     sum1_low = add(half1[0][0], near1[0])
     moving0 = send("d", add(sum0_low[1], moving0))
@@ -531,66 +538,63 @@
     gate_grad_out = jnp.sum(jnp.where(hit, gate_back[:, None, :], 0.0), axis=2).astype(bf16)
 
     tile = 256
-    firsts = [cut // tile for cut in cuts]
-
-    def tile_spec(n):
-        top = firsts[n + 1] - firsts[n] - 1
-        return pl.BlockSpec(
-            (half_rows, tile), lambda b: (0, jnp.clip(b - firsts[n], 0, top))
-        )
-
-    tile_specs = [tile_spec(n) for n in range(3) for _ in range(2)]
     tn = (((0,), (0,)), ((), ()))
 
     def tn_dot(a, b):
         return lax.dot_general(a, b, tn, preferred_element_type=f32)
 
-    def side_weights(*refs):
-        halves, (pgg0, pgg1, pug0, pug1), (gate_out, up_out) = refs[:6], refs[6:10], refs[10:]
-        step = pl.program_id(0)
-        for n in range(3):
-
-            @pl.when((step >= firsts[n]) & (step < firsts[n + 1]))
-            def _(n=n):
-                x0, x1 = halves[2 * n][...], halves[2 * n + 1][...]
-                gate_out[...] = (tn_dot(x0, pgg0[...]) + tn_dot(x1, pgg1[...])).astype(bf16)
-                up_out[...] = (tn_dot(x0, pug0[...]) + tn_dot(x1, pug1[...])).astype(bf16)
-
-    def down_weights(*refs):
-        halves, (w0, w1), out = refs[:6], refs[6:8], refs[8]
-        step = pl.program_id(0)
-        for n in range(3):
-
-            @pl.when((step >= firsts[n]) & (step < firsts[n + 1]))
-            def _(n=n):
-                c0_tile, c1_tile = halves[2 * n][...], halves[2 * n + 1][...]
-                out[...] = (tn_dot(w0[...], c0_tile) + tn_dot(w1[...], c1_tile)).astype(bf16)
-
-    half_spec = pl.BlockSpec(
-        (half_rows, hidden_width), lambda b: (0, 0), pipeline_mode=pl.Buffered(1)
-    )
-    grad_spec = pl.BlockSpec((tile, hidden_width), lambda b: (b, 0))
-    grad_shape = jax.ShapeDtypeStruct((model_width, hidden_width), bf16)
-    w_gate_grad, w_up_grad = pl.pallas_call(
-        side_weights,
-        grid=(firsts[3],),
-        out_shape=(grad_shape, grad_shape),
-        in_specs=tile_specs + [half_spec] * 4,
-        out_specs=(grad_spec, grad_spec),
-        compiler_params=pltpu.CompilerParams(vmem_limit_bytes=28 * 2**20),
-        cost_estimate=pl.CostEstimate(
-            flops=2 * unit, bytes_accessed=20 * 2**20, transcendentals=0
-        ),
-    )(*rows, *sides_tied)
-    w_down_grad = pl.pallas_call(
-        down_weights,
-        grid=(firsts[3],),
-        out_shape=jax.ShapeDtypeStruct((hidden_width, model_width), bf16),
-        in_specs=tile_specs + [half_spec] * 2,
-        out_specs=pl.BlockSpec((hidden_width, tile), lambda b: (0, b)),
-        compiler_params=pltpu.CompilerParams(vmem_limit_bytes=28 * 2**20),
-        cost_estimate=pl.CostEstimate(flops=unit, bytes_accessed=14 * 2**20, transcendentals=0),
-    )(*cot_rows, *weighted_tied)
+    def weight_call(body, halves, cuts, wide, out_spec, out_shape):
+        firsts = [cut // tile for cut in cuts]
+        count = len(halves)
+
+        def run(*refs):
+            step = pl.program_id(0)
+            for n in range(count // 2):
+
+                @pl.when((step >= firsts[n]) & (step < firsts[n + 1]))
+                def _(n=n):
+                    tiles = (refs[2 * n][...], refs[2 * n + 1][...])
+                    refs[-1][...] = body(tiles, refs[count : count + 2]).astype(bf16)
+
+        def tile_spec(n):
+            low, top = firsts[n], firsts[n + 1] - firsts[n] - 1
+            return pl.BlockSpec((half_rows, tile), lambda b: (0, jnp.clip(b - low, 0, top)))
+
+        half_spec = pl.BlockSpec(
+            (half_rows, hidden_width), lambda b: (0, 0), pipeline_mode=pl.Buffered(1)
+        )
+        return pl.pallas_call(
+            run,
+            grid=(firsts[-1],),
+            out_shape=jax.ShapeDtypeStruct(out_shape, bf16),
+            in_specs=[tile_spec(n // 2) for n in range(count)] + [half_spec] * 2,
+            out_specs=out_spec,
+            compiler_params=pltpu.CompilerParams(vmem_limit_bytes=16 * 2**20),
+            cost_estimate=pl.CostEstimate(
+                flops=unit, bytes_accessed=14 * 2**20, transcendentals=0
+            ),
+        )(*halves, *wide)
+
+    def side_weights(sides):
+        return weight_call(
+            lambda x, side: tn_dot(x[0], side[0][...]) + tn_dot(x[1], side[1][...]),
+            rows,
+            t_cuts,
+            sides,
+            pl.BlockSpec((tile, hidden_width), lambda b: (b, 0)),
+            (model_width, hidden_width),
+        )
+
+    w_gate_grad = side_weights(gate_tied)
+    w_up_grad = side_weights(up_tied)
+    w_down_grad = weight_call(
+        lambda c, w: tn_dot(w[0][...], c[0]) + tn_dot(w[1][...], c[1]),
+        cot_rows,
+        c_cuts,
+        weighted_tied,
+        pl.BlockSpec((hidden_width, tile), lambda b: (0, b)),
+        (hidden_width, model_width),
+    )
     return (input_grad, gate_grad_out, w_gate_grad[None], w_up_grad[None], w_down_grad[None])
 
 

time: 331 us -> 326 us (0.985); the launches traced: 331 us -> 320 us
  waiting for transfers between devices: 156 us -> 133 us
  Pallas kernels: 83.7 us -> 95.7 us
  local copies, waits for them, and re-layouts: 12.9 us -> 22.7 us
  starting transfers between devices: 64.6 us -> 56.4 us
    ppermute x9, waiting for transfers between devices: 33.4 us -> 18.4 us  [ring_down(): lax.ppermute(v, 'expert', [(q, (q - 2) % expert_count) for q in range(exp...]
    ppermute x15 -> x12, waiting for transfers between devices: 30.5 us -> 20.8 us  [swap_x(): return lax.ppermute(v, 'dp', [(p, p ^ 2) for p in range(dp_count)])]
    ppermute x15 -> x12, starting transfers between devices: 20.5 us -> 11.2 us  [swap_x(): return lax.ppermute(v, 'dp', [(p, p ^ 2) for p in range(dp_count)])]
    unnamed x58 -> x77, local copies, waits for them, and re-layouts: 9.7 us -> 18.7 us
    pallas_call x6 -> x5, Pallas kernels: 4.96 us -> 13.3 us  [compact(): pl.pallas_call(body, out_shape=(shape, shape), in_specs=[pl.BlockSpec(mem...]
    ppermute x9, starting transfers between devices: 14.9 us -> 20.3 us  [ring_down(): lax.ppermute(v, 'expert', [(q, (q - 2) % expert_count) for q in range(exp...]
    ppermute x15 -> x12, starting transfers between devices: 17.1 us -> 12.3 us  [swap_y(): return lax.ppermute(v, 'expert', [(q, q ^ 1) for q in range(expert_count)])]
    pallas_call x6 -> x8, Pallas kernels: 78.7 us -> 82.4 us  [the longest x5 50.2 us: row_call(): pl.pallas_call(body, grid=(steps,), out_shape=tuple((jax.ShapeDtypeStruct...]
  transfers between devices with their start and end apart: 66 -> 56, of which waited for: 28 -> 24; matrix products, arithmetic and copies ran while one was open for 3% -> 5% of each run, Pallas kernels for 19% -> 24%
where the time goes in v4:
time: 326 us; the launch traced here: 320 us
  waiting for transfers between devices  133 us (41%)
  Pallas kernels  95.7 us (29%)
  starting transfers between devices  56.4 us (17%)
  local copies, waits for them, and re-layouts  22.7 us (7%)
  matrix products  5.31 us (2%)
  other arithmetic  5.01 us (2%)
    ppermute x15, waiting for transfers between devices, ring_up(): lax.ppermute(v, 'expert', [(q, (q + 2) % expert_count) for q in range(exp...  69.3 us
    pallas_call x5, Pallas kernels, row_call(): pl.pallas_call(body, grid=(steps,), out_shape=tuple((jax.ShapeDtypeStruct...  50.2 us
    pallas_call x3, Pallas kernels, weight_call(): pl.pallas_call(run, grid=(firsts[-1],), out_shape=jax.ShapeDtypeStruct(ou...  32.2 us
    ppermute x12, waiting for transfers between devices, swap_x(): return lax.ppermute(v, 'dp', [(p, p ^ 2) for p in range(dp_count)])  20.8 us
    ppermute x9, starting transfers between devices, ring_down(): lax.ppermute(v, 'expert', [(q, (q - 2) % expert_count) for q in range(exp...  20.3 us
    ppermute x12, waiting for transfers between devices, swap_y(): return lax.ppermute(v, 'expert', [(q, q ^ 1) for q in range(expert_count)])  18.9 us
    unnamed x77, local copies, waits for them, and re-layouts  18.7 us
    ppermute x9, waiting for transfers between devices, ring_down(): lax.ppermute(v, 'expert', [(q, (q - 2) % expert_count) for q in range(exp...  18.4 us
  transfers between devices with their start and end apart: 56, of which 24 were waited for; matrix products, arithmetic and copies ran while one was open for 5% of the time, Pallas kernels for 24%

profile of v4, /device:TPU:0, one launch (start us, length us, event | category | flops | bytes accessed | tf_op | source)
XLA Modules:
  0.0 320.0 jit_solution(9693212720040409750)
XLA Ops:
  2.3 1.1 slice_bitcast_fusion.21
  3.7 3.1 collective-permute-start
  6.8 1.6 collective-permute-start.5
  8.4 1.6 collective-permute-start.2
  12.0 9.4 %collective-permute-done.5 = bf16[128,1024]{1,0:T(8,128)(2,1)S(1)} collective-permute-done((bf16[128,1024]{1,0:T(8,128)(2,1)S(1)}, bf16[128,1024]{1,0:T(8,128)(2,1)S(1)}, u32[]{:S(2)}, u32[]{:S(2)}) %collective-permute-start.5) | collective-permute-done | bytes 262176 | tf_op jit(solution)/shard_map/ppermute | solution.py:186
  21.5 1.6 collective-permute-start.9
  23.1 1.6 collective-permute-start.10
  24.7 1.3 collective-permute-start.4
  26.6 7.5 %collective-permute-done.12 = bf16[128,1024]{1,0:T(8,128)(2,1)S(1)} collective-permute-done((bf16[128,1024]{1,0:T(8,128)(2,1)S(1)}, bf16[128,1024]{1,0:T(8,128)(2,1)S(1)}, u32[]{:S(2)}, u32[]{:S(2)}) %collective-permute-start.12) | collective-permute-done | bytes 262176 | tf_op jit(solution)/shard_map/ppermute | solution.py:186
  34.1 5.4 %collective-permute-done.4 = bf16[128,1152]{1,0:T(8,128)(2,1)S(1)} collective-permute-done((bf16[128,1152]{1,0:T(8,128)(2,1)S(1)}, bf16[128,1152]{1,0:T(8,128)(2,1)S(1)}, u32[]{:S(2)}, u32[]{:S(2)}) %collective-permute-start.4) | collective-permute-done | bytes 294944 | tf_op jit(solution)/shard_map/ppermute | solution.py:186
  39.5 1.9 collective-permute-done.17
  42.3 1.6 collective-permute-start.11
  43.9 6.6 %collective-permute-done.13 = bf16[128,1024]{1,0:T(8,128)(2,1)S(1)} collective-permute-done((bf16[128,1024]{1,0:T(8,128)(2,1)S(1)}, bf16[128,1024]{1,0:T(8,128)(2,1)S(1)}, u32[]{:S(2)}, u32[]{:S(2)}) %collective-permute-start.13) | collective-permute-done | bytes 262176 | tf_op jit(solution)/shard_map/ppermute | solution.py:186
  51.5 2.8 collective-permute-done.6
  55.4 1.3 collective-permute-start.7
  56.7 1.8 collective-permute-done.18
  59.2 6.6 %collective-permute-done.19 = bf16[128,512]{1,0:T(8,128)(2,1)S(1)} collective-permute-done((bf16[128,512]{1,0:T(8,128)(2,1)S(1)}, bf16[128,512]{1,0:T(8,128)(2,1)S(1)}, u32[]{:S(2)}, u32[]{:S(2)}) %collective-permute-start.19) | collective-permute-done | bytes 131104 | tf_op jit(solution)/shard_map/ppermute | solution.py:186
  66.5 6.1 %collective-permute-done.22 = bf16[128,512]{1,0:T(8,128)(2,1)S(1)} collective-permute-done((bf16[128,512]{1,0:T(8,128)(2,1)S(1)}, bf16[128,512]{1,0:T(8,128)(2,1)S(1)}, u32[]{:S(2)}, u32[]{:S(2)}) %collective-permute-start.22) | collective-permute-done | bytes 131104 | tf_op jit(solution)/shard_map/ppermute | solution.py:186
  72.6 10.9 %collective-permute-done.7 = bf16[2,128,1152]{2,1,0:T(8,128)(2,1)S(1)} collective-permute-done((bf16[2,128,1152]{2,1,0:T(8,128)(2,1)S(1)}, bf16[2,128,1152]{2,1,0:T(8,128)(2,1)S(1)}, u32[]{:S(2)}, u32[]{:S(2)}) %collective-permute-start.7) | collective-permute-done | bytes 589856 | tf_op jit(solution)/shard_map/ppermute | solution.py:183
  85.9 1.6 collective-permute-start.28
  87.6 1.6 collective-permute-start.15
  89.2 20.4 %collective-permute-done.23.refs_1_ = bf16[4,128,1024]{2,1,0:T(8,128)(2,1)S(1)} collective-permute-done((bf16[4,128,1024]{2,1,0:T(8,128)(2,1)S(1)}, bf16[4,128,1024]{2,1,0:T(8,128)(2,1)S(1)}, u32[]{:S(2)}, u32[]{:S(2)}) %collective-permute-start.23) | collective-permute-done | bytes 1048608 | tf_op jit(solution)/shard_map/ppermute | solution.py:186
  110.4 2.7 shard_map.110
  114.1 2.3 shard_map.111
  116.8 1.2 collective-permute-start.21
  119.3 8.2 %collective-permute-done.29 = bf16[4,128,512]{2,1,0:T(8,128)(2,1)S(1)} collective-permute-done((bf16[4,128,512]{2,1,0:T(8,128)(2,1)S(1)}, bf16[4,128,512]{2,1,0:T(8,128)(2,1)S(1)}, u32[]{:S(2)}, u32[]{:S(2)}) %collective-permute-start.29) | collective-permute-done | bytes 524320 | tf_op jit(solution)/shard_map/ppermute | solution.py:180
  128.4 2.6 collective-permute-done.21
  131.8 1.1 collective-permute-start.30
  133.6 1.9 collective-permute-start.32
  135.5 1.5 collective-permute-start.26
  137.0 8.3 %shard_map.112 = (f32[896,768]{1,0:T(8,128)S(1)}, f32[896,768]{1,0:T(8,128)S(1)}, f32[896,768]{1,0:T(8,128)S(1)}, bf16[896,768]{1,0:T(8,128)(2,1)S(1)}) custom-call(bf16[896,1152]{1,0:T(8,128)(2,1)S(1)} %bitcast.237, bf16[896,1024]{1,0:T(8,128)(2,1)S(1)} %bitcast.243, f32[1,128]{1,0:T(1,128)S(1)} %compare_convert_fusion.refs_2_.refs_5_, ...), custom_call_target="tpu_custom_call" | custom-call | flops 11274289152 | bytes 56371444 | tf_op jit(solution)/shard_map/pallas_call | solution.py:277
  145.3 1.5 copy-done.2
  146.8 1.6 copy-done.3
  149.4 1.4 copy-done.18
  150.8 1.6 copy-done.19
  152.4 8.6 %shard_map.113 = (f32[896,768]{1,0:T(8,128)S(1)}, f32[896,768]{1,0:T(8,128)S(1)}, f32[896,768]{1,0:T(8,128)S(1)}, bf16[896,768]{1,0:T(8,128)(2,1)S(1)}) custom-call(bf16[896,1152]{1,0:T(8,128)(2,1)S(1)} %bitcast.240, bf16[896,1024]{1,0:T(8,128)(2,1)} %bitcast.21.refs_1_.refs_3_, f32[1,128]{1,0:T(1,128)S(1)} %compare_convert_fusion.refs_2_.refs_5_, ...), custom_call_target="tpu_custom_call" | custom-call | flops 11274289152 | bytes 56371444 | tf_op jit(solution)/shard_map/pallas_call | solution.py:277
  161.0 1.5 copy-done.5
  162.5 1.1 copy-done.25
  163.6 2.8 shard_map.115
  166.5 1.9 shard_map.114
  168.9 2.1 collective-permute-done.27
  171.0 3.8 %shard_map.116 = (f32[896,768]{1,0:T(8,128)S(1)}, f32[896,768]{1,0:T(8,128)S(1)}) custom-call(bf16[896,512]{1,0:T(8,128)(2,1)S(1)} %bitcast.233, bf16[896,512]{1,0:T(8,128)(2,1)S(1)} %bitcast.235, bf16[896,512]{1,0:T(8,128)(2,1)S(1)} %bitcast.229, bf16[896,512]{1,0:T(8,128)(2,1)S(1)} %bitcast.231, bf16[768,2048]{1,0:T(8,128)(2,1)S(1)} %bitcast.211), custom_call_target="tpu_custom_call" | custom-call | flops 1024 | bytes 5 | tf_op jit(solution)/shard_map/pallas_call | solution.py:277
  174.9 3.6 %shard_map.117 = (bf16[16,56,1024]{2,1,0:T(8,128)(2,1)S(1)}, bf16[16,56,1024]{2,1,0:T(8,128)(2,1)S(1)}) custom-call(bf16[16,112,128]{2,1,0:T(8,128)(2,1)S(1)} %add_convert_fusion.7.places, bf16[4,128,1024]{2,1,0:T(8,128)(2,1)S(1)} %pad_maximum_fusion.4.refs_0_, bf16[4,128,1024]{2,1,0:T(8,128)(2,1)S(1)} %collective-permute-done.23.refs_1_, ...), custom_call_target="tpu_custom_call" | custom-call | flops 469762048 | bytes 12582912 | tf_op jit(solution)/shard_map/pallas_call | solution.py:257
  179.0 3.4 %collective-permute-done.33 = bf16[16,56,1024]{2,1,0:T(8,128)(2,1)S(1)} collective-permute-done((bf16[16,56,1024]{2,1,0:T(8,128)(2,1)S(1)}, bf16[16,56,1024]{2,1,0:T(8,128)(2,1)S(1)}, u32[]{:S(2)}, u32[]{:S(2)}) %collective-permute-start.33) | collective-permute-done | bytes 1835040 | tf_op jit(solution)/shard_map/ppermute | solution.py:177
  182.4 2.4 copy-done.7
  184.9 15.0 %shard_map.118 = (bf16[896,768]{1,0:T(8,128)(2,1)S(1)}, bf16[896,768]{1,0:T(8,128)(2,1)S(1)}, bf16[896,896]{1,0:T(8,128)(2,1)S(1)}, bf16[896,768]{1,0:T(8,128)(2,1)}, bf16[896,512]{1,0:T(8,128)(2,1)}) custom-call(bf16[896,1024]{1,0:T(8,128)(2,1)S(1)} %bitcast.226, f32[896,768]{1,0:T(8,128)S(1)} %copy-done.7, f32[896,768]{1,0:T(8,128)S(1)} %get-tuple-element.129.refs_2_, ...), custom_call_target="tpu_custom_call" | custom-call | flops 1024 | bytes 5 | tf_op jit(solution)/shard_map/pallas_call | solution.py:277
  201.0 14.5 %shard_map.119 = (bf16[896,768]{1,0:T(8,128)(2,1)S(1)}, bf16[896,768]{1,0:T(8,128)(2,1)S(1)}, bf16[896,896]{1,0:T(8,128)(2,1)S(1)}, bf16[896,768]{1,0:T(8,128)(2,1)S(1)}, bf16[896,512]{1,0:T(8,128)(2,1)S(1)}) custom-call(bf16[896,1024]{1,0:T(8,128)(2,1)S(1)} %bitcast.224, f32[896,768]{1,0:T(8,128)S(1)} %get-tuple-element.134.refs_1_, ...), custom_call_target="tpu_custom_call" | custom-call | flops 1024 | bytes 5 | tf_op jit(solution)/shard_map/pallas_call | solution.py:277
  219.1 3.2 collective-permute-start.41
  223.8 10.8 %shard_map.120 = bf16[2048,768]{1,0:T(8,128)(2,1)} custom-call(bf16[896,1152]{1,0:T(8,128)(2,1)S(1)} %bitcast.238, bf16[896,1152]{1,0:T(8,128)(2,1)S(1)} %bitcast.241, bf16[896,1024]{1,0:T(8,128)(2,1)S(1)} %bitcast.244, bf16[896,1024]{1,0:T(8,128)(2,1)} %bitcast.21.refs_1_.refs_3_, bf16[896,768]{1,0:T(8,128)(2,1)S(1)} %get-tuple-element.167.refs_4_, ...), custom_call_target="tpu_custom_call" | custom-call | flops 5637144576 | bytes 14680064 | tf_op jit(solution)/shard_map/pallas_call | solution.py:566
  235.0 2.9 collective-permute-start.42
  237.9 11.1 %shard_map.121 = bf16[2048,768]{1,0:T(8,128)(2,1)} custom-call(bf16[896,1152]{1,0:T(8,128)(2,1)S(1)} %bitcast.239, bf16[896,1152]{1,0:T(8,128)(2,1)S(1)} %bitcast.242, bf16[896,1024]{1,0:T(8,128)(2,1)S(1)} %bitcast.245, bf16[896,1024]{1,0:T(8,128)(2,1)} %bitcast.21.refs_1_.refs_3_, bf16[896,768]{1,0:T(8,128)(2,1)S(1)} %get-tuple-element.169.refs_4_, ...), custom_call_target="tpu_custom_call" | custom-call | flops 5637144576 | bytes 14680064 | tf_op jit(solution)/shard_map/pallas_call | solution.py:566
  249.4 5.4 %collective-permute-done.38 = bf16[2,2,128,768]{2,3,1,0:T(8,128)(2,1)S(1)} collective-permute-done((bf16[2,2,128,768]{2,3,1,0:T(8,128)(2,1)S(1)}, bf16[2,2,128,768]{2,3,1,0:T(8,128)(2,1)S(1)}, u32[]{:S(2)}, u32[]{:S(2)}) %collective-permute-start.38) | collective-permute-done | bytes 786464 | tf_op jit(solution)/shard_map/ppermute | solution.py:183
  256.4 3.8 %collective-permute-done.40 = bf16[2,2,128,896]{2,3,1,0:T(8,128)(2,1)S(1)} collective-permute-done((bf16[2,2,128,896]{2,3,1,0:T(8,128)(2,1)S(1)}, bf16[2,2,128,896]{2,3,1,0:T(8,128)(2,1)S(1)}, u32[]{:S(2)}, u32[]{:S(2)}) %collective-permute-start.40) | collective-permute-done | bytes 917536 | tf_op jit(solution)/shard_map/ppermute | solution.py:180
  261.3 10.3 %shard_map.122 = bf16[768,2048]{1,0:T(8,128)(2,1)} custom-call(bf16[896,512]{1,0:T(8,128)(2,1)S(1)} %bitcast.234, bf16[896,512]{1,0:T(8,128)(2,1)S(1)} %bitcast.236, bf16[896,512]{1,0:T(8,128)(2,1)S(1)} %bitcast.230, bf16[896,512]{1,0:T(8,128)(2,1)S(1)} %bitcast.232, bf16[896,1024]{1,0:T(8,128)(2,1)S(1)} %bitcast.225, bf16[896,1024]{1,0:T(8,128)(2,1)S(1)} %bitcast.227, ...), custom_call_target="tpu_custom_call" | custom-call | flops 5637144576 | bytes 14680064 | tf_op jit(solution)/shard_map/pallas_call | solution.py:566
  272.4 3.2 collective-permute-start.45
  276.5 8.7 %collective-permute-done.47 = bf16[2,128,768]{1,2,0:T(8,128)(2,1)S(1)} collective-permute-done((bf16[2,128,768]{1,2,0:T(8,128)(2,1)S(1)}, bf16[2,128,768]{1,2,0:T(8,128)(2,1)S(1)}, u32[]{:S(2)}, u32[]{:S(2)}) %collective-permute-start.47) | collective-permute-done | bytes 393248 | tf_op jit(solution)/shard_map/ppermute | solution.py:180
  286.2 1.5 collective-permute-start.44
  288.2 1.3 collective-permute-start.54
  289.5 2.9 collective-permute-done.48
  292.5 2.4 collective-permute-done.44
  294.9 4.3 %collective-permute-start.46 = (bf16[128,896]{0,1:T(8,128)(2,1)S(1)}, bf16[128,896]{0,1:T(8,128)(2,1)S(1)}, u32[]{:S(2)}, u32[]{:S(2)}) collective-permute-start(bf16[128,896]{0,1:T(8,128)(2,1)S(1)} %fusion.43), channel_id=1, source_target_pairs={{0,6},{1,7},{2,0},{3,1},{4,2},{5,3},{6,4},{7,5},{8,14},{9,15},{10,... | collective-permute-start | bytes 688136 | tf_op jit(solution)/shard_map/ppermute | solution.py:191
  300.0 6.7 %collective-permute-done.52 = bf16[128,768]{0,1:T(8,128)(2,1)S(1)} collective-permute-done((bf16[128,768]{0,1:T(8,128)(2,1)S(1)}, bf16[128,768]{0,1:T(8,128)(2,1)S(1)}, u32[]{:S(2)}, u32[]{:S(2)}) %collective-permute-start.52) | collective-permute-done | bytes 196640 | tf_op jit(solution)/shard_map/ppermute | solution.py:191
  306.8 4.3 %collective-permute-start.49 = (bf16[128,896]{0,1:T(8,128)(2,1)S(1)}, bf16[128,896]{0,1:T(8,128)(2,1)S(1)}, u32[]{:S(2)}, u32[]{:S(2)}) collective-permute-start(bf16[128,896]{0,1:T(8,128)(2,1)S(1)} %fusion.44), channel_id=1, source_target_pairs={{0,6},{1,7},{2,0},{3,1},{4,2},{5,3},{6,4},{7,5},{8,14},{9,15},{10,... | collective-permute-start | bytes 688136 | tf_op jit(solution)/shard_map/ppermute | solution.py:191
  311.3 6.4 %collective-permute-done.53 = bf16[128,768]{0,1:T(8,128)(2,1)S(1)} collective-permute-done((bf16[128,768]{0,1:T(8,128)(2,1)S(1)}, bf16[128,768]{0,1:T(8,128)(2,1)S(1)}, u32[]{:S(2)}, u32[]{:S(2)}) %collective-permute-start.53) | collective-permute-done | bytes 196640 | tf_op jit(solution)/shard_map/ppermute | solution.py:191
  (208 shorter events, 34.9 us)
Async XLA Ops:
  0.6 7.7 %copy-start.27 = (bf16[128,2048]{1,0:T(8,128)(2,1)S(1)}, bf16[128,2048]{1,0:T(8,128)(2,1)}, u32[]{:S(2)}) copy-start(bf16[128,2048]{1,0:T(8,128)(2,1)} %param.8) | copy-start | bytes 1572868
  3.7 19.3 %collective-permute-start = (bf16[128,1152]{1,0:T(8,128)(2,1)S(1)}, bf16[128,1152]{1,0:T(8,128)(2,1)S(1)}, u32[]{:S(2)}, u32[]{:S(2)}) collective-permute-start(bf16[128,1152]{1,0:T(8,128)(2,1)S(1)} %concatenate.72), channel_id=1, source_target_pairs={{0,2},{1,3},{2,4},{3,5},{4,6},{5,7},{6,0},{7,1},{8,10},{9,11},{10,... | collective-permute-start | bytes 884744 | tf_op jit(solution)/shard_map/ppermute | solution.py:186
  6.8 14.7 %collective-permute-start.5 = (bf16[128,1024]{1,0:T(8,128)(2,1)S(1)}, bf16[128,1024]{1,0:T(8,128)(2,1)S(1)}, u32[]{:S(2)}, u32[]{:S(2)}) collective-permute-start(bf16[128,1024]{1,0:T(8,128)(2,1)S(1)} %get-tuple-element.195), channel_id=1, source_target_pairs={{0,2},{1,3},{2,4},{3,5},{4,6},{5,7},{6,0},{7,1},{8,10},{9,11},{10,... | collective-permute-start | bytes 786440 | tf_op jit(solution)/shard_map/ppermute | solution.py:186
  8.4 14.7 %collective-permute-start.2 = (bf16[1,128,1024]{2,1,0:T(8,128)(2,1)S(1)}, bf16[1,128,1024]{2,1,0:T(8,128)(2,1)S(1)}, u32[]{:S(2)}, u32[]{:S(2)}) collective-permute-start(bf16[1,128,1024]{2,1,0:T(8,128)(2,1)S(1)} %slice_bitcast_fusion.8), channel_id=1, source_target_pairs={{0,16},{8,24},{16,0},{24,8},{1,17},{9,25},{17,1},{25,9},{2,18},{10... | collective-permute-start | bytes 786440 | tf_op jit(solution)/shard_map/ppermute | solution.py:180
  21.4 12.7 %copy-start.29 = (bf16[128,512]{1,0:T(8,128)(2,1)S(1)}, bf16[128,512]{1,0:T(8,128)(2,1)}, u32[]{:S(2)}) copy-start(bf16[128,512]{1,0:T(8,128)(2,1)} %get-tuple-element.103) | copy-start | bytes 393220
  21.4 12.7 %copy-start.28 = (bf16[16,128,128]{2,1,0:T(8,128)(2,1)S(1)}, bf16[16,128,128]{2,1,0:T(8,128)(2,1)}, u32[]{:S(2)}) copy-start(bf16[16,128,128]{2,1,0:T(8,128)(2,1)} %constant_dynamic-update-slice_fusion.3) | copy-start | bytes 1572868
  21.5 20.6 %collective-permute-start.9 = (bf16[2,128,1024]{2,1,0:T(8,128)(2,1)S(1)}, bf16[2,128,1024]{2,1,0:T(8,128)(2,1)S(1)}, u32[]{:S(2)}, u32[]{:S(2)}) collective-permute-start(bf16[2,128,1024]{2,1,0:T(8,128)(2,1)S(1)} %pad_maximum_fusion.9), channel_id=1, source_target_pairs={{0,16},{8,24},{16,0},{24,8},{1,17},{9,25},{17,1},{25,9},{2,18},{10... | collective-permute-start | bytes 1572872 | tf_op jit(solution)/shard_map/ppermute | solution.py:180
  23.1 11.0 %collective-permute-start.12 = (bf16[128,1024]{1,0:T(8,128)(2,1)S(1)}, bf16[128,1024]{1,0:T(8,128)(2,1)S(1)}, u32[]{:S(2)}, u32[]{:S(2)}) collective-permute-start(bf16[128,1024]{1,0:T(8,128)(2,1)S(1)} %collective-permute-done.5), channel_id=1, source_target_pairs={{0,2},{1,3},{2,4},{3,5},{4,6},{5,7},{6,0},{7,1},{8,10},{9,11},{10,... | collective-permute-start | bytes 786440 | tf_op jit(solution)/shard_map/ppermute | solution.py:186
  23.1 19.1 %collective-permute-start.10 = (bf16[2,128,1024]{2,1,0:T(8,128)(2,1)S(1)}, bf16[2,128,1024]{2,1,0:T(8,128)(2,1)S(1)}, u32[]{:S(2)}, u32[]{:S(2)}) collective-permute-start(bf16[2,128,1024]{2,1,0:T(8,128)(2,1)S(1)} %pad_maximum_fusion.10), channel_id=1, source_target_pairs={{0,1},{1,0},{2,3},{3,2},{4,5},{5,4},{6,7},{7,6},{8,9},{9,8},{10,11... | collective-permute-start | bytes 1572872 | tf_op jit(solution)/shard_map/ppermute | solution.py:183
  24.7 14.8 %collective-permute-start.4 = (bf16[128,1152]{1,0:T(8,128)(2,1)S(1)}, bf16[128,1152]{1,0:T(8,128)(2,1)S(1)}, u32[]{:S(2)}, u32[]{:S(2)}) collective-permute-start(bf16[128,1152]{1,0:T(8,128)(2,1)S(1)} %collective-permute-done), channel_id=1, source_target_pairs={{0,2},{1,3},{2,4},{3,5},{4,6},{5,7},{6,0},{7,1},{8,10},{9,11},{10,... | collective-permute-start | bytes 884744 | tf_op jit(solution)/shard_map/ppermute | solution.py:186
  26.1 28.2 %collective-permute-start.1 = (bf16[2,128,1152]{2,1,0:T(8,128)(2,1)S(1)}, bf16[2,128,1152]{2,1,0:T(8,128)(2,1)S(1)}, u32[]{:S(2)}, u32[]{:S(2)}) collective-permute-start(bf16[2,128,1152]{2,1,0:T(8,128)(2,1)S(1)} %pad_maximum_fusion.7), channel_id=1, source_target_pairs={{0,1},{1,0},{2,3},{3,2},{4,5},{5,4},{6,7},{7,6},{8,9},{9,8},{10,11... | collective-permute-start | bytes 1769480 | tf_op jit(solution)/shard_map/ppermute | solution.py:183
  34.1 7.4 %collective-permute-start.17 = (bf16[128,512]{1,0:T(8,128)(2,1)S(1)}, bf16[128,512]{1,0:T(8,128)(2,1)S(1)}, u32[]{:S(2)}, u32[]{:S(2)}) collective-permute-start(bf16[128,512]{1,0:T(8,128)(2,1)S(1)} %copy-done.29), channel_id=1, source_target_pairs={{0,2},{1,3},{2,4},{3,5},{4,6},{5,7},{6,0},{7,1},{8,10},{9,11},{10,... | collective-permute-start | bytes 393224 | tf_op jit(solution)/shard_map/ppermute | solution.py:186
  39.5 11.0 %collective-permute-start.13 = (bf16[128,1024]{1,0:T(8,128)(2,1)S(1)}, bf16[128,1024]{1,0:T(8,128)(2,1)S(1)}, u32[]{:S(2)}, u32[]{:S(2)}) collective-permute-start(bf16[128,1024]{1,0:T(8,128)(2,1)S(1)} %collective-permute-done.12), channel_id=1, source_target_pairs={{0,2},{1,3},{2,4},{3,5},{4,6},{5,7},{6,0},{7,1},{8,10},{9,11},{10,... | collective-permute-start | bytes 786440 | tf_op jit(solution)/shard_map/ppermute | solution.py:186
  41.5 12.8 %collective-permute-start.6 = (bf16[128,1152]{1,0:T(8,128)(2,1)S(1)}, bf16[128,1152]{1,0:T(8,128)(2,1)S(1)}, u32[]{:S(2)}, u32[]{:S(2)}) collective-permute-start(bf16[128,1152]{1,0:T(8,128)(2,1)S(1)} %collective-permute-done.4), channel_id=1, source_target_pairs={{0,2},{1,3},{2,4},{3,5},{4,6},{5,7},{6,0},{7,1},{8,10},{9,11},{10,... | collective-permute-start | bytes 884744 | tf_op jit(solution)/shard_map/ppermute | solution.py:186
  42.3 45.3 %collective-permute-start.11 = (bf16[4,128,1024]{2,1,0:T(8,128)(2,1)S(1)}, bf16[4,128,1024]{2,1,0:T(8,128)(2,1)S(1)}, u32[]{:S(2)}, u32[]{:S(2)}) collective-permute-start(bf16[4,128,1024]{2,1,0:T(8,128)(2,1)S(1)} %pad_maximum_fusion.2.refs_0_), channel_id=1, source_target_pairs={{0,1},{1,0},{2,3},{3,2},{4,5},{5,4},{6,7},{7,6},{8,9},{9,8},{10,11... | collective-permute-start | bytes 3145736 | tf_op jit(solution)/shard_map/ppermute | solution.py:183
  50.6 7.9 %collective-permute-start.18 = (bf16[128,512]{1,0:T(8,128)(2,1)S(1)}, bf16[128,512]{1,0:T(8,128)(2,1)S(1)}, u32[]{:S(2)}, u32[]{:S(2)}) collective-permute-start(bf16[128,512]{1,0:T(8,128)(2,1)S(1)} %collective-permute-done.17), channel_id=1, source_target_pairs={{0,2},{1,3},{2,4},{3,5},{4,6},{5,7},{6,0},{7,1},{8,10},{9,11},{10,... | collective-permute-start | bytes 393224 | tf_op jit(solution)/shard_map/ppermute | solution.py:186
  50.6 35.2 %collective-permute-start.14 = (bf16[2,128,1024]{2,1,0:T(8,128)(2,1)S(1)}, bf16[2,128,1024]{2,1,0:T(8,128)(2,1)S(1)}, u32[]{:S(2)}, u32[]{:S(2)}) collective-permute-start(bf16[2,128,1024]{2,1,0:T(8,128)(2,1)S(1)} %pad_maximum_fusion.11), channel_id=1, source_target_pairs={{0,16},{8,24},{16,0},{24,8},{1,17},{9,25},{17,1},{25,9},{2,18},{10... | collective-permute-start | bytes 1572872 | tf_op jit(solution)/shard_map/ppermute | solution.py:180
  54.4 30.2 %collective-permute-start.3 = (bf16[4,128,1152]{2,1,0:T(8,128)(2,1)S(1)}, bf16[4,128,1152]{2,1,0:T(8,128)(2,1)S(1)}, u32[]{:S(2)}, u32[]{:S(2)}) collective-permute-start(bf16[4,128,1152]{2,1,0:T(8,128)(2,1)S(1)} %pad_maximum_fusion.refs_0_), channel_id=1, source_target_pairs={{0,16},{8,24},{16,0},{24,8},{1,17},{9,25},{17,1},{25,9},{2,18},{10... | collective-permute-start | bytes 3538952 | tf_op jit(solution)/shard_map/ppermute | solution.py:180
  55.4 28.2 %collective-permute-start.7 = (bf16[2,128,1152]{2,1,0:T(8,128)(2,1)S(1)}, bf16[2,128,1152]{2,1,0:T(8,128)(2,1)S(1)}, u32[]{:S(2)}, u32[]{:S(2)}) collective-permute-start(bf16[2,128,1152]{2,1,0:T(8,128)(2,1)S(1)} %pad_maximum_fusion.8), channel_id=1, source_target_pairs={{0,1},{1,0},{2,3},{3,2},{4,5},{5,4},{6,7},{7,6},{8,9},{9,8},{10,11... | collective-permute-start | bytes 1769480 | tf_op jit(solution)/shard_map/ppermute | solution.py:183
  58.5 7.3 %collective-permute-start.19 = (bf16[128,512]{1,0:T(8,128)(2,1)S(1)}, bf16[128,512]{1,0:T(8,128)(2,1)S(1)}, u32[]{:S(2)}, u32[]{:S(2)}) collective-permute-start(bf16[128,512]{1,0:T(8,128)(2,1)S(1)} %get-tuple-element.105), channel_id=1, source_target_pairs={{0,2},{1,3},{2,4},{3,5},{4,6},{5,7},{6,0},{7,1},{8,10},{9,11},{10,... | collective-permute-start | bytes 393224 | tf_op jit(solution)/shard_map/ppermute | solution.py:186
  65.8 6.8 %collective-permute-start.22 = (bf16[128,512]{1,0:T(8,128)(2,1)S(1)}, bf16[128,512]{1,0:T(8,128)(2,1)S(1)}, u32[]{:S(2)}, u32[]{:S(2)}) collective-permute-start(bf16[128,512]{1,0:T(8,128)(2,1)S(1)} %collective-permute-done.19), channel_id=1, source_target_pairs={{0,2},{1,3},{2,4},{3,5},{4,6},{5,7},{6,0},{7,1},{8,10},{9,11},{10,... | collective-permute-start | bytes 393224 | tf_op jit(solution)/shard_map/ppermute | solution.py:186
  72.6 16.6 %collective-permute-start.20 = (bf16[128,512]{1,0:T(8,128)(2,1)S(1)}, bf16[128,512]{1,0:T(8,128)(2,1)S(1)}, u32[]{:S(2)}, u32[]{:S(2)}) collective-permute-start(bf16[128,512]{1,0:T(8,128)(2,1)S(1)} %collective-permute-done.18), channel_id=1, source_target_pairs={{0,2},{1,3},{2,4},{3,5},{4,6},{5,7},{6,0},{7,1},{8,10},{9,11},{10,... | collective-permute-start | bytes 393224 | tf_op jit(solution)/shard_map/ppermute | solution.py:186
  83.5 26.1 %collective-permute-start.23 = (bf16[4,128,1024]{2,1,0:T(8,128)(2,1)S(1)}, bf16[4,128,1024]{2,1,0:T(8,128)(2,1)S(1)}, u32[]{:S(2)}, u32[]{:S(2)}) collective-permute-start(bf16[4,128,1024]{2,1,0:T(8,128)(2,1)S(1)} %pad_maximum_fusion.4.refs_0_), channel_id=1, source_target_pairs={{0,2},{1,3},{2,4},{3,5},{4,6},{5,7},{6,0},{7,1},{8,10},{9,11},{10,... | collective-permute-start | bytes 3145736 | tf_op jit(solution)/shard_map/ppermute | solution.py:186
  84.6 25.1 %collective-permute-start.8 = (bf16[4,128,1152]{2,1,0:T(8,128)(2,1)S(1)}, bf16[4,128,1152]{2,1,0:T(8,128)(2,1)S(1)}, u32[]{:S(2)}, u32[]{:S(2)}) collective-permute-start(bf16[4,128,1152]{2,1,0:T(8,128)(2,1)S(1)} %pad_maximum_fusion.1.refs_2_), channel_id=1, source_target_pairs={{0,16},{8,24},{16,0},{24,8},{1,17},{9,25},{17,1},{25,9},{2,18},{10... | collective-permute-start | bytes 3538952 | tf_op jit(solution)/shard_map/ppermute | solution.py:180
  85.9 27.2 %collective-permute-start.28 = (bf16[128,512]{1,0:T(8,128)(2,1)S(1)}, bf16[128,512]{1,0:T(8,128)(2,1)S(1)}, u32[]{:S(2)}, u32[]{:S(2)}) collective-permute-start(bf16[128,512]{1,0:T(8,128)(2,1)S(1)} %collective-permute-done.22), channel_id=1, source_target_pairs={{0,2},{1,3},{2,4},{3,5},{4,6},{5,7},{6,0},{7,1},{8,10},{9,11},{10,... | collective-permute-start | bytes 393224 | tf_op jit(solution)/shard_map/ppermute | solution.py:186
  87.6 26.6 %collective-permute-start.15 = (bf16[4,128,1024]{2,1,0:T(8,128)(2,1)S(1)}, bf16[4,128,1024]{2,1,0:T(8,128)(2,1)S(1)}, u32[]{:S(2)}, u32[]{:S(2)}) collective-permute-start(bf16[4,128,1024]{2,1,0:T(8,128)(2,1)S(1)} %pad_maximum_fusion.3.refs_2_), channel_id=1, source_target_pairs={{0,1},{1,0},{2,3},{3,2},{4,5},{5,4},{6,7},{7,6},{8,9},{9,8},{10,11... | collective-permute-start | bytes 3145736 | tf_op jit(solution)/shard_map/ppermute | solution.py:183
  109.7 23.9 %collective-permute-start.24 = (bf16[4,128,1024]{2,1,0:T(8,128)(2,1)S(1)}, bf16[4,128,1024]{2,1,0:T(8,128)(2,1)}, u32[]{:S(2)}, u32[]{:S(2)}) collective-permute-start(bf16[4,128,1024]{2,1,0:T(8,128)(2,1)S(1)} %collective-permute-done.23.refs_1_), channel_id=1, source_target_pairs={{0,2},{1,3},{2,4},{3,5},{4,6},{5,7},{6,0},{7,1},{8,10},{9,11},{10,... | collective-permute-start | bytes 3145736 | tf_op jit(solution)/shard_map/ppermute | solution.py:186
  113.1 23.9 %copy-start.16 = (bf16[16,56,1152]{2,1,0:T(8,128)(2,1)}, bf16[16,56,1152]{2,1,0:T(8,128)(2,1)S(1)}, u32[]{:S(2)}) copy-start(bf16[16,56,1152]{2,1,0:T(8,128)(2,1)S(1)} %get-tuple-element.94) | copy-start | bytes 6193156
  113.1 36.4 %collective-permute-start.16 = (bf16[16,56,1152]{2,1,0:T(8,128)(2,1)}, bf16[16,56,1152]{2,1,0:T(8,128)(2,1)S(1)}, u32[]{:S(2)}, u32[]{:S(2)}) collective-permute-start(bf16[16,56,1152]{2,1,0:T(8,128)(2,1)} %get-tuple-element.102), channel_id=1, source_target_pairs={{0,8},{8,0},{16,24},{24,16},{1,9},{9,1},{17,25},{25,17},{2,10},{10... | collective-permute-start | bytes 6193160 | tf_op jit(solution)/shard_map/ppermute | solution.py:177
  113.2 14.4 %collective-permute-start.29 = (bf16[4,128,512]{2,1,0:T(8,128)(2,1)S(1)}, bf16[4,128,512]{2,1,0:T(8,128)(2,1)S(1)}, u32[]{:S(2)}, u32[]{:S(2)}) collective-permute-start(bf16[4,128,512]{2,1,0:T(8,128)(2,1)S(1)} %pad_maximum_fusion.13), channel_id=1, source_target_pairs={{0,16},{8,24},{16,0},{24,8},{1,17},{9,25},{17,1},{25,9},{2,18},{10... | collective-permute-start | bytes 1572872 | tf_op jit(solution)/shard_map/ppermute | solution.py:180
  116.5 20.5 %copy-start.21 = (bf16[16,56,1024]{2,1,0:T(8,128)(2,1)}, bf16[16,56,1024]{2,1,0:T(8,128)(2,1)S(1)}, u32[]{:S(2)}) copy-start(bf16[16,56,1024]{2,1,0:T(8,128)(2,1)S(1)} %get-tuple-element.100) | copy-start | bytes 5505028
  116.5 34.3 %collective-permute-start.25 = (bf16[16,56,1024]{2,1,0:T(8,128)(2,1)}, bf16[16,56,1024]{2,1,0:T(8,128)(2,1)}, u32[]{:S(2)}, u32[]{:S(2)}) collective-permute-start(bf16[16,56,1024]{2,1,0:T(8,128)(2,1)} %get-tuple-element.112), channel_id=1, source_target_pairs={{0,8},{8,0},{16,24},{24,16},{1,9},{9,1},{17,25},{25,17},{2,10},{10... | collective-permute-start | bytes 5505032 | tf_op jit(solution)/shard_map/ppermute | solution.py:177
  116.7 20.3 %copy-start.1 = (bf16[1,2048,768]{2,1,0:T(8,128)(2,1)S(1)}, bf16[1,2048,768]{2,1,0:T(8,128)(2,1)}, u32[]{:S(2)}) copy-start(bf16[1,2048,768]{2,1,0:T(8,128)(2,1)} %param.11) | copy-start | bytes 9437188
  116.8 14.2 %collective-permute-start.21 = (bf16[4,128,512]{2,1,0:T(8,128)(2,1)S(1)}, bf16[4,128,512]{2,1,0:T(8,128)(2,1)S(1)}, u32[]{:S(2)}, u32[]{:S(2)}) collective-permute-start(bf16[4,128,512]{2,1,0:T(8,128)(2,1)S(1)} %pad_maximum_fusion.12), channel_id=1, source_target_pairs={{0,1},{1,0},{2,3},{3,2},{4,5},{5,4},{6,7},{7,6},{8,9},{9,8},{10,11... | collective-permute-start | bytes 1572872 | tf_op jit(solution)/shard_map/ppermute | solution.py:183
  131.8 31.8 %collective-permute-start.30 = (bf16[8,128,512]{2,1,0:T(8,128)(2,1)}, bf16[8,128,512]{2,1,0:T(8,128)(2,1)S(1)}, u32[]{:S(2)}, u32[]{:S(2)}) collective-permute-start(bf16[8,128,512]{2,1,0:T(8,128)(2,1)} %constant_dynamic-update-slice_fusion.9.refs_0_), channel_id=1, source_target_pairs={{0,1},{1,0},{2,3},{3,2},{4,5},{5,4},{6,7},{7,6},{8,9},{9,8},{10,11... | collective-permute-start | bytes 3145736 | tf_op jit(solution)/shard_map/ppermute | solution.py:183
  133.6 41.3 %collective-permute-start.32 = (bf16[4,128,1024]{2,1,0:T(8,128)(2,1)}, bf16[4,128,1024]{2,1,0:T(8,128)(2,1)}, u32[]{:S(2)}, u32[]{:S(2)}) collective-permute-start(bf16[4,128,1024]{2,1,0:T(8,128)(2,1)} %collective-permute-done.24.refs_2_), channel_id=1, source_target_pairs={{0,2},{1,3},{2,4},{3,5},{4,6},{5,7},{6,0},{7,1},{8,10},{9,11},{10,... | collective-permute-start | bytes 3145736 | tf_op jit(solution)/shard_map/ppermute | solution.py:186
  135.5 31.0 %collective-permute-start.26 = (bf16[8,128,512]{2,1,0:T(8,128)(2,1)}, bf16[8,128,512]{2,1,0:T(8,128)(2,1)S(1)}, u32[]{:S(2)}, u32[]{:S(2)}) collective-permute-start(bf16[8,128,512]{2,1,0:T(8,128)(2,1)} %constant_dynamic-update-slice_fusion.4.refs_0_), channel_id=1, source_target_pairs={{0,16},{8,24},{16,0},{24,8},{1,17},{9,25},{17,1},{25,9},{2,18},{10... | collective-permute-start | bytes 3145736 | tf_op jit(solution)/shard_map/ppermute | solution.py:180
  163.6 7.4 %copy-start = (bf16[1,768,2048]{2,1,0:T(8,128)(2,1)S(1)}, bf16[1,768,2048]{2,1,0:T(8,128)(2,1)}, u32[]{:S(2)}) copy-start(bf16[1,768,2048]{2,1,0:T(8,128)(2,1)} %param.13) | copy-start | bytes 9437188
  166.4 2.5 collective-permute-start.31
  168.4 2.7 collective-permute-start.27
  178.6 3.9 %collective-permute-start.33 = (bf16[16,56,1024]{2,1,0:T(8,128)(2,1)S(1)}, bf16[16,56,1024]{2,1,0:T(8,128)(2,1)S(1)}, u32[]{:S(2)}, u32[]{:S(2)}) collective-permute-start(bf16[16,56,1024]{2,1,0:T(8,128)(2,1)S(1)} %get-tuple-element.127), channel_id=1, source_target_pairs={{0,8},{8,0},{16,24},{24,16},{1,9},{9,1},{17,25},{25,17},{2,10},{10... | collective-permute-start | bytes 5505032 | tf_op jit(solution)/shard_map/ppermute | solution.py:177
  182.4 17.5 %copy-start.8 = (bf16[16,56,1024]{2,1,0:T(8,128)(2,1)}, bf16[16,56,1024]{2,1,0:T(8,128)(2,1)S(1)}, u32[]{:S(2)}) copy-start(bf16[16,56,1024]{2,1,0:T(8,128)(2,1)S(1)} %collective-permute-done.33) | copy-start | bytes 5505028
  199.9 16.2 %collective-permute-start.36 = (bf16[896,768]{1,0:T(8,128)(2,1)}, bf16[896,768]{1,0:T(8,128)(2,1)S(1)}, u32[]{:S(2)}, u32[]{:S(2)}) collective-permute-start(bf16[896,768]{1,0:T(8,128)(2,1)} %get-tuple-element.143), channel_id=1, source_target_pairs={{0,8},{8,0},{16,24},{24,16},{1,9},{9,1},{17,25},{25,17},{2,10},{10... | collective-permute-start | bytes 4128776 | tf_op jit(solution)/shard_map/ppermute | solution.py:177
  200.3 16.7 %collective-permute-start.34 = (bf16[896,896]{1,0:T(8,128)(2,1)S(1)}, bf16[896,896]{1,0:T(8,128)(2,1)S(1)}, u32[]{:S(2)}, u32[]{:S(2)}) collective-permute-start(bf16[896,896]{1,0:T(8,128)(2,1)S(1)} %get-tuple-element.139), channel_id=1, source_target_pairs={{0,8},{8,0},{16,24},{24,16},{1,9},{9,1},{17,25},{25,17},{2,10},{10... | collective-permute-start | bytes 4816904 | tf_op jit(solution)/shard_map/ppermute | solution.py:177
  200.5 15.1 %collective-permute-start.35 = (bf16[896,512]{1,0:T(8,128)(2,1)}, bf16[896,512]{1,0:T(8,128)(2,1)S(1)}, u32[]{:S(2)}, u32[]{:S(2)}) collective-permute-start(bf16[896,512]{1,0:T(8,128)(2,1)} %get-tuple-element.141), channel_id=1, source_target_pairs={{0,8},{8,0},{16,24},{24,16},{1,9},{9,1},{17,25},{25,17},{2,10},{10... | collective-permute-start | bytes 2752520 | tf_op jit(solution)/shard_map/ppermute | solution.py:177
  218.0 37.2 %collective-permute-start.37 = (bf16[2,2,128,896]{2,3,1,0:T(8,128)(2,1)S(1)}, bf16[2,2,128,896]{2,3,1,0:T(8,128)(2,1)S(1)}, u32[]{:S(2)}, u32[]{:S(2)}) collective-permute-start(bf16[2,2,128,896]{2,3,1,0:T(8,128)(2,1)S(1)} %convolution_convert_fusion.1), channel_id=1, source_target_pairs={{0,16},{8,24},{16,0},{24,8},{1,17},{9,25},{17,1},{25,9},{2,18},{10... | collective-permute-start | bytes 2752520 | tf_op jit(solution)/shard_map/ppermute | solution.py:180
  218.6 30.3 %collective-permute-start.50 = (bf16[2,2,128,768]{2,3,1,0:T(8,128)(2,1)S(1)}, bf16[2,2,128,768]{2,3,1,0:T(8,128)(2,1)S(1)}, u32[]{:S(2)}, u32[]{:S(2)}) collective-permute-start(bf16[2,2,128,768]{2,3,1,0:T(8,128)(2,1)S(1)} %convolution_convert_fusion.3), channel_id=1, source_target_pairs={{0,1},{1,0},{2,3},{3,2},{4,5},{5,4},{6,7},{7,6},{8,9},{9,8},{10,11... | collective-permute-start | bytes 2359304 | tf_op jit(solution)/shard_map/ppermute | solution.py:183
  219.1 15.6 %collective-permute-start.41 = (bf16[2,2,128,512]{2,3,0,1:T(8,128)(2,1)S(1)}, bf16[2,2,128,512]{2,3,0,1:T(8,128)(2,1)S(1)}, u32[]{:S(2)}, u32[]{:S(2)}) collective-permute-start(bf16[2,2,128,512]{2,3,0,1:T(8,128)(2,1)S(1)} %convolution_convert_fusion.4), channel_id=1, source_target_pairs={{0,6},{1,7},{2,0},{3,1},{4,2},{5,3},{6,4},{7,5},{8,14},{9,15},{10,... | collective-permute-start | bytes 1572872 | tf_op jit(solution)/shard_map/ppermute | solution.py:191
  222.3 32.5 %collective-permute-start.38 = (bf16[2,2,128,768]{2,3,1,0:T(8,128)(2,1)S(1)}, bf16[2,2,128,768]{2,3,1,0:T(8,128)(2,1)S(1)}, u32[]{:S(2)}, u32[]{:S(2)}) collective-permute-start(bf16[2,2,128,768]{2,3,1,0:T(8,128)(2,1)S(1)} %convolution_convert_fusion.2), channel_id=1, source_target_pairs={{0,1},{1,0},{2,3},{3,2},{4,5},{5,4},{6,7},{7,6},{8,9},{9,8},{10,11... | collective-permute-start | bytes 2359304 | tf_op jit(solution)/shard_map/ppermute | solution.py:183
  222.8 37.4 %collective-permute-start.40 = (bf16[2,2,128,896]{2,3,1,0:T(8,128)(2,1)S(1)}, bf16[2,2,128,896]{2,3,1,0:T(8,128)(2,1)S(1)}, u32[]{:S(2)}, u32[]{:S(2)}) collective-permute-start(bf16[2,2,128,896]{2,3,1,0:T(8,128)(2,1)S(1)} %convolution_convert_fusion), channel_id=1, source_target_pairs={{0,16},{8,24},{16,0},{24,8},{1,17},{9,25},{17,1},{25,9},{2,18},{10... | collective-permute-start | bytes 2752520 | tf_op jit(solution)/shard_map/ppermute | solution.py:180
  235.0 36.5 %collective-permute-start.42 = (bf16[2,2,128,512]{2,3,0,1:T(8,128)(2,1)S(1)}, bf16[2,2,128,512]{2,3,0,1:T(8,128)(2,1)S(1)}, u32[]{:S(2)}, u32[]{:S(2)}) collective-permute-start(bf16[2,2,128,512]{2,3,0,1:T(8,128)(2,1)S(1)} %add_convert_fusion.6), channel_id=1, source_target_pairs={{0,6},{1,7},{2,0},{3,1},{4,2},{5,3},{6,4},{7,5},{8,14},{9,15},{10,... | collective-permute-start | bytes 1572872 | tf_op jit(solution)/shard_map/ppermute | solution.py:191
  255.9 20.5 %collective-permute-start.39 = (bf16[2,128,896]{1,2,0:T(8,128)(2,1)S(1)}, bf16[2,128,896]{1,2,0:T(8,128)(2,1)S(1)}, u32[]{:S(2)}, u32[]{:S(2)}) collective-permute-start(bf16[2,128,896]{1,2,0:T(8,128)(2,1)S(1)} %slice_bitcast_fusion), channel_id=1, source_target_pairs={{0,1},{1,0},{2,3},{3,2},{4,5},{5,4},{6,7},{7,6},{8,9},{9,8},{10,11... | collective-permute-start | bytes 1376264 | tf_op jit(solution)/shard_map/ppermute | solution.py:183
  260.1 16.1 %collective-permute-start.51 = (bf16[2,128,768]{1,2,0:T(8,128)(2,1)S(1)}, bf16[2,128,768]{1,2,0:T(8,128)(2,1)S(1)}, u32[]{:S(2)}, u32[]{:S(2)}) collective-permute-start(bf16[2,128,768]{1,2,0:T(8,128)(2,1)S(1)} %slice_bitcast_fusion.3), channel_id=1, source_target_pairs={{0,16},{8,24},{16,0},{24,8},{1,17},{9,25},{17,1},{25,9},{2,18},{10... | collective-permute-start | bytes 1179656 | tf_op jit(solution)/shard_map/ppermute | solution.py:180
  271.9 14.2 %collective-permute-start.43 = (bf16[2,128,896]{1,2,0:T(8,128)(2,1)S(1)}, bf16[2,128,896]{1,2,0:T(8,128)(2,1)S(1)}, u32[]{:S(2)}, u32[]{:S(2)}) collective-permute-start(bf16[2,128,896]{1,2,0:T(8,128)(2,1)S(1)} %slice_bitcast_fusion.2), channel_id=1, source_target_pairs={{0,1},{1,0},{2,3},{3,2},{4,5},{5,4},{6,7},{7,6},{8,9},{9,8},{10,11... | collective-permute-start | bytes 1376264 | tf_op jit(solution)/shard_map/ppermute | solution.py:183
  272.4 15.4 %collective-permute-start.45 = (bf16[2,2,128,512]{2,3,0,1:T(8,128)(2,1)S(1)}, bf16[2,2,128,512]{2,3,0,1:T(8,128)(2,1)S(1)}, u32[]{:S(2)}, u32[]{:S(2)}) collective-permute-start(bf16[2,2,128,512]{2,3,0,1:T(8,128)(2,1)S(1)} %add_convert_fusion.5), channel_id=1, source_target_pairs={{0,6},{1,7},{2,0},{3,1},{4,2},{5,3},{6,4},{7,5},{8,14},{9,15},{10,... | collective-permute-start | bytes 1572872 | tf_op jit(solution)/shard_map/ppermute | solution.py:191
  275.6 9.5 %collective-permute-start.47 = (bf16[2,128,768]{1,2,0:T(8,128)(2,1)S(1)}, bf16[2,128,768]{1,2,0:T(8,128)(2,1)S(1)}, u32[]{:S(2)}, u32[]{:S(2)}) collective-permute-start(bf16[2,128,768]{1,2,0:T(8,128)(2,1)S(1)} %slice_bitcast_fusion.5), channel_id=1, source_target_pairs={{0,16},{8,24},{16,0},{24,8},{1,17},{9,25},{17,1},{25,9},{2,18},{10... | collective-permute-start | bytes 1179656 | tf_op jit(solution)/shard_map/ppermute | solution.py:180
  285.3 7.1 %collective-permute-start.48 = (bf16[128,768]{0,1:T(8,128)(2,1)S(1)}, bf16[128,768]{0,1:T(8,128)(2,1)S(1)}, u32[]{:S(2)}, u32[]{:S(2)}) collective-permute-start(bf16[128,768]{0,1:T(8,128)(2,1)S(1)} %slice_bitcast_fusion.16), channel_id=1, source_target_pairs={{0,6},{1,7},{2,0},{3,1},{4,2},{5,3},{6,4},{7,5},{8,14},{9,15},{10,... | collective-permute-start | bytes 589832 | tf_op jit(solution)/shard_map/ppermute | solution.py:191
  286.2 8.6 %collective-permute-start.44 = (bf16[128,896]{0,1:T(8,128)(2,1)S(1)}, bf16[128,896]{0,1:T(8,128)(2,1)S(1)}, u32[]{:S(2)}, u32[]{:S(2)}) collective-permute-start(bf16[128,896]{0,1:T(8,128)(2,1)S(1)} %slice_bitcast_fusion.9), channel_id=1, source_target_pairs={{0,6},{1,7},{2,0},{3,1},{4,2},{5,3},{6,4},{7,5},{8,14},{9,15},{10,... | collective-permute-start | bytes 688136 | tf_op jit(solution)/shard_map/ppermute | solution.py:191
  288.2 11.1 %collective-permute-start.54 = (bf16[2,128,512]{1,2,0:T(8,128)(2,1)S(1)}, bf16[2,128,512]{1,2,0:T(8,128)(2,1)S(1)}, u32[]{:S(2)}, u32[]{:S(2)}) collective-permute-start(bf16[2,128,512]{1,2,0:T(8,128)(2,1)S(1)} %slice_bitcast_fusion.6), channel_id=1, source_target_pairs={{0,1},{1,0},{2,3},{3,2},{4,5},{5,4},{6,7},{7,6},{8,9},{9,8},{10,11... | collective-permute-start | bytes 786440 | tf_op jit(solution)/shard_map/ppermute | solution.py:183
  294.9 11.8 %collective-permute-start.46 = (bf16[128,896]{0,1:T(8,128)(2,1)S(1)}, bf16[128,896]{0,1:T(8,128)(2,1)S(1)}, u32[]{:S(2)}, u32[]{:S(2)}) collective-permute-start(bf16[128,896]{0,1:T(8,128)(2,1)S(1)} %fusion.43), channel_id=1, source_target_pairs={{0,6},{1,7},{2,0},{3,1},{4,2},{5,3},{6,4},{7,5},{8,14},{9,15},{10,... | collective-permute-start | bytes 688136 | tf_op jit(solution)/shard_map/ppermute | solution.py:191
  299.2 7.5 %collective-permute-start.52 = (bf16[128,768]{0,1:T(8,128)(2,1)S(1)}, bf16[128,768]{0,1:T(8,128)(2,1)S(1)}, u32[]{:S(2)}, u32[]{:S(2)}) collective-permute-start(bf16[128,768]{0,1:T(8,128)(2,1)S(1)} %fusion.59), channel_id=1, source_target_pairs={{0,6},{1,7},{2,0},{3,1},{4,2},{5,3},{6,4},{7,5},{8,14},{9,15},{10,... | collective-permute-start | bytes 589832 | tf_op jit(solution)/shard_map/ppermute | solution.py:191
  299.4 11.8 %collective-permute-start.55 = (bf16[128,512]{0,1:T(8,128)(2,1)S(1)}, bf16[128,512]{0,1:T(8,128)(2,1)S(1)}, u32[]{:S(2)}, u32[]{:S(2)}) collective-permute-start(bf16[128,512]{0,1:T(8,128)(2,1)S(1)} %slice_bitcast_fusion.17), channel_id=1, source_target_pairs={{0,16},{8,24},{16,0},{24,8},{1,17},{9,25},{17,1},{25,9},{2,18},{10... | collective-permute-start | bytes 393224 | tf_op jit(solution)/shard_map/ppermute | solution.py:180
  306.8 10.9 %collective-permute-start.49 = (bf16[128,896]{0,1:T(8,128)(2,1)S(1)}, bf16[128,896]{0,1:T(8,128)(2,1)S(1)}, u32[]{:S(2)}, u32[]{:S(2)}) collective-permute-start(bf16[128,896]{0,1:T(8,128)(2,1)S(1)} %fusion.44), channel_id=1, source_target_pairs={{0,6},{1,7},{2,0},{3,1},{4,2},{5,3},{6,4},{7,5},{8,14},{9,15},{10,... | collective-permute-start | bytes 688136 | tf_op jit(solution)/shard_map/ppermute | solution.py:191
  311.2 6.5 %collective-permute-start.53 = (bf16[128,768]{0,1:T(8,128)(2,1)S(1)}, bf16[128,768]{0,1:T(8,128)(2,1)S(1)}, u32[]{:S(2)}, u32[]{:S(2)}) collective-permute-start(bf16[128,768]{0,1:T(8,128)(2,1)S(1)} %fusion.60), channel_id=1, source_target_pairs={{0,6},{1,7},{2,0},{3,1},{4,2},{5,3},{6,4},{7,5},{8,14},{9,15},{10,... | collective-permute-start | bytes 589832 | tf_op jit(solution)/shard_map/ppermute | solution.py:191
  (23 other events, 90.3 us)
